TPU v7x, 256 devices: a whole 4x4x8 slice. The times are simulated.
256 devices in a mesh: wall: 32 (over y, z), span: 2 (over x_hi), stream: 4 (over x_lo, core).
Axes of the slice: x: 4 (x_hi: 2, x_lo: 2; x = x_hi * 2 + x_lo), y: 4, z: 8, core: 2. Of those that a mesh axis runs over, the one named last changes fastest.
Arguments:
- right_side: float32 [1024, 128, 512], P('wall', 'span', 'stream'), may hold values from -6 to 6
- viscosity: float32 [1024, 128, 512], P('wall', 'span', 'stream'), may hold values from 0.05 to 1
- wall_metric: float32 [1024], P('wall'), may hold values from 0.5 to 4
- line_inverse: bfloat16 [1024, 1024], replicated
Outputs:
- solution: float32 [1024, 128, 512], P('wall', 'span', 'stream')
- residual: float32 [1024, 128, 512], P('wall', 'span', 'stream')
All inputs are finite; a program needn't handle non-finite values.
Results may differ from a plain program's by a relative error of at most 0.0057.
Values may be sent and summed in bfloat16 or wider, within the bound.
No kernel may reach another device: no remote copies, remote signals or barrier semaphores. Data moves between devices by JAX's collectives and lax.ppermute only.
A program may use at most 128 MiB of HBM per device.

v0:
```python
import functools

import jax
import jax.numpy as jnp
from jax import lax
from jax.experimental import pallas as pl
from jax.experimental.pallas import tpu as pltpu
from jax.sharding import PartitionSpec as P

STEPS = 3
NW, WY, WZ = 1024, 4, 8
ROWS, SPAN, LANES = 32, 64, 128
BS, BX = 16, 16
CELLS = BS * BX
CHUNKS = NW // 128
LP, FIRST, BUSY, ROW_COUNT = BX + 2, 24, 288, 336
RUN = 48
CP = SPAN + 3
BLOCK_ROWS = 2280
TAIL = 8
MID = 0.5
F32, BF16 = jnp.float32, jnp.bfloat16
MIB = 1024 * 1024


def chebyshev_weights(steps):
    lowest = 0.25
    highest = 2.5
    center = 0.5 * (highest + lowest)
    half = 0.5 * (highest - lowest)
    ratio = center / half
    weights = [(0.0, 1.0 / center)]
    rho_old = 1.0 / ratio
    for step in range(1, steps):
        rho_new = 1.0 / (2.0 * ratio - rho_old)
        weights.append((rho_new * rho_old, 2.0 * rho_new / half))
        rho_old = rho_new
    return weights


WEIGHTS = chebyshev_weights(STEPS)


def shape(dims, dtype):
    return jax.ShapeDtypeStruct(dims, dtype)


def call(kernel, outs, scratch=(), limit=40 * MIB, **specs):
    return pl.pallas_call(
        kernel,
        out_shape=outs,
        scratch_shapes=list(scratch),
        compiler_params=pltpu.CompilerParams(vmem_limit_bytes=limit),
        cost_estimate=pl.CostEstimate(flops=10**7, bytes_accessed=4 * 10**6, transcendentals=0),
        **specs,
    )


def skew(arrays):
    block = lax.broadcasted_iota(jnp.int32, arrays[0].shape, 1) // BX
    arrays = list(arrays)
    for bit in range(3):
        step = 1 << bit
        upper = (block // step) % 2 == 1
        arrays = [jnp.where(upper, arrays[(j + step) % 8], arrays[j]) for j in range(8)]
    return [arrays[-z % 8] for z in range(8)]


def to_blocks(rows):
    return skew([pltpu.roll(row, BX * i, 1) if i else row for i, row in enumerate(rows)])


def from_blocks(blocks):
    return [pltpu.roll(row, LANES - BX * i, 1) if i else row for i, row in enumerate(skew(blocks))]


def turned(p):
    z, odd = lax.axis_index("wall") % WZ, lax.axis_index("stream") % 2
    return (p - (z + odd * (WZ - 1 - 2 * z)) + WZ) % WZ


def owner(t, z):
    span, odd = lax.axis_index("span"), lax.axis_index("stream") % 2
    return WZ * (t + span * (WY - 1 - 2 * t)) + z + odd * (WZ - 1 - 2 * z)


def strided(s):
    return pl.ds(s, ROWS, stride=SPAN + 1)


def edge_lanes(blocks, pick, turn, offset):
    at = lax.broadcasted_iota(jnp.int32, (LANES, LANES), 0)
    to = lax.broadcasted_iota(jnp.int32, (LANES, LANES), 1)
    one = jnp.where((at % BX == pick) & (to == (at // BX + turn) % 8), 1.0, 0.0).astype(BF16)
    eights = jnp.dot(blocks.reshape(8 * ROWS, LANES), one, preferred_element_type=F32)
    out = jnp.zeros((ROWS, LANES), F32)
    for q in range(8):
        out += pltpu.roll(eights[ROWS * q : ROWS * (q + 1)], (8 * q + offset) % LANES, 1)
    return out.astype(BF16)


def pack(
    b_hbm, v_hbm, m_hbm, send_hbm, es_hbm, dl_hbm, dr_hbm, b_buf, v_buf, m_buf, send, es, dl, dr, cl, cr,
    sems, done, small,
):
    def copy(k, w):
        src, dst = ((v_hbm, v_buf), (b_hbm, b_buf))[k]
        return pltpu.make_async_copy(src.at[w], dst.at[pl.ds((SPAN + 1) * w, SPAN)], sems.at[k, w])

    def result(y):
        peers = pl.ds(WZ * y, WZ)
        return pltpu.make_async_copy(send.at[peers], send_hbm.at[peers], done.at[y])

    for k in range(2):
        for w in range(ROWS):
            copy(k, w).start()
    metric = pltpu.make_async_copy(m_hbm, m_buf, small.at[3])
    metric.start()
    edges = [
        pltpu.make_async_copy(src, dst, small.at[n])
        for n, (src, dst) in enumerate(((es, es_hbm), (dl, dl_hbm), (dr, dr_hbm)))
    ]
    metric.wait()
    rest = m_buf[...]
    parts = []
    for _ in range(3):
        part = rest.astype(BF16)
        rest = rest - part.astype(F32)
        parts.append(part.astype(F32))
    tail = jnp.concatenate(parts + [jnp.zeros((TAIL - 3, ROWS), F32)], axis=0)
    tail = jnp.concatenate([tail, jnp.zeros((TAIL, LANES - ROWS), F32)], axis=1).astype(BF16)
    for k in range(WY * WZ):
        send[k, 4 * ROWS :, :] = tail

    def move(t, k, buf, mid):
        for g in range(2):
            parts = [buf[strided(16 * t + 8 * g + i), :] - mid for i in range(8)]
            parts = to_blocks([part.astype(BF16) for part in parts])
            rows = slice(ROWS * (2 * k + g), ROWS * (2 * k + g + 1))
            for z in range(WZ):
                send[owner(t, z), rows, :] = parts[z]
            if k:
                cl[2 * t + g] = parts[0]
                cr[2 * t + g] = parts[7]
        return 0

    for w in range(ROWS):
        copy(0, w).wait()
    lax.fori_loop(0, WY, lambda t, _: move(t, 1, v_buf, MID), 0)
    es[0] = (v_buf[strided(0), :] - MID).astype(BF16)
    es[1] = (v_buf[strided(SPAN - 1), :] - MID).astype(BF16)
    dl[...] = edge_lanes(cl[...], 0, 0, SPAN)
    dr[...] = edge_lanes(cr[...], BX - 1, 1, SPAN)
    for edge in edges:
        edge.start()
    for w in range(ROWS):
        copy(1, w).wait()

    def last(t, _):
        move(t, 0, b_buf, 0.0)
        result(owner(t, 0) // WZ).start()
        return 0

    lax.fori_loop(0, WY, last, 0)
    for t in range(WY):
        result(t).wait()
    for edge in edges:
        edge.wait()


def to_lines(recv, bf, hf, b0, metric, ends, *edges):
    count = WY * WZ
    nothing = jnp.zeros((1, LANES), F32)
    for k in range(count):
        rows = []
        for g in range(2):
            for other, at in ((k - 1, ROWS - 1), (k + 1, 0)):
                if not 0 <= other < count:
                    rows.append(nothing)
                    continue
                m = jnp.sum(recv[other, 4 * ROWS :, :].astype(F32), axis=0, keepdims=True)
                v = recv[other, ROWS * (2 + g) : ROWS * (3 + g), :].astype(F32) + MID
                rows.append(v[at : at + 1] * m[:, at : at + 1])
        ends[k] = jnp.concatenate(rows, axis=0)
    for i in range(8):
        row = jnp.zeros((TAIL, LANES), F32)
        for j in range(4):
            row += pltpu.roll(recv[4 * i + j, 4 * ROWS :, :].astype(F32), ROWS * j, 1)
        metric[:, i * LANES : (i + 1) * LANES] = jnp.sum(row, axis=0, keepdims=True)
    for k, ref in enumerate((bf, hf)):
        for i in range(CHUNKS):
            for g in range(2):
                tile = recv[4 * i : 4 * i + 4, ROWS * (2 * k + g) : ROWS * (2 * k + g + 1), :]
                tile = tile.astype(F32).reshape(LANES, LANES).T
                if k:
                    tile = 0.5 * tile + 0.5 * MID
                for p in range(8):
                    ref[line_rows(i, 8 * g + turned(p)), :] = tile[BX * p : BX * (p + 1)]
    for i in range(CHUNKS):
        lanes = slice(i * LANES, (i + 1) * LANES)
        b0[:, lanes] = bf[pl.ds(ROW_COUNT * i + FIRST, BUSY), :].astype(BF16)
        for n, rows in enumerate(edge_rows(i)):
            edges[n][:BX, lanes] = bf[rows, :].astype(BF16)
            edges[n][BX:, lanes] = (2.0 * hf[rows, :] - MID).astype(BF16)


def line_rows(i, s):
    return pl.ds(ROW_COUNT * i + FIRST + LP * s, BX)


def edge_rows(i):
    base = ROW_COUNT * i + FIRST
    return (
        line_rows(i, 0),
        line_rows(i, BS - 1),
        pl.ds(base, BS, stride=LP),
        pl.ds(base + BX - 1, BS, stride=LP),
    )


def near_rows(i):
    base = ROW_COUNT * i + FIRST
    return (
        line_rows(i, -1),
        line_rows(i, BS),
        pl.ds(base - 1, BS, stride=LP),
        pl.ds(base + BX, BS, stride=LP),
    )


def busy(i):
    return pl.ds(ROW_COUNT * i + FIRST, BUSY)


def apply_lines(rows, line):
    return lax.dot_general(rows, line, (((1,), (1,)), ((), ())), preferred_element_type=F32)


def first_lines(b0, hf, metric, line, x1, fw):
    y = WEIGHTS[0][1] * apply_lines(b0[...], line[...])
    for i in range(CHUNKS):
        x1[busy(i), :] = y[:, i * LANES : (i + 1) * LANES]
    last = lax.broadcasted_iota(jnp.int32, (RUN, LANES), 1) == LANES - 1

    def one(c, _):
        after = jnp.zeros((RUN, LANES), F32)
        for i in reversed(range(CHUNKS)):
            rows = pl.ds(ROW_COUNT * i + FIRST + RUN * c, RUN)
            half = hf[rows, :] * metric[:, i * LANES : (i + 1) * LANES]
            moved = pltpu.roll(half, LANES - 1, 1)
            fw[rows, :] = half + jnp.where(last, after, moved)
            after = moved
        return 0

    lax.fori_loop(0, BUSY // RUN, one, 0)


def line_resid(bf, xe, he, fw, metric, out):
    lane = lax.broadcasted_iota(jnp.int32, (RUN, LANES), 1)
    last, first = lane == LANES - 1, lane == 0

    def one(c, _):
        def load(ref, i, shift=0):
            return ref[pl.ds(ROW_COUNT * i + FIRST + shift + RUN * c, RUN), :]

        xc = load(xe, 0)
        moved_x = pltpu.roll(xc, LANES - 1, 1)
        entry = load(he, 0) * metric[:, :LANES] * -xc
        for i in range(CHUNKS):
            if i + 1 < CHUNKS:
                after = load(xe, i + 1)
                moved_after = pltpu.roll(after, LANES - 1, 1)
            else:
                after = moved_after = jnp.zeros((RUN, LANES), F32)
            above = load(fw, i) * (xc - jnp.where(last, moved_after, moved_x))
            below = pltpu.roll(above, 1, 1)
            hc = load(he, i)
            total = above - jnp.where(first, entry, below)
            for shift in (-LP, -1, 1, LP):
                total += (hc + load(he, i, shift)) * (xc - load(xe, i, shift))
            rows = pl.ds(pl.multiple_of(RUN * c, BX), RUN)
            out[rows, i * LANES : (i + 1) * LANES] = (load(bf, i) - (xc + total)).astype(BF16)
            xc, moved_x, entry = after, moved_after, below
        return 0

    lax.fori_loop(0, BUSY // RUN, one, 0)


def second_step(x1, bf, hf, fw, su, sd, xl, xr, line, metric, x2, d2, he, e0, e1, e2, e3, xe, rt, ends):
    for k, ref in enumerate((su, sd, xl, xr)):
        ends[k * BX : (k + 1) * BX] = ref[0:BX]
    ends1 = WEIGHTS[0][1] * apply_lines(ends[...], line[...])
    for i in range(CHUNKS):
        lanes = slice(i * LANES, (i + 1) * LANES)
        xe[busy(i), :] = x1[busy(i), :]
        he[busy(i), :] = hf[busy(i), :]
        for k, (rows, ref) in enumerate(zip(near_rows(i), (su, sd, xl, xr))):
            xe[rows, :] = ends1[k * BX : (k + 1) * BX, lanes]
            he[rows, :] = 0.5 * ref[BX : 2 * BX, lanes].astype(F32) + 0.5 * MID
    line_resid(bf, xe, he, fw, metric, rt)
    keep, scale = WEIGHTS[1]
    y = scale * apply_lines(rt[...], line[...])
    for i in range(CHUNKS):
        lanes = slice(i * LANES, (i + 1) * LANES)
        x = x1[busy(i), :]
        d = keep * x + y[:, lanes]
        d2[busy(i), :] = d
        x2[busy(i), :] = x + d
        for rows, ref in zip(edge_rows(i), (e0, e1, e2, e3)):
            ref[:, lanes] = x2[rows, :].astype(BF16)


def third_step(x2, d2, bf, he, fw, su, sd, xl, xr, line, metric, ends, send, xe, rt):
    for i in range(CHUNKS):
        lanes = slice(i * LANES, (i + 1) * LANES)
        xe[busy(i), :] = x2[busy(i), :]
        for rows, ref in zip(near_rows(i), (su, sd, xl, xr)):
            xe[rows, :] = ref[:, lanes].astype(F32)
    line_resid(bf, xe, he, fw, metric, rt)
    keep, scale = WEIGHTS[2]
    y = scale * apply_lines(rt[...], line[...])
    count = WY * WZ
    nothing = jnp.zeros((1, LANES), F32)
    firsts, lasts = {}, {}
    for i in range(CHUNKS):
        xe[busy(i), :] = x2[busy(i), :] + keep * d2[busy(i), :] + y[:, i * LANES : (i + 1) * LANES]
        for j in range(2):
            tile = jnp.concatenate([xe[line_rows(i, 8 * j + turned(p)), :] for p in range(8)], axis=0).T
            for k in range(4):
                part = tile[ROWS * k : ROWS * (k + 1)]
                send[4 * i + k, ROWS * j : ROWS * (j + 1), :] = part.astype(BF16)
                firsts[4 * i + k, j] = part[:1]
                lasts[4 * i + k, j] = part[ROWS - 1 :]
    for k in range(count):
        rows = []
        for j in range(2):
            rows += [lasts.get((k - 1, j), nothing), firsts.get((k + 1, j), nothing)]
            rows.append(ends[k, 2 * j : 2 * j + 2, :])
        send[k, 2 * ROWS :, :] = jnp.concatenate(rows, axis=0).astype(BF16)


def block_row(w, s=0):
    return CP * (w + 1) + 1 + s


def unpack(recv, ves, vdl, vdr, xf, kappas, es, dl, dr, cl, cr):
    def one(t, _):
        for g in range(2):
            rows = slice(ROWS * g, ROWS * (g + 1))
            parts = [recv[owner(t, z), rows, :] for z in range(WZ)]
            cl[2 * t + g] = parts[0]
            cr[2 * t + g] = parts[7]
            parts = from_blocks(parts)
            for i in range(8):
                s = 16 * t + 8 * g + i
                xf[pl.ds(block_row(0) + s, ROWS, stride=CP), :] = parts[i].astype(F32)
        parts = from_blocks([recv[owner(t, z), 2 * ROWS :, :].astype(F32) for z in range(WZ)])
        for g in range(2):
            for i in range(8):
                s = 16 * t + 8 * g + i
                for k, (ref, row) in enumerate(
                    ((xf, block_row(-1)), (xf, block_row(ROWS)), (kappas, 0), (kappas, SPAN))
                ):
                    ref[pl.ds(row + s, 1), :] = parts[i][4 * g + k : 4 * g + k + 1]
        return 0

    lax.fori_loop(0, WY, one, 0)
    es[0] = xf[pl.ds(block_row(0), ROWS, stride=CP), :].astype(BF16)
    es[1] = xf[pl.ds(block_row(0, SPAN - 1), ROWS, stride=CP), :].astype(BF16)
    es[2] = ves[0]
    es[3] = ves[1]
    dl[...] = edge_lanes(cl[...], 0, 0, 0) + vdl[...]
    dr[...] = edge_lanes(cr[...], BX - 1, 1, 0) + vdr[...]


def stage(xf, v_ref, kappas, m_ref, x3, hf, gx, gk, x_buf, sems):
    def result(n):
        rows = pl.ds(4 * n, 4)
        return pltpu.make_async_copy(x_buf.at[rows], x3.at[rows], sems.at[n])

    def four(n, below):
        for k in range(4):
            w = 4 * n + k
            x_buf[w] = xf[pl.ds(block_row(w), SPAN), :]
        result(n).start()
        for k in range(4):
            w = 4 * n + k
            half = 0.5 * v_ref[w]
            hf[pl.ds(block_row(w), SPAN), :] = half
            cells = pl.ds(pl.multiple_of(SPAN * w, SPAN), SPAN)
            gx[cells, :] = half + pltpu.roll(half, LANES - 1, 1)
            half = m_ref[w] * half
            gk[cells, :] = below + half
            below = half
        return below

    below = lax.fori_loop(0, ROWS // 4, four, 0.5 * kappas[:SPAN, :])
    gk[SPAN * ROWS :, :] = below + 0.5 * kappas[SPAN:, :]
    for n in range(ROWS // 4):
        result(n).wait()


def last_resid(xf, hf, gx, gk, b_ref, spans, lefts, rights, dl, dr, out, xe, he, r_buf, sems):
    xe[...] = xf[...]
    he[...] = hf[...]
    for s, k in ((-1, 1), (SPAN, 0)):
        rows = pl.ds(block_row(0, s), ROWS, stride=CP)
        xe[rows, :] = spans[k].astype(F32)
        he[rows, :] = 0.5 * spans[2 + k].astype(F32) + 0.5 * MID
    at = lax.broadcasted_iota(jnp.int32, (2 * ROWS, LANES), 0)
    to = lax.broadcasted_iota(jnp.int32, (2 * ROWS, LANES), 1)
    place = jnp.where(to == 2 * (at % ROWS) + at // ROWS, 1.0, 0.0).astype(BF16)

    def placed(right, left):
        both = jnp.concatenate([right[...], left[...]], axis=0)
        return lax.dot_general(both, place, (((0,), (0,)), ((), ())), preferred_element_type=F32)

    own, near = placed(dr, dl), placed(rights, lefts)
    sides = (0.5 * (own[SPAN:] + near[SPAN:]) + MID) * (own[:SPAN] - near[:SPAN])
    lane = lax.broadcasted_iota(jnp.int32, (ROWS, LANES), 1)
    halves = (0, ROWS)

    def load(ref, w, s):
        return ref[pl.ds(block_row(w, s), ROWS), :]

    def results(q):
        rows = pl.ds(4 * q, 4)
        return pltpu.make_async_copy(r_buf.at[rows], out.at[rows], sems.at[q])

    def four(q, carry):
        carry = list(carry)
        for n in range(4):
            w = 4 * q + n
            for h, s in enumerate(halves):
                xc, hc = load(xe, w, s), load(he, w, s)
                above = gk[pl.ds(SPAN * (w + 1) + s, ROWS), :] * (xc - load(xe, w + 1, s))
                total = above - carry[h]
                carry[h] = above
                for d in (-1, 1):
                    total += (hc + load(he, w, s + d)) * (xc - load(xe, w, s + d))
                side = pltpu.roll(sides[s : s + ROWS], LANES - 1 - 2 * w, 1)
                right = gx[pl.ds(SPAN * w + s, ROWS), :] * (xc - pltpu.roll(xc, LANES - 1, 1))
                total += jnp.where(lane == LANES - 1, side, right)
                total += jnp.where(lane == 0, side, -pltpu.roll(right, 1, 1))
                r_buf[w, s : s + ROWS, :] = b_ref[w, s : s + ROWS, :] - (xc + total)
        results(q).start()
        return tuple(carry)

    start = [gk[s : s + ROWS, :] * (load(xe, -1, s) - load(xe, 0, s)) for s in halves]
    lax.fori_loop(0, ROWS // 4, four, tuple(start))
    for q in range(ROWS // 4):
        results(q).wait()


def block_edges(es, dl, dr):
    streams = lax.axis_size("stream")
    right = [(i, (i + 1) % streams) for i in range(streams)]
    left = [((i + 1) % streams, i) for i in range(streams)]
    return (
        lax.ppermute(es, "span", [(0, 1), (1, 0)]),
        lax.ppermute(dr, "stream", right),
        lax.ppermute(dl, "stream", left),
    )


def line_shift(value, ds, dx):
    spans, streams = lax.axis_size("span"), lax.axis_size("stream")

    def device(sb, xb):
        sp, y = divmod(sb % (spans * WY), WY)
        st, z = divmod(xb % (streams * WZ), WZ)
        y, z = (WY - 1 - y if sp % 2 else y), (WZ - 1 - z if st % 2 else z)
        return ((y * WZ + z) * spans + sp) * streams + st

    pairs = [
        (device(sb, xb), device(sb + ds, xb + dx))
        for sb in range(spans * WY)
        for xb in range(streams * WZ)
    ]
    return lax.ppermute(value, ("wall", "span", "stream"), pairs)


def line_edges(*edges):
    return (
        line_shift(edges[1], 1, 0),
        line_shift(edges[0], -1, 0),
        line_shift(edges[3], 0, 1),
        line_shift(edges[2], 0, -1),
    )


def body(right_side, viscosity, wall_metric, line_inverse):
    block = pltpu.VMEM((ROWS, SPAN, LANES), F32)
    side = pltpu.VMEM((8, ROWS, LANES), BF16)
    dense = shape((ROWS, LANES), BF16)
    hbm, vmem = pl.BlockSpec(memory_space=pltpu.HBM), pl.BlockSpec(memory_space=pltpu.VMEM)
    sent = (WY * WZ, 4 * ROWS + TAIL, LANES)
    loose = pltpu.VMEM(((SPAN + 1) * ROWS, LANES), F32)
    dma = pltpu.SemaphoreType.DMA
    send, *v_edges = call(
        pack,
        (shape(sent, BF16), shape((2, ROWS, LANES), BF16), dense, dense),
        (
            loose,
            loose,
            pltpu.VMEM((1, ROWS), F32),
            pltpu.VMEM(sent, BF16),
            pltpu.VMEM((2, ROWS, LANES), BF16),
            pltpu.VMEM((ROWS, LANES), BF16),
            pltpu.VMEM((ROWS, LANES), BF16),
            side,
            side,
            dma((2, ROWS)),
            dma((WY,)),
            dma((4,)),
        ),
        62 * MIB + MIB // 2,
        in_specs=(hbm,) * 3,
        out_specs=(hbm,) * 4,
    )(right_side, viscosity, wall_metric.reshape(1, ROWS))
    recv = lax.all_to_all(send, "wall", 0, 0, tiled=True)
    field = shape((CHUNKS * ROW_COUNT, LANES), F32)
    bf, hf, b0, metric, ends, *edges = call(
        to_lines,
        (field, field, shape((BUSY, NW), BF16), shape((1, NW), F32))
        + (shape((WY * WZ, 4, LANES), F32),)
        + (shape((2 * BX, NW), BF16),) * 4,
    )(recv)
    near = line_edges(*edges)
    x1, fw = call(first_lines, (field, field))(b0, hf, metric, line_inverse)
    ext = pltpu.VMEM((CHUNKS * ROW_COUNT, LANES), F32)
    rounded = pltpu.VMEM((BUSY, NW), BF16)
    x2, d2, he, *edges = call(
        second_step,
        (field, field, field) + (shape((BX, NW), BF16),) * 4,
        (ext, rounded, pltpu.VMEM((4 * BX, NW), BF16)),
    )(x1, bf, hf, fw, *near, line_inverse, metric)
    x_near = line_edges(*edges)
    send = call(
        third_step, shape((WY * WZ, 2 * ROWS + TAIL, LANES), BF16), (ext, rounded)
    )(x2, d2, bf, he, fw, *x_near, line_inverse, metric, ends)
    recv = lax.all_to_all(send, "wall", 0, 0, tiled=True)
    cells = shape((BLOCK_ROWS, LANES), F32)
    xf, kappas, *edges = call(
        unpack,
        (cells, shape((2 * SPAN, LANES), F32), shape((4, ROWS, LANES), BF16), dense, dense),
        (side, side),
    )(recv, *v_edges)
    x_edges = block_edges(*edges)
    whole = shape(right_side.shape, F32)
    smem = pl.BlockSpec(memory_space=pltpu.SMEM)
    x3, hf, gx, gk = call(
        stage,
        (
            whole,
            cells,
            shape((ROWS * SPAN, LANES), F32),
            shape(((ROWS + 1) * SPAN, LANES), F32),
        ),
        (block, dma((ROWS // 4,))),
        in_specs=(vmem, vmem, vmem, smem),
        out_specs=(hbm, vmem, vmem, vmem),
    )(xf, viscosity, kappas, wall_metric)
    loose = pltpu.VMEM((BLOCK_ROWS, LANES), F32)
    residual = call(
        last_resid,
        whole,
        (loose, loose, block, dma((ROWS // 4,))),
        out_specs=hbm,
    )(xf, hf, gx, gk, right_side, *x_edges, *edges[1:])
    return x3, residual


def solution(mesh):
    in_specs = (P("wall", "span", "stream"), P("wall", "span", "stream"), P("wall"), P())
    out_specs = (P("wall", "span", "stream"), P("wall", "span", "stream"))
    return jax.shard_map(body, mesh=mesh, in_specs=in_specs, out_specs=out_specs, check_vma=False)
```

profile of v0, /device:TPU:1, one launch (start us, length us, event | category | flops | bytes accessed | tf_op | source)
XLA Modules:
  0.0 106.1 jit_solution(1640119694493189324)
XLA Ops:
  0.6 4.0 %shard_map.59 = (bf16[32,136,128]{2,1,0:T(8,128)(2,1)}, bf16[2,32,128]{2,1,0:T(8,128)(2,1)}, bf16[32,128]{1,0:T(8,128)(2,1)}, bf16[32,128]{1,0:T(8,128)(2,1)}) custom-call(f32[32,64,128]{2,1,0:T(8,128)} %b_ref.1, f32[32,64,128]{2,1,0:T(8,128)} %v_ref.1, f32[1,32]{1,0:T(1,128)} %bitcast.1), custom_call_target="tpu_custom_call" | custom-call | flops 10000000 | bytes 4000000 | tf_op jit(solution)/shard_map/pallas_call | solution.py:500
  4.7 0.0 copy-start
  4.7 42.6 %all_to_all.10.recv = bf16[32,136,128]{2,1,0:T(8,128)(2,1)S(1)} all-to-all(bf16[32,136,128]{2,1,0:T(8,128)(2,1)} %get-tuple-element.33), channel_id=1, replica_groups=mesh['wall'=32,'span'=2,'stream'=4] {'wall'}, dimensions={0} | all-to-all | bytes 2228224 | tf_op jit(solution)/shard_map/all_to_all | solution.py:521
  47.3 0.7 shard_map.60
  47.9 0.4 collective-permute-start
  48.3 2.7 %collective-permute-start.1 = (bf16[32,1024]{1,0:T(8,128)(2,1)S(1)}, bf16[32,1024]{1,0:T(8,128)(2,1)S(1)}, u32[]{:S(2)}, u32[]{:S(2)}) collective-permute-start(bf16[32,1024]{1,0:T(8,128)(2,1)S(1)} %get-tuple-element.41), channel_id=1, source_target_pairs={{0,4},{8,12},{16,20},{24,28},{32,36},{40,44},{48,52},{56,60},{57,6... | collective-permute-start | bytes 196616 | tf_op jit(solution)/shard_map/ppermute | solution.py:480
  51.0 3.9 %collective-permute-start.2 = (bf16[32,1024]{1,0:T(8,128)(2,1)S(1)}, bf16[32,1024]{1,0:T(8,128)(2,1)S(1)}, u32[]{:S(2)}, u32[]{:S(2)}) collective-permute-start(bf16[32,1024]{1,0:T(8,128)(2,1)S(1)} %get-tuple-element.42), channel_id=1, source_target_pairs={{0,8},{8,16},{16,24},{24,32},{32,40},{40,48},{48,56},{56,57},{57,4... | collective-permute-start | bytes 196616 | tf_op jit(solution)/shard_map/ppermute | solution.py:480
  54.9 1.5 %shard_map.61 = (f32[2688,128]{1,0:T(8,128)S(1)}, f32[2688,128]{1,0:T(8,128)S(1)}) custom-call(bf16[288,1024]{1,0:T(8,128)(2,1)S(1)} %get-tuple-element.34.b0, f32[2688,128]{1,0:T(8,128)S(1)} %get-tuple-element.35.hf, f32[1,1024]{1,0:T(1,128)S(1)} %get-tuple-element.36.metric, bf16[1024,1024]{1,0:T(8,128)(2,1)S(1)} %copy-done), custom_call_target="tpu_custom_call" | custom-call | flops 10000000 | bytes 4000000 | tf_op jit(solution)/shard_map/pallas_call | solution.py:530
  56.5 2.1 %collective-permute-done.3.xr = bf16[32,1024]{1,0:T(8,128)(2,1)S(1)} collective-permute-done((bf16[32,1024]{1,0:T(8,128)(2,1)S(1)}, bf16[32,1024]{1,0:T(8,128)(2,1)S(1)}, u32[]{:S(2)}, u32[]{:S(2)}) %collective-permute-start.3) | collective-permute-done | bytes 65568 | tf_op jit(solution)/shard_map/ppermute | solution.py:480
  58.6 3.7 %shard_map.62 = (f32[2688,128]{1,0:T(8,128)S(1)}, f32[2688,128]{1,0:T(8,128)S(1)}, f32[2688,128]{1,0:T(8,128)S(1)}, bf16[16,1024]{1,0:T(8,128)(2,1)S(1)}, bf16[1...) custom-call(f32[2688,128]{1,0:T(8,128)S(1)} %get-tuple-element.37.x1, ...), custom_call_target="tpu_custom_call" | custom-call | flops 10000000 | bytes 4000000 | tf_op jit(solution)/shard_map/pallas_call | solution.py:533
  62.2 0.1 collective-permute-start.4
  62.3 3.0 %collective-permute-start.5 = (bf16[16,1024]{1,0:T(8,128)(2,1)S(1)}, bf16[16,1024]{1,0:T(8,128)(2,1)S(1)}, u32[]{:S(2)}, u32[]{:S(2)}) collective-permute-start(bf16[16,1024]{1,0:T(8,128)(2,1)S(1)} %get-tuple-element.48), channel_id=1, source_target_pairs={{0,4},{8,12},{16,20},{24,28},{32,36},{40,44},{48,52},{56,60},{57,6... | collective-permute-start | bytes 98312 | tf_op jit(solution)/shard_map/ppermute | solution.py:480
  65.3 2.0 %collective-permute-start.6 = (bf16[16,1024]{1,0:T(8,128)(2,1)S(1)}, bf16[16,1024]{1,0:T(8,128)(2,1)S(1)}, u32[]{:S(2)}, u32[]{:S(2)}) collective-permute-start(bf16[16,1024]{1,0:T(8,128)(2,1)S(1)} %get-tuple-element.49), channel_id=1, source_target_pairs={{0,8},{8,16},{16,24},{24,32},{32,40},{40,48},{48,56},{56,57},{57,4... | collective-permute-start | bytes 98312 | tf_op jit(solution)/shard_map/ppermute | solution.py:480
  67.4 1.0 collective-permute-done.6.xl
  68.4 2.3 %collective-permute-done.7.xr = bf16[16,1024]{1,0:T(8,128)(2,1)S(1)} collective-permute-done((bf16[16,1024]{1,0:T(8,128)(2,1)S(1)}, bf16[16,1024]{1,0:T(8,128)(2,1)S(1)}, u32[]{:S(2)}, u32[]{:S(2)}) %collective-permute-start.7) | collective-permute-done | bytes 32800 | tf_op jit(solution)/shard_map/ppermute | solution.py:480
  70.7 3.2 %shard_map.63 = bf16[32,72,128]{2,1,0:T(8,128)(2,1)S(1)} custom-call(f32[2688,128]{1,0:T(8,128)S(1)} %get-tuple-element.44.x2, f32[2688,128]{1,0:T(8,128)S(1)} %get-tuple-element.45.d2, f32[2688,128]{1,0:T(8,128)S(1)} %get-tuple-element.38.bf, f32[2688,128]{1,0:T(8,128)S(1)} %get-tuple-element.46.he, f32[2688,128]{1,0:T(8,128)S(1)} %get-tuple-element.39.fw, ...), custom_call_target="tpu_custom_call" | custom-call | flops 10000000 | bytes 4000000 | tf_op jit(solution)/shard_map/pallas_call | solution.py:539
  73.9 0.0 copy-start.2
  74.0 18.2 %all_to_all.11.recv = bf16[32,72,128]{2,1,0:T(8,128)(2,1)S(1)} all-to-all(bf16[32,72,128]{2,1,0:T(8,128)(2,1)S(1)} %shard_map.63), channel_id=1, replica_groups=mesh['wall'=32,'span'=2,'stream'=4] {'wall'}, dimensions={0} | all-to-all | bytes 1179648 | tf_op jit(solution)/shard_map/all_to_all | solution.py:542
  92.2 0.8 shard_map.64
  93.0 0.3 collective-permute-start.8
  93.4 6.3 %collective-permute-start.9 = (bf16[32,128]{1,0:T(8,128)(2,1)S(1)}, bf16[32,128]{1,0:T(8,128)(2,1)S(1)}, u32[]{:S(2)}, u32[]{:S(2)}) collective-permute-start(bf16[32,128]{1,0:T(8,128)(2,1)S(1)} %get-tuple-element.62.dr), channel_id=1, source_target_pairs={{0,1},{1,2},{2,3},{3,0},{4,5},{5,6},{6,7},{7,4},{8,9},{9,10},{10,1... | collective-permute-start | bytes 24584 | tf_op jit(solution)/shard_map/ppermute | solution.py:461
  99.7 2.0 %shard_map.65 = (f32[32,64,128]{2,1,0:T(8,128)}, f32[2280,128]{1,0:T(8,128)S(1)}, f32[2048,128]{1,0:T(8,128)S(1)}, f32[2112,128]{1,0:T(8,128)S(1)}) custom-call(f32[2280,128]{1,0:T(8,128)S(1)} %get-tuple-element.55.xf, f32[32,64,128]{2,1,0:T(8,128)S(1)} %copy-done.2, f32[128,128]{1,0:T(8,128)S(1)} %get-tuple-element.56.kappas, f32[32]{0:T(128)S(1)} %copy-done.6), custom_call_target="tpu_custom_call" | custom-call | flops 10000000 | bytes 4000000 | tf_op jit(solution)/shard_map/pallas_call | solution.py:552
  101.7 1.3 %collective-permute-done.10.rights = bf16[32,128]{1,0:T(8,128)(2,1)S(1)} collective-permute-done((bf16[32,128]{1,0:T(8,128)(2,1)S(1)}, bf16[32,128]{1,0:T(8,128)(2,1)S(1)}, u32[]{:S(2)}, u32[]{:S(2)}) %collective-permute-start.10) | collective-permute-done | bytes 8224 | tf_op jit(solution)/shard_map/ppermute | solution.py:462
  103.0 2.9 %shard_map.66 = f32[32,64,128]{2,1,0:T(8,128)} custom-call(f32[2280,128]{1,0:T(8,128)S(1)} %get-tuple-element.55.xf, f32[2280,128]{1,0:T(8,128)S(1)} %get-tuple-element.58.hf, f32[2048,128]{1,0:T(8,128)S(1)} %get-tuple-element.59.gx, f32[2112,128]{1,0:T(8,128)S(1)} %get-tuple-element.60.gk, f32[32,64,128]{2,1,0:T(8,128)S(1)} %copy-done.1, ...), custom_call_target="tpu_custom_call" | custom-call | flops 10000000 | bytes 4000000 | tf_op jit(solution)/shard_map/pallas_call | solution.py:565
  (22 shorter events, 0.1 us)
Async XLA Ops:
  4.7 50.2 %copy-start = (bf16[1024,1024]{1,0:T(8,128)(2,1)S(1)}, bf16[1024,1024]{1,0:T(8,128)(2,1)}, u32[]{:S(2)}) copy-start(bf16[1024,1024]{1,0:T(8,128)(2,1)} %line.5) | copy-start | bytes 6291460
  47.9 8.5 %collective-permute-start = (bf16[32,1024]{1,0:T(8,128)(2,1)S(1)}, bf16[32,1024]{1,0:T(8,128)(2,1)S(1)}, u32[]{:S(2)}, u32[]{:S(2)}) collective-permute-start(bf16[32,1024]{1,0:T(8,128)(2,1)S(1)} %get-tuple-element.40), channel_id=1, source_target_pairs={{0,64},{8,72},{16,80},{24,88},{32,96},{40,104},{48,112},{56,120},{... | collective-permute-start | bytes 196616 | tf_op jit(solution)/shard_map/ppermute | solution.py:480
  48.3 8.1 %collective-permute-start.1 = (bf16[32,1024]{1,0:T(8,128)(2,1)S(1)}, bf16[32,1024]{1,0:T(8,128)(2,1)S(1)}, u32[]{:S(2)}, u32[]{:S(2)}) collective-permute-start(bf16[32,1024]{1,0:T(8,128)(2,1)S(1)} %get-tuple-element.41), channel_id=1, source_target_pairs={{0,4},{8,12},{16,20},{24,28},{32,36},{40,44},{48,52},{56,60},{57,6... | collective-permute-start | bytes 196616 | tf_op jit(solution)/shard_map/ppermute | solution.py:480
  51.0 5.5 %collective-permute-start.2 = (bf16[32,1024]{1,0:T(8,128)(2,1)S(1)}, bf16[32,1024]{1,0:T(8,128)(2,1)S(1)}, u32[]{:S(2)}, u32[]{:S(2)}) collective-permute-start(bf16[32,1024]{1,0:T(8,128)(2,1)S(1)} %get-tuple-element.42), channel_id=1, source_target_pairs={{0,8},{8,16},{16,24},{24,32},{32,40},{40,48},{48,56},{56,57},{57,4... | collective-permute-start | bytes 196616 | tf_op jit(solution)/shard_map/ppermute | solution.py:480
  54.9 3.7 %collective-permute-start.3 = (bf16[32,1024]{1,0:T(8,128)(2,1)S(1)}, bf16[32,1024]{1,0:T(8,128)(2,1)S(1)}, u32[]{:S(2)}, u32[]{:S(2)}) collective-permute-start(bf16[32,1024]{1,0:T(8,128)(2,1)S(1)} %get-tuple-element.43), channel_id=1, source_target_pairs={{0,3},{8,0},{16,8},{24,16},{32,24},{40,32},{48,40},{56,48},{57,56}... | collective-permute-start | bytes 196616 | tf_op jit(solution)/shard_map/ppermute | solution.py:480
  62.2 5.1 %collective-permute-start.4 = (bf16[16,1024]{1,0:T(8,128)(2,1)S(1)}, bf16[16,1024]{1,0:T(8,128)(2,1)S(1)}, u32[]{:S(2)}, u32[]{:S(2)}) collective-permute-start(bf16[16,1024]{1,0:T(8,128)(2,1)S(1)} %get-tuple-element.47), channel_id=1, source_target_pairs={{0,64},{8,72},{16,80},{24,88},{32,96},{40,104},{48,112},{56,120},{... | collective-permute-start | bytes 98312 | tf_op jit(solution)/shard_map/ppermute | solution.py:480
  62.3 5.0 %collective-permute-start.5 = (bf16[16,1024]{1,0:T(8,128)(2,1)S(1)}, bf16[16,1024]{1,0:T(8,128)(2,1)S(1)}, u32[]{:S(2)}, u32[]{:S(2)}) collective-permute-start(bf16[16,1024]{1,0:T(8,128)(2,1)S(1)} %get-tuple-element.48), channel_id=1, source_target_pairs={{0,4},{8,12},{16,20},{24,28},{32,36},{40,44},{48,52},{56,60},{57,6... | collective-permute-start | bytes 98312 | tf_op jit(solution)/shard_map/ppermute | solution.py:480
  65.3 3.1 %collective-permute-start.6 = (bf16[16,1024]{1,0:T(8,128)(2,1)S(1)}, bf16[16,1024]{1,0:T(8,128)(2,1)S(1)}, u32[]{:S(2)}, u32[]{:S(2)}) collective-permute-start(bf16[16,1024]{1,0:T(8,128)(2,1)S(1)} %get-tuple-element.49), channel_id=1, source_target_pairs={{0,8},{8,16},{16,24},{24,32},{32,40},{40,48},{48,56},{56,57},{57,4... | collective-permute-start | bytes 98312 | tf_op jit(solution)/shard_map/ppermute | solution.py:480
  67.3 3.3 %collective-permute-start.7 = (bf16[16,1024]{1,0:T(8,128)(2,1)S(1)}, bf16[16,1024]{1,0:T(8,128)(2,1)S(1)}, u32[]{:S(2)}, u32[]{:S(2)}) collective-permute-start(bf16[16,1024]{1,0:T(8,128)(2,1)S(1)} %get-tuple-element.50), channel_id=1, source_target_pairs={{0,3},{8,0},{16,8},{24,16},{32,24},{40,32},{48,40},{56,48},{57,56}... | collective-permute-start | bytes 98312 | tf_op jit(solution)/shard_map/ppermute | solution.py:480
  70.7 21.5 %copy-start.3 = (bf16[2,32,128]{2,1,0:T(8,128)(2,1)S(1)}, bf16[2,32,128]{2,1,0:T(8,128)(2,1)}, u32[]{:S(2)}) copy-start(bf16[2,32,128]{2,1,0:T(8,128)(2,1)} %get-tuple-element.52.ves) | copy-start | bytes 49156
  70.7 21.5 %copy-start.4 = (bf16[32,128]{1,0:T(8,128)(2,1)S(1)}, bf16[32,128]{1,0:T(8,128)(2,1)}, u32[]{:S(2)}) copy-start(bf16[32,128]{1,0:T(8,128)(2,1)} %get-tuple-element.53.vdl) | copy-start | bytes 24580
  70.7 21.5 %copy-start.5 = (bf16[32,128]{1,0:T(8,128)(2,1)S(1)}, bf16[32,128]{1,0:T(8,128)(2,1)}, u32[]{:S(2)}) copy-start(bf16[32,128]{1,0:T(8,128)(2,1)} %get-tuple-element.54.vdr) | copy-start | bytes 24580
  73.9 25.7 %copy-start.2 = (f32[32,64,128]{2,1,0:T(8,128)S(1)}, f32[32,64,128]{2,1,0:T(8,128)}, u32[]{:S(2)}) copy-start(f32[32,64,128]{2,1,0:T(8,128)} %v_ref.1) | copy-start | bytes 3145732
  74.0 25.7 %copy-start.6 = (f32[32]{0:T(128)S(1)}, f32[32]{0:T(128)}, u32[]{:S(2)}) copy-start(f32[32]{0:T(128)} %m_ref.1) | copy-start | bytes 388
  92.2 10.9 %copy-start.1 = (f32[32,64,128]{2,1,0:T(8,128)S(1)}, f32[32,64,128]{2,1,0:T(8,128)}, u32[]{:S(2)}) copy-start(f32[32,64,128]{2,1,0:T(8,128)} %b_ref.1) | copy-start | bytes 3145732
  93.0 10.0 %collective-permute-start.8 = (bf16[4,32,128]{2,1,0:T(8,128)(2,1)S(1)}, bf16[4,32,128]{2,1,0:T(8,128)(2,1)S(1)}, u32[]{:S(2)}, u32[]{:S(2)}) collective-permute-start(bf16[4,32,128]{2,1,0:T(8,128)(2,1)S(1)} %get-tuple-element.61), channel_id=1, source_target_pairs={{0,4},{4,0},{1,5},{5,1},{2,6},{6,2},{3,7},{7,3},{8,12},{12,8},{9,1... | collective-permute-start | bytes 98312 | tf_op jit(solution)/shard_map/ppermute | solution.py:460
  93.4 8.4 %collective-permute-start.9 = (bf16[32,128]{1,0:T(8,128)(2,1)S(1)}, bf16[32,128]{1,0:T(8,128)(2,1)S(1)}, u32[]{:S(2)}, u32[]{:S(2)}) collective-permute-start(bf16[32,128]{1,0:T(8,128)(2,1)S(1)} %get-tuple-element.62.dr), channel_id=1, source_target_pairs={{0,1},{1,2},{2,3},{3,0},{4,5},{5,6},{6,7},{7,4},{8,9},{9,10},{10,1... | collective-permute-start | bytes 24584 | tf_op jit(solution)/shard_map/ppermute | solution.py:461
  99.6 3.4 %collective-permute-start.10 = (bf16[32,128]{1,0:T(8,128)(2,1)S(1)}, bf16[32,128]{1,0:T(8,128)(2,1)S(1)}, u32[]{:S(2)}, u32[]{:S(2)}) collective-permute-start(bf16[32,128]{1,0:T(8,128)(2,1)S(1)} %get-tuple-element.63.dl), channel_id=1, source_target_pairs={{1,0},{2,1},{3,2},{0,3},{5,4},{6,5},{7,6},{4,7},{9,8},{10,9},{11,1... | collective-permute-start | bytes 24584 | tf_op jit(solution)/shard_map/ppermute | solution.py:462
where the time goes:
time: 106 us
  blocking collectives  60.8 us (57%)
  Pallas kernels  18.9 us (18%)
  starting transfers between devices  18.7 us (18%)
  waiting for transfers between devices  6.77 us (6%)
    all_to_all x2, blocking collectives, body(): recv = lax.all_to_all(send, 'wall', 0, 0, tiled=True)  60.8 us
    ppermute x8, starting transfers between devices, line_shift(): return lax.ppermute(value, ('wall', 'span', 'stream'), pairs)  12.1 us
    ppermute x1, starting transfers between devices, block_edges(): lax.ppermute(dr, 'stream', right)  6.3 us
    ppermute x8, waiting for transfers between devices, line_shift(): return lax.ppermute(value, ('wall', 'span', 'stream'), pairs)  5.46 us
    pallas_call x1, Pallas kernels, body(): call(pack, (shape(sent, BF16), shape((2, ROWS, LANES), BF16), dense, dens...  4.03 us
    pallas_call x1, Pallas kernels, body(): call(second_step, (field, field, field) + (shape((BX, NW), BF16),) * 4, (...  3.65 us
    pallas_call x1, Pallas kernels, body(): call(third_step, shape((WY * WZ, 2 * ROWS + TAIL, LANES), BF16), (ext, ro...  3.24 us
    pallas_call x1, Pallas kernels, body(): call(last_resid, whole, (loose, loose, block, dma((ROWS // 4,))), out_spe...  2.89 us
  transfers between devices with their start and end apart: 11, of which 4 were waited for; matrix products, arithmetic and copies ran while one was open for 0% of the time, Pallas kernels for 3%

commit v1 on v0

--- a/solution.py
+++ b/solution.py
@@ -202,6 +202,7 @@
         for n, rows in enumerate(edge_rows(i)):
             edges[n][:BX, lanes] = bf[rows, :].astype(BF16)
             edges[n][BX:, lanes] = (2.0 * hf[rows, :] - MID).astype(BF16)
+    mirror(hf)
 
 
 def line_rows(i, s):
@@ -228,6 +229,12 @@
     )
 
 
+def mirror(field):
+    for i in range(CHUNKS):
+        for near, edge in zip(near_rows(i), edge_rows(i)):
+            field[near, :] = field[edge, :]
+
+
 def busy(i):
     return pl.ds(ROW_COUNT * i + FIRST, BUSY)
 
@@ -236,10 +243,11 @@
     return lax.dot_general(rows, line, (((1,), (1,)), ((), ())), preferred_element_type=F32)
 
 
-def first_lines(b0, hf, metric, line, x1, fw):
+def first_lines(b0, bf, hf, metric, line, x1, fw, resid):
     y = WEIGHTS[0][1] * apply_lines(b0[...], line[...])
     for i in range(CHUNKS):
         x1[busy(i), :] = y[:, i * LANES : (i + 1) * LANES]
+    mirror(x1)
     last = lax.broadcasted_iota(jnp.int32, (RUN, LANES), 1) == LANES - 1
 
     def one(c, _):
@@ -253,6 +261,7 @@
         return 0
 
     lax.fori_loop(0, BUSY // RUN, one, 0)
+    line_resid(bf, x1, hf, fw, metric, resid)
 
 
 def line_resid(bf, xe, he, fw, metric, out):
@@ -278,26 +287,33 @@
             total = above - jnp.where(first, entry, below)
             for shift in (-LP, -1, 1, LP):
                 total += (hc + load(he, i, shift)) * (xc - load(xe, i, shift))
-            rows = pl.ds(pl.multiple_of(RUN * c, BX), RUN)
-            out[rows, i * LANES : (i + 1) * LANES] = (load(bf, i) - (xc + total)).astype(BF16)
+            out[pl.ds(ROW_COUNT * i + FIRST + RUN * c, RUN), :] = load(bf, i) - (xc + total)
             xc, moved_x, entry = after, moved_after, below
         return 0
 
     lax.fori_loop(0, BUSY // RUN, one, 0)
 
 
-def second_step(x1, bf, hf, fw, su, sd, xl, xr, line, metric, x2, d2, he, e0, e1, e2, e3, xe, rt, ends):
-    for k, ref in enumerate((su, sd, xl, xr)):
+def finish_resid(resid, x, hf, near, x_near, out, rounded):
+    for i in range(CHUNKS):
+        lanes = slice(i * LANES, (i + 1) * LANES)
+        out[busy(i), :] = resid[busy(i), :]
+        for k, rows in enumerate(edge_rows(i)):
+            weight = hf[rows, :] + 0.5 * near[k][BX:, lanes].astype(F32) + 0.5 * MID
+            out[rows, :] = out[rows, :] - weight * (x[rows, :] - x_near(k, i))
+        rounded[:, lanes] = out[busy(i), :].astype(BF16)
+
+
+def second_step(resid, x1, hf, su, sd, xl, xr, line, x2, d2, e0, e1, e2, e3, full, rt, ends):
+    near = (su, sd, xl, xr)
+    for k, ref in enumerate(near):
         ends[k * BX : (k + 1) * BX] = ref[0:BX]
     ends1 = WEIGHTS[0][1] * apply_lines(ends[...], line[...])
-    for i in range(CHUNKS):
-        lanes = slice(i * LANES, (i + 1) * LANES)
-        xe[busy(i), :] = x1[busy(i), :]
-        he[busy(i), :] = hf[busy(i), :]
-        for k, (rows, ref) in enumerate(zip(near_rows(i), (su, sd, xl, xr))):
-            xe[rows, :] = ends1[k * BX : (k + 1) * BX, lanes]
-            he[rows, :] = 0.5 * ref[BX : 2 * BX, lanes].astype(F32) + 0.5 * MID
-    line_resid(bf, xe, he, fw, metric, rt)
+
+    def x_near(k, i):
+        return ends1[k * BX : (k + 1) * BX, i * LANES : (i + 1) * LANES]
+
+    finish_resid(resid, x1, hf, near, x_near, full, rt)
     keep, scale = WEIGHTS[1]
     y = scale * apply_lines(rt[...], line[...])
     for i in range(CHUNKS):
@@ -308,15 +324,18 @@
         x2[busy(i), :] = x + d
         for rows, ref in zip(edge_rows(i), (e0, e1, e2, e3)):
             ref[:, lanes] = x2[rows, :].astype(BF16)
-
-
-def third_step(x2, d2, bf, he, fw, su, sd, xl, xr, line, metric, ends, send, xe, rt):
-    for i in range(CHUNKS):
-        lanes = slice(i * LANES, (i + 1) * LANES)
-        xe[busy(i), :] = x2[busy(i), :]
-        for rows, ref in zip(near_rows(i), (su, sd, xl, xr)):
-            xe[rows, :] = ref[:, lanes].astype(F32)
-    line_resid(bf, xe, he, fw, metric, rt)
+    mirror(x2)
+
+
+def third_step(
+    resid, x2, d2, hf, su, sd, xl, xr, vsu, vsd, vxl, vxr, line, ends, send, xe, rt
+):
+    x_edges = (su, sd, xl, xr)
+
+    def x_near(k, i):
+        return x_edges[k][:, i * LANES : (i + 1) * LANES].astype(F32)
+
+    finish_resid(resid, x2, hf, (vsu, vsd, vxl, vxr), x_near, xe, rt)
     keep, scale = WEIGHTS[2]
     y = scale * apply_lines(rt[...], line[...])
     count = WY * WZ
@@ -343,6 +362,10 @@
     return CP * (w + 1) + 1 + s
 
 
+def block_span(s):
+    return pl.ds(block_row(0, s), ROWS, stride=CP)
+
+
 def unpack(recv, ves, vdl, vdr, xf, kappas, es, dl, dr, cl, cr):
     def one(t, _):
         for g in range(2):
@@ -365,24 +388,18 @@
         return 0
 
     lax.fori_loop(0, WY, one, 0)
-    es[0] = xf[pl.ds(block_row(0), ROWS, stride=CP), :].astype(BF16)
-    es[1] = xf[pl.ds(block_row(0, SPAN - 1), ROWS, stride=CP), :].astype(BF16)
+    for k, (s, beside) in enumerate(((0, -1), (SPAN - 1, SPAN))):
+        edge = xf[block_span(s), :]
+        xf[block_span(beside), :] = edge
+        es[k] = edge.astype(BF16)
     es[2] = ves[0]
     es[3] = ves[1]
     dl[...] = edge_lanes(cl[...], 0, 0, 0) + vdl[...]
     dr[...] = edge_lanes(cr[...], BX - 1, 1, 0) + vdr[...]
 
 
-def stage(xf, v_ref, kappas, m_ref, x3, hf, gx, gk, x_buf, sems):
-    def result(n):
-        rows = pl.ds(4 * n, 4)
-        return pltpu.make_async_copy(x_buf.at[rows], x3.at[rows], sems.at[n])
-
+def weights(v_ref, m_ref, hf, gx, gk):
     def four(n, below):
-        for k in range(4):
-            w = 4 * n + k
-            x_buf[w] = xf[pl.ds(block_row(w), SPAN), :]
-        result(n).start()
         for k in range(4):
             w = 4 * n + k
             half = 0.5 * v_ref[w]
@@ -394,60 +411,86 @@
             below = half
         return below
 
-    below = lax.fori_loop(0, ROWS // 4, four, 0.5 * kappas[:SPAN, :])
-    gk[SPAN * ROWS :, :] = below + 0.5 * kappas[SPAN:, :]
-    for n in range(ROWS // 4):
-        result(n).wait()
-
-
-def last_resid(xf, hf, gx, gk, b_ref, spans, lefts, rights, dl, dr, out, xe, he, r_buf, sems):
-    xe[...] = xf[...]
-    he[...] = hf[...]
-    for s, k in ((-1, 1), (SPAN, 0)):
-        rows = pl.ds(block_row(0, s), ROWS, stride=CP)
-        xe[rows, :] = spans[k].astype(F32)
-        he[rows, :] = 0.5 * spans[2 + k].astype(F32) + 0.5 * MID
-    at = lax.broadcasted_iota(jnp.int32, (2 * ROWS, LANES), 0)
-    to = lax.broadcasted_iota(jnp.int32, (2 * ROWS, LANES), 1)
-    place = jnp.where(to == 2 * (at % ROWS) + at // ROWS, 1.0, 0.0).astype(BF16)
-
-    def placed(right, left):
-        both = jnp.concatenate([right[...], left[...]], axis=0)
-        return lax.dot_general(both, place, (((0,), (0,)), ((), ())), preferred_element_type=F32)
-
-    own, near = placed(dr, dl), placed(rights, lefts)
-    sides = (0.5 * (own[SPAN:] + near[SPAN:]) + MID) * (own[:SPAN] - near[:SPAN])
+    gk[SPAN * ROWS :, :] = lax.fori_loop(0, ROWS // 4, four, jnp.zeros((SPAN, LANES), F32))
+    for s in (-1, SPAN):
+        hf[block_span(s), :] = jnp.zeros((ROWS, LANES), F32)
+
+
+def inner_resid(xf, hf, gx, gk, kappas, b_ref, x3, resid, x_buf, sems):
     lane = lax.broadcasted_iota(jnp.int32, (ROWS, LANES), 1)
     halves = (0, ROWS)
 
     def load(ref, w, s):
         return ref[pl.ds(block_row(w, s), ROWS), :]
 
-    def results(q):
-        rows = pl.ds(4 * q, 4)
-        return pltpu.make_async_copy(r_buf.at[rows], out.at[rows], sems.at[q])
+    def result(n):
+        rows = pl.ds(4 * n, 4)
+        return pltpu.make_async_copy(x_buf.at[rows], x3.at[rows], sems.at[n])
 
     def four(q, carry):
         carry = list(carry)
         for n in range(4):
             w = 4 * q + n
+            top = jnp.where(w == ROWS - 1, 0.5, 0.0)
             for h, s in enumerate(halves):
-                xc, hc = load(xe, w, s), load(he, w, s)
-                above = gk[pl.ds(SPAN * (w + 1) + s, ROWS), :] * (xc - load(xe, w + 1, s))
+                xc, hc = load(xf, w, s), load(hf, w, s)
+                x_buf[w, s : s + ROWS, :] = xc
+                weight = gk[pl.ds(SPAN * (w + 1) + s, ROWS), :] + top * kappas[SPAN + s : SPAN + s + ROWS, :]
+                above = weight * (xc - load(xf, w + 1, s))
                 total = above - carry[h]
                 carry[h] = above
                 for d in (-1, 1):
-                    total += (hc + load(he, w, s + d)) * (xc - load(xe, w, s + d))
-                side = pltpu.roll(sides[s : s + ROWS], LANES - 1 - 2 * w, 1)
+                    total += (hc + load(hf, w, s + d)) * (xc - load(xf, w, s + d))
                 right = gx[pl.ds(SPAN * w + s, ROWS), :] * (xc - pltpu.roll(xc, LANES - 1, 1))
-                total += jnp.where(lane == LANES - 1, side, right)
-                total += jnp.where(lane == 0, side, -pltpu.roll(right, 1, 1))
-                r_buf[w, s : s + ROWS, :] = b_ref[w, s : s + ROWS, :] - (xc + total)
+                right = jnp.where(lane == LANES - 1, 0.0, right)
+                total += right - pltpu.roll(right, 1, 1)
+                resid[w, s : s + ROWS, :] = b_ref[w, s : s + ROWS, :] - (xc + total)
+        result(q).start()
+        return tuple(carry)
+
+    start = []
+    for s in halves:
+        weight = gk[s : s + ROWS, :] + 0.5 * kappas[s : s + ROWS, :]
+        start.append(weight * (load(xf, -1, s) - load(xf, 0, s)))
+    lax.fori_loop(0, ROWS // 4, four, tuple(start))
+    for q in range(ROWS // 4):
+        result(q).wait()
+
+
+def last_resid(resid, xf, hf, spans, lefts, rights, dl, dr, out, side_rows, r_buf, sems):
+    for k, s in enumerate((0, SPAN - 1)):
+        weight = hf[block_span(s), :] + 0.5 * spans[3 - k].astype(F32) + 0.5 * MID
+        side_rows[k] = weight * (xf[block_span(s), :] - spans[1 - k].astype(F32))
+    at = lax.broadcasted_iota(jnp.int32, (2 * ROWS, LANES), 0)
+    to = lax.broadcasted_iota(jnp.int32, (2 * ROWS, LANES), 1)
+    place = jnp.where(to == 2 * (at % ROWS) + at // ROWS, 1.0, 0.0).astype(BF16)
+
+    def placed(right, left):
+        both = jnp.concatenate([right[...], left[...]], axis=0)
+        return lax.dot_general(both, place, (((0,), (0,)), ((), ())), preferred_element_type=F32)
+
+    own, near = placed(dr, dl), placed(rights, lefts)
+    sides = (0.5 * (own[SPAN:] + near[SPAN:]) + MID) * (own[:SPAN] - near[:SPAN])
+    lane = lax.broadcasted_iota(jnp.int32, (SPAN, LANES), 1)
+    ends = (lane == 0) | (lane == LANES - 1)
+    row = lax.broadcasted_iota(jnp.int32, (8, LANES), 0)
+
+    def results(q):
+        rows = pl.ds(4 * q, 4)
+        return pltpu.make_async_copy(r_buf.at[rows], out.at[rows], sems.at[q])
+
+    def four(q, carry):
+        for n in range(4):
+            w = 4 * q + n
+            r = resid[w] - jnp.where(ends, pltpu.roll(sides, LANES - 1 - 2 * w, 1), 0.0)
+            r_buf[w, 8 : SPAN - 8, :] = r[8 : SPAN - 8]
+            for k, s in enumerate((0, SPAN - 8)):
+                flux = side_rows[k, pl.ds(w, 1), :]
+                r_buf[w, s : s + 8, :] = r[s : s + 8] - jnp.where(row == 7 * k, flux, 0.0)
         results(q).start()
-        return tuple(carry)
-
-    start = [gk[s : s + ROWS, :] * (load(xe, -1, s) - load(xe, 0, s)) for s in halves]
-    lax.fori_loop(0, ROWS // 4, four, tuple(start))
+        return carry
+
+    lax.fori_loop(0, ROWS // 4, four, 0)
     for q in range(ROWS // 4):
         results(q).wait()
 
@@ -527,20 +570,29 @@
         + (shape((2 * BX, NW), BF16),) * 4,
     )(recv)
     near = line_edges(*edges)
-    x1, fw = call(first_lines, (field, field))(b0, hf, metric, line_inverse)
+    x1, fw, resid = call(first_lines, (field, field, field))(b0, bf, hf, metric, line_inverse)
     ext = pltpu.VMEM((CHUNKS * ROW_COUNT, LANES), F32)
     rounded = pltpu.VMEM((BUSY, NW), BF16)
-    x2, d2, he, *edges = call(
+    x2, d2, *edges = call(
         second_step,
-        (field, field, field) + (shape((BX, NW), BF16),) * 4,
+        (field, field) + (shape((BX, NW), BF16),) * 4,
         (ext, rounded, pltpu.VMEM((4 * BX, NW), BF16)),
-    )(x1, bf, hf, fw, *near, line_inverse, metric)
+    )(resid, x1, hf, *near, line_inverse)
     x_near = line_edges(*edges)
+    resid = call(line_resid, field)(bf, x2, hf, fw, metric)
+    v, m, _ = lax.optimization_barrier((viscosity, wall_metric, d2))
+    smem = pl.BlockSpec(memory_space=pltpu.SMEM)
+    cells = shape((BLOCK_ROWS, LANES), F32)
+    face_weights = call(
+        weights,
+        (cells, shape((ROWS * SPAN, LANES), F32), shape(((ROWS + 1) * SPAN, LANES), F32)),
+        in_specs=(vmem, smem),
+    )(v, m)
+    face_weights, resid = lax.optimization_barrier((face_weights, resid))
     send = call(
         third_step, shape((WY * WZ, 2 * ROWS + TAIL, LANES), BF16), (ext, rounded)
-    )(x2, d2, bf, he, fw, *x_near, line_inverse, metric, ends)
+    )(resid, x2, d2, hf, *x_near, *near, line_inverse, ends)
     recv = lax.all_to_all(send, "wall", 0, 0, tiled=True)
-    cells = shape((BLOCK_ROWS, LANES), F32)
     xf, kappas, *edges = call(
         unpack,
         (cells, shape((2 * SPAN, LANES), F32), shape((4, ROWS, LANES), BF16), dense, dense),
@@ -548,26 +600,15 @@
     )(recv, *v_edges)
     x_edges = block_edges(*edges)
     whole = shape(right_side.shape, F32)
-    smem = pl.BlockSpec(memory_space=pltpu.SMEM)
-    x3, hf, gx, gk = call(
-        stage,
-        (
-            whole,
-            cells,
-            shape((ROWS * SPAN, LANES), F32),
-            shape(((ROWS + 1) * SPAN, LANES), F32),
-        ),
-        (block, dma((ROWS // 4,))),
-        in_specs=(vmem, vmem, vmem, smem),
-        out_specs=(hbm, vmem, vmem, vmem),
-    )(xf, viscosity, kappas, wall_metric)
-    loose = pltpu.VMEM((BLOCK_ROWS, LANES), F32)
+    x3, resid = call(
+        inner_resid, (whole, whole), (block, dma((ROWS // 4,))), out_specs=(hbm, vmem)
+    )(xf, *face_weights, kappas, right_side)
     residual = call(
         last_resid,
         whole,
-        (loose, loose, block, dma((ROWS // 4,))),
+        (pltpu.VMEM((2, ROWS, LANES), F32), block, dma((ROWS // 4,))),
         out_specs=hbm,
-    )(xf, hf, gx, gk, right_side, *x_edges, *edges[1:])
+    )(resid, xf, face_weights[0], *x_edges, *edges[1:])
     return x3, residual
 
 

time: 106 us -> 102 us (0.962)
  waiting for transfers between devices: 6.77 us -> 1.53 us
  starting transfers between devices: 18.7 us -> 21.1 us
  blocking collectives: 60.8 us -> 59.1 us
    ppermute x8, waiting for transfers between devices: 5.46 us -> 0.72 us  [line_shift(): return lax.ppermute(value, ('wall', 'span', 'stream'), pairs)]
    pallas_call x4 -> x6, Pallas kernels: 10.1 us -> 12.1 us  [the longest x1 3.49 us: body(): call(first_lines, (field, field, field))(b0, bf, hf, metric, line_inverse)]
    pallas_call x1, Pallas kernels: 3.24 us -> 1.29 us  [body(): call(third_step, shape((WY * WZ, 2 * ROWS + TAIL, LANES), BF16), (ext, ro...]
    all_to_all x2, blocking collectives: 60.8 us -> 59.1 us  [body(): recv = lax.all_to_all(send, 'wall', 0, 0, tiled=True)]
    ppermute x1, starting transfers between devices: 0.34 us -> 1.56 us  [block_edges(): lax.ppermute(es, 'span', [(0, 1), (1, 0)])]
    ppermute x1, starting transfers between devices: 6.3 us -> 7.38 us  [block_edges(): lax.ppermute(dr, 'stream', right)]
  transfers between devices with their start and end apart: 11 -> 11, of which waited for: 4 -> 3; matrix products, arithmetic and copies ran while one was open for 0% -> 0% of each run, Pallas kernels for 3% -> 9%
where the time goes in v1:
time: 102 us
  blocking collectives  59.1 us (58%)
  starting transfers between devices  21.1 us (21%)
  Pallas kernels  18.9 us (19%)
  waiting for transfers between devices  1.53 us (2%)
    all_to_all x2, blocking collectives, body(): recv = lax.all_to_all(send, 'wall', 0, 0, tiled=True)  59.1 us
    ppermute x8, starting transfers between devices, line_shift(): return lax.ppermute(value, ('wall', 'span', 'stream'), pairs)  12.2 us
    ppermute x1, starting transfers between devices, block_edges(): lax.ppermute(dr, 'stream', right)  7.38 us
    pallas_call x1, Pallas kernels, body(): call(pack, (shape(sent, BF16), shape((2, ROWS, LANES), BF16), dense, dens...  4.03 us
    pallas_call x1, Pallas kernels, body(): call(first_lines, (field, field, field))(b0, bf, hf, metric, line_inverse)  3.49 us
    pallas_call x1, Pallas kernels, body(): call(inner_resid, (whole, whole), (block, dma((ROWS // 4,))), out_specs=(...  2.24 us
  transfers between devices with their start and end apart: 11, of which 3 were waited for; matrix products, arithmetic and copies ran while one was open for 0% of the time, Pallas kernels for 9%

profile of v1, /device:TPU:1, one launch (start us, length us, event | category | flops | bytes accessed | tf_op | source)
XLA Modules:
  0.0 101.7 jit_solution(15019036012679333495)
XLA Ops:
  0.6 4.0 %shard_map.59 = (bf16[32,136,128]{2,1,0:T(8,128)(2,1)}, bf16[2,32,128]{2,1,0:T(8,128)(2,1)}, bf16[32,128]{1,0:T(8,128)(2,1)}, bf16[32,128]{1,0:T(8,128)(2,1)}) custom-call(f32[32,64,128]{2,1,0:T(8,128)} %b_ref.1, f32[32,64,128]{2,1,0:T(8,128)} %v_ref, f32[1,32]{1,0:T(1,128)} %bitcast.1), custom_call_target="tpu_custom_call" | custom-call | flops 10000000 | bytes 4000000 | tf_op jit(solution)/shard_map/pallas_call | solution.py:543
  4.7 42.6 %all_to_all.10.recv = bf16[32,136,128]{2,1,0:T(8,128)(2,1)S(1)} all-to-all(bf16[32,136,128]{2,1,0:T(8,128)(2,1)} %get-tuple-element.40), channel_id=1, replica_groups=mesh['wall'=32,'span'=2,'stream'=4] {'wall'}, dimensions={0} | all-to-all | bytes 2228224 | tf_op jit(solution)/shard_map/all_to_all | solution.py:564
  47.3 0.7 shard_map.60
  48.0 0.4 collective-permute-start
  48.3 2.7 %collective-permute-start.1 = (bf16[32,1024]{1,0:T(8,128)(2,1)S(1)}, bf16[32,1024]{1,0:T(8,128)(2,1)S(1)}, u32[]{:S(2)}, u32[]{:S(2)}) collective-permute-start(bf16[32,1024]{1,0:T(8,128)(2,1)S(1)} %get-tuple-element.48), channel_id=1, source_target_pairs={{0,4},{8,12},{16,20},{24,28},{32,36},{40,44},{48,52},{56,60},{57,6... | collective-permute-start | bytes 196616 | tf_op jit(solution)/shard_map/ppermute | solution.py:523
  51.0 3.9 %collective-permute-start.2 = (bf16[32,1024]{1,0:T(8,128)(2,1)S(1)}, bf16[32,1024]{1,0:T(8,128)(2,1)S(1)}, u32[]{:S(2)}, u32[]{:S(2)}) collective-permute-start(bf16[32,1024]{1,0:T(8,128)(2,1)S(1)} %get-tuple-element.49), channel_id=1, source_target_pairs={{0,8},{8,16},{16,24},{24,32},{32,40},{40,48},{48,56},{56,57},{57,4... | collective-permute-start | bytes 196616 | tf_op jit(solution)/shard_map/ppermute | solution.py:523
  54.9 3.5 %shard_map.61 = (f32[2688,128]{1,0:T(8,128)S(1)}, f32[2688,128]{1,0:T(8,128)S(1)}, f32[2688,128]{1,0:T(8,128)S(1)}) custom-call(bf16[288,1024]{1,0:T(8,128)(2,1)S(1)} %get-tuple-element.41.b0, f32[2688,128]{1,0:T(8,128)S(1)} %get-tuple-element.42.bf, f32[2688,128]{1,0:T(8,128)S(1)} %get-tuple-element.43.hf.he, f32[1,1024]{1,0:T(1,128)S(1)} %get-tuple-element.44.metric, ...), custom_call_target="tpu_custom_call" | custom-call | flops 10000000 | bytes 4000000 | tf_op jit(solution)/shard_map/pallas_call | solution.py:573
  58.4 0.2 collective-permute-done.3.xr.vxr
  58.6 1.6 %shard_map.62 = (f32[2688,128]{1,0:T(8,128)S(1)}, f32[2688,128]{1,0:T(8,128)S(1)}, bf16[16,1024]{1,0:T(8,128)(2,1)S(1)}, bf16[16,1024]{1,0:T(8,128)(2,1)S(1)}, b...) custom-call(f32[2688,128]{1,0:T(8,128)S(1)} %get-tuple-element.45.resid, f32[2688,128]{1,0:T(8,128)S(1)} %get-tuple-element.46.x1, ...), custom_call_target="tpu_custom_call" | custom-call | flops 10000000 | bytes 4000000 | tf_op jit(solution)/shard_map/pallas_call | solution.py:576
  60.2 0.1 collective-permute-start.4
  60.3 3.0 %collective-permute-start.5 = (bf16[16,1024]{1,0:T(8,128)(2,1)S(1)}, bf16[16,1024]{1,0:T(8,128)(2,1)S(1)}, u32[]{:S(2)}, u32[]{:S(2)}) collective-permute-start(bf16[16,1024]{1,0:T(8,128)(2,1)S(1)} %get-tuple-element.61), channel_id=1, source_target_pairs={{0,4},{8,12},{16,20},{24,28},{32,36},{40,44},{48,52},{56,60},{57,6... | collective-permute-start | bytes 98312 | tf_op jit(solution)/shard_map/ppermute | solution.py:523
  63.3 2.2 %collective-permute-start.6 = (bf16[16,1024]{1,0:T(8,128)(2,1)S(1)}, bf16[16,1024]{1,0:T(8,128)(2,1)S(1)}, u32[]{:S(2)}, u32[]{:S(2)}) collective-permute-start(bf16[16,1024]{1,0:T(8,128)(2,1)S(1)} %get-tuple-element.62), channel_id=1, source_target_pairs={{0,8},{8,16},{16,24},{24,32},{32,40},{40,48},{48,56},{56,57},{57,4... | collective-permute-start | bytes 98312 | tf_op jit(solution)/shard_map/ppermute | solution.py:523
  65.4 1.6 %shard_map.64.resid = f32[2688,128]{1,0:T(8,128)S(1)} custom-call(f32[2688,128]{1,0:T(8,128)S(1)} %get-tuple-element.42.bf, f32[2688,128]{1,0:T(8,128)S(1)} %get-tuple-element.57.xe.x2, f32[2688,128]{1,0:T(8,128)S(1)} %get-tuple-element.43.hf.he, f32[2688,128]{1,0:T(8,128)S(1)} %get-tuple-element.58.fw, f32[1,1024]{1,0:T(1,128)S(1)} %get-tuple-element.44.metric), custom_call_target="tpu_custom_call" | custom-call | flops 10000000 | bytes 4000000 | tf_op jit(solution)/shard_map/pallas_call | solution.py:582
  67.1 1.4 %shard_map.63 = (f32[2280,128]{1,0:T(8,128)S(1)}, f32[2048,128]{1,0:T(8,128)S(1)}, f32[2112,128]{1,0:T(8,128)S(1)}) custom-call(f32[32,64,128]{2,1,0:T(8,128)S(1)} %copy-done.1, f32[32]{0:T(128)S(1)} %copy-done.6), custom_call_target="tpu_custom_call" | custom-call | flops 10000000 | bytes 4000000 | tf_op jit(solution)/shard_map/pallas_call | solution.py:586
  68.5 0.5 collective-permute-done.7.xr
  69.1 1.3 %shard_map.65 = bf16[32,72,128]{2,1,0:T(8,128)(2,1)S(1)} custom-call(f32[2688,128]{1,0:T(8,128)S(1)} %shard_map.64.resid, f32[2688,128]{1,0:T(8,128)S(1)} %get-tuple-element.57.xe.x2, f32[2688,128]{1,0:T(8,128)S(1)} %get-tuple-element.51.d2, f32[2688,128]{1,0:T(8,128)S(1)} %get-tuple-element.43.hf.he, bf16[16,1024]{1,0:T(8,128)(2,1)S(1)} %collective-permute-done.4.su, ...), custom_call_target="tpu_custom_call" | custom-call | flops 10000000 | bytes 4000000 | tf_op jit(solution)/shard_map/pallas_call | solution.py:592
  70.4 0.0 copy-start.2
  70.4 16.5 %all_to_all.11.recv = bf16[32,72,128]{2,1,0:T(8,128)(2,1)S(1)} all-to-all(bf16[32,72,128]{2,1,0:T(8,128)(2,1)S(1)} %shard_map.65), channel_id=1, replica_groups=mesh['wall'=32,'span'=2,'stream'=4] {'wall'}, dimensions={0} | all-to-all | bytes 1179648 | tf_op jit(solution)/shard_map/all_to_all | solution.py:595
  86.9 0.8 shard_map.66
  87.8 1.6 %collective-permute-start.8 = (bf16[4,32,128]{2,1,0:T(8,128)(2,1)S(1)}, bf16[4,32,128]{2,1,0:T(8,128)(2,1)S(1)}, u32[]{:S(2)}, u32[]{:S(2)}) collective-permute-start(bf16[4,32,128]{2,1,0:T(8,128)(2,1)S(1)} %get-tuple-element.75), channel_id=1, source_target_pairs={{0,4},{4,0},{1,5},{5,1},{2,6},{6,2},{3,7},{7,3},{8,12},{12,8},{9,1... | collective-permute-start | bytes 98312 | tf_op jit(solution)/shard_map/ppermute | solution.py:503
  89.3 7.4 %collective-permute-start.9 = (bf16[32,128]{1,0:T(8,128)(2,1)S(1)}, bf16[32,128]{1,0:T(8,128)(2,1)S(1)}, u32[]{:S(2)}, u32[]{:S(2)}) collective-permute-start(bf16[32,128]{1,0:T(8,128)(2,1)S(1)} %get-tuple-element.76.dr), channel_id=1, source_target_pairs={{0,1},{1,2},{2,3},{3,0},{4,5},{5,6},{6,7},{7,4},{8,9},{9,10},{10,1... | collective-permute-start | bytes 24584 | tf_op jit(solution)/shard_map/ppermute | solution.py:504
  96.7 2.2 %shard_map.67 = (f32[32,64,128]{2,1,0:T(8,128)}, f32[32,64,128]{2,1,0:T(8,128)S(1)}) custom-call(f32[2280,128]{1,0:T(8,128)S(1)} %get-tuple-element.68.xf, f32[2280,128]{1,0:T(8,128)S(1)} %get-tuple-element.69.hf, f32[2048,128]{1,0:T(8,128)S(1)} %get-tuple-element.70.gx, f32[2112,128]{1,0:T(8,128)S(1)} %get-tuple-element.71.gk, ...), custom_call_target="tpu_custom_call" | custom-call | flops 10000000 | bytes 4000000 | tf_op jit(solution)/shard_map/pallas_call | solution.py:603
  99.0 0.8 collective-permute-done.10.rights
  99.8 1.7 %shard_map.68 = f32[32,64,128]{2,1,0:T(8,128)} custom-call(f32[32,64,128]{2,1,0:T(8,128)S(1)} %get-tuple-element.74.resid, f32[2280,128]{1,0:T(8,128)S(1)} %get-tuple-element.68.xf, f32[2280,128]{1,0:T(8,128)S(1)} %get-tuple-element.69.hf, bf16[4,32,128]{2,1,0:T(8,128)(2,1)S(1)} %collective-permute-done.8.spans, ...), custom_call_target="tpu_custom_call" | custom-call | flops 10000000 | bytes 4000000 | tf_op jit(solution)/shard_map/pallas_call | solution.py:606
  (24 shorter events, 0.1 us)
Async XLA Ops:
  4.7 50.2 %copy-start = (bf16[1024,1024]{1,0:T(8,128)(2,1)S(1)}, bf16[1024,1024]{1,0:T(8,128)(2,1)}, u32[]{:S(2)}) copy-start(bf16[1024,1024]{1,0:T(8,128)(2,1)} %line.5) | copy-start | bytes 6291460
  48.0 10.5 %collective-permute-start = (bf16[32,1024]{1,0:T(8,128)(2,1)S(1)}, bf16[32,1024]{1,0:T(8,128)(2,1)S(1)}, u32[]{:S(2)}, u32[]{:S(2)}) collective-permute-start(bf16[32,1024]{1,0:T(8,128)(2,1)S(1)} %get-tuple-element.47), channel_id=1, source_target_pairs={{0,64},{8,72},{16,80},{24,88},{32,96},{40,104},{48,112},{56,120},{... | collective-permute-start | bytes 196616 | tf_op jit(solution)/shard_map/ppermute | solution.py:523
  48.3 10.1 %collective-permute-start.1 = (bf16[32,1024]{1,0:T(8,128)(2,1)S(1)}, bf16[32,1024]{1,0:T(8,128)(2,1)S(1)}, u32[]{:S(2)}, u32[]{:S(2)}) collective-permute-start(bf16[32,1024]{1,0:T(8,128)(2,1)S(1)} %get-tuple-element.48), channel_id=1, source_target_pairs={{0,4},{8,12},{16,20},{24,28},{32,36},{40,44},{48,52},{56,60},{57,6... | collective-permute-start | bytes 196616 | tf_op jit(solution)/shard_map/ppermute | solution.py:523
  51.0 7.4 %collective-permute-start.2 = (bf16[32,1024]{1,0:T(8,128)(2,1)S(1)}, bf16[32,1024]{1,0:T(8,128)(2,1)S(1)}, u32[]{:S(2)}, u32[]{:S(2)}) collective-permute-start(bf16[32,1024]{1,0:T(8,128)(2,1)S(1)} %get-tuple-element.49), channel_id=1, source_target_pairs={{0,8},{8,16},{16,24},{24,32},{32,40},{40,48},{48,56},{56,57},{57,4... | collective-permute-start | bytes 196616 | tf_op jit(solution)/shard_map/ppermute | solution.py:523
  54.9 3.7 %collective-permute-start.3 = (bf16[32,1024]{1,0:T(8,128)(2,1)S(1)}, bf16[32,1024]{1,0:T(8,128)(2,1)S(1)}, u32[]{:S(2)}, u32[]{:S(2)}) collective-permute-start(bf16[32,1024]{1,0:T(8,128)(2,1)S(1)} %get-tuple-element.50), channel_id=1, source_target_pairs={{0,3},{8,0},{16,8},{24,16},{32,24},{40,32},{48,40},{56,48},{57,56}... | collective-permute-start | bytes 196616 | tf_op jit(solution)/shard_map/ppermute | solution.py:523
  60.2 8.3 %collective-permute-start.4 = (bf16[16,1024]{1,0:T(8,128)(2,1)S(1)}, bf16[16,1024]{1,0:T(8,128)(2,1)S(1)}, u32[]{:S(2)}, u32[]{:S(2)}) collective-permute-start(bf16[16,1024]{1,0:T(8,128)(2,1)S(1)} %get-tuple-element.60), channel_id=1, source_target_pairs={{0,64},{8,72},{16,80},{24,88},{32,96},{40,104},{48,112},{56,120},{... | collective-permute-start | bytes 98312 | tf_op jit(solution)/shard_map/ppermute | solution.py:523
  60.3 8.2 %collective-permute-start.5 = (bf16[16,1024]{1,0:T(8,128)(2,1)S(1)}, bf16[16,1024]{1,0:T(8,128)(2,1)S(1)}, u32[]{:S(2)}, u32[]{:S(2)}) collective-permute-start(bf16[16,1024]{1,0:T(8,128)(2,1)S(1)} %get-tuple-element.61), channel_id=1, source_target_pairs={{0,4},{8,12},{16,20},{24,28},{32,36},{40,44},{48,52},{56,60},{57,6... | collective-permute-start | bytes 98312 | tf_op jit(solution)/shard_map/ppermute | solution.py:523
  63.3 5.2 %collective-permute-start.6 = (bf16[16,1024]{1,0:T(8,128)(2,1)S(1)}, bf16[16,1024]{1,0:T(8,128)(2,1)S(1)}, u32[]{:S(2)}, u32[]{:S(2)}) collective-permute-start(bf16[16,1024]{1,0:T(8,128)(2,1)S(1)} %get-tuple-element.62), channel_id=1, source_target_pairs={{0,8},{8,16},{16,24},{24,32},{32,40},{40,48},{48,56},{56,57},{57,4... | collective-permute-start | bytes 98312 | tf_op jit(solution)/shard_map/ppermute | solution.py:523
  65.4 3.6 %collective-permute-start.7 = (bf16[16,1024]{1,0:T(8,128)(2,1)S(1)}, bf16[16,1024]{1,0:T(8,128)(2,1)S(1)}, u32[]{:S(2)}, u32[]{:S(2)}) collective-permute-start(bf16[16,1024]{1,0:T(8,128)(2,1)S(1)} %get-tuple-element.63), channel_id=1, source_target_pairs={{0,3},{8,0},{16,8},{24,16},{32,24},{40,32},{48,40},{56,48},{57,56}... | collective-permute-start | bytes 98312 | tf_op jit(solution)/shard_map/ppermute | solution.py:523
  65.4 1.7 %copy-start.1 = (f32[32,64,128]{2,1,0:T(8,128)S(1)}, f32[32,64,128]{2,1,0:T(8,128)}, u32[]{:S(2)}) copy-start(f32[32,64,128]{2,1,0:T(8,128)} %v_ref) | copy-start | bytes 3145732
  65.4 1.7 %copy-start.6 = (f32[32]{0:T(128)S(1)}, f32[32]{0:T(128)}, u32[]{:S(2)}) copy-start(f32[32]{0:T(128)} %m_ref) | copy-start | bytes 388
  69.0 17.9 %copy-start.3 = (bf16[2,32,128]{2,1,0:T(8,128)(2,1)S(1)}, bf16[2,32,128]{2,1,0:T(8,128)(2,1)}, u32[]{:S(2)}) copy-start(bf16[2,32,128]{2,1,0:T(8,128)(2,1)} %get-tuple-element.65.ves) | copy-start | bytes 49156
  69.1 17.9 %copy-start.4 = (bf16[32,128]{1,0:T(8,128)(2,1)S(1)}, bf16[32,128]{1,0:T(8,128)(2,1)}, u32[]{:S(2)}) copy-start(bf16[32,128]{1,0:T(8,128)(2,1)} %get-tuple-element.66.vdl) | copy-start | bytes 24580
  69.1 17.9 %copy-start.5 = (bf16[32,128]{1,0:T(8,128)(2,1)S(1)}, bf16[32,128]{1,0:T(8,128)(2,1)}, u32[]{:S(2)}) copy-start(bf16[32,128]{1,0:T(8,128)(2,1)} %get-tuple-element.67.vdr) | copy-start | bytes 24580
  70.4 26.4 %copy-start.2 = (f32[32,64,128]{2,1,0:T(8,128)S(1)}, f32[32,64,128]{2,1,0:T(8,128)}, u32[]{:S(2)}) copy-start(f32[32,64,128]{2,1,0:T(8,128)} %b_ref.1) | copy-start | bytes 3145732
  87.8 12.0 %collective-permute-start.8 = (bf16[4,32,128]{2,1,0:T(8,128)(2,1)S(1)}, bf16[4,32,128]{2,1,0:T(8,128)(2,1)S(1)}, u32[]{:S(2)}, u32[]{:S(2)}) collective-permute-start(bf16[4,32,128]{2,1,0:T(8,128)(2,1)S(1)} %get-tuple-element.75), channel_id=1, source_target_pairs={{0,4},{4,0},{1,5},{5,1},{2,6},{6,2},{3,7},{7,3},{8,12},{12,8},{9,1... | collective-permute-start | bytes 98312 | tf_op jit(solution)/shard_map/ppermute | solution.py:503
  89.3 9.6 %collective-permute-start.9 = (bf16[32,128]{1,0:T(8,128)(2,1)S(1)}, bf16[32,128]{1,0:T(8,128)(2,1)S(1)}, u32[]{:S(2)}, u32[]{:S(2)}) collective-permute-start(bf16[32,128]{1,0:T(8,128)(2,1)S(1)} %get-tuple-element.76.dr), channel_id=1, source_target_pairs={{0,1},{1,2},{2,3},{3,0},{4,5},{5,6},{6,7},{7,4},{8,9},{9,10},{10,1... | collective-permute-start | bytes 24584 | tf_op jit(solution)/shard_map/ppermute | solution.py:504
  96.7 3.1 %collective-permute-start.10 = (bf16[32,128]{1,0:T(8,128)(2,1)S(1)}, bf16[32,128]{1,0:T(8,128)(2,1)S(1)}, u32[]{:S(2)}, u32[]{:S(2)}) collective-permute-start(bf16[32,128]{1,0:T(8,128)(2,1)S(1)} %get-tuple-element.77.dl), channel_id=1, source_target_pairs={{1,0},{2,1},{3,2},{0,3},{5,4},{6,5},{7,6},{4,7},{9,8},{10,9},{11,1... | collective-permute-start | bytes 24584 | tf_op jit(solution)/shard_map/ppermute | solution.py:505

commit v2 on v1

--- a/solution.py
+++ b/solution.py
@@ -85,7 +85,7 @@
 
 
 def strided(s):
-    return pl.ds(s, ROWS, stride=SPAN + 1)
+    return pl.ds(s, ROWS, stride=SPAN)
 
 
 def edge_lanes(blocks, pick, turn, offset):
@@ -103,23 +103,51 @@
     b_hbm, v_hbm, m_hbm, send_hbm, es_hbm, dl_hbm, dr_hbm, b_buf, v_buf, m_buf, send, es, dl, dr, cl, cr,
     sems, done, small,
 ):
-    def copy(k, w):
+    def copy(k, t):
         src, dst = ((v_hbm, v_buf), (b_hbm, b_buf))[k]
-        return pltpu.make_async_copy(src.at[w], dst.at[pl.ds((SPAN + 1) * w, SPAN)], sems.at[k, w])
+        rows = pl.ds(BS * t, BS)
+        return pltpu.make_async_copy(src.at[:, rows, :], dst.at[:, rows, :], sems.at[k, t])
 
     def result(y):
         peers = pl.ds(WZ * y, WZ)
         return pltpu.make_async_copy(send.at[peers], send_hbm.at[peers], done.at[y])
 
     for k in range(2):
-        for w in range(ROWS):
-            copy(k, w).start()
+        for t in range(WY):
+            copy(k, t).start()
     metric = pltpu.make_async_copy(m_hbm, m_buf, small.at[3])
     metric.start()
     edges = [
         pltpu.make_async_copy(src, dst, small.at[n])
         for n, (src, dst) in enumerate(((es, es_hbm), (dl, dl_hbm), (dr, dr_hbm)))
     ]
+
+    def move(t, k, buf, mid):
+        for g in range(2):
+            parts = [buf[strided(16 * t + 8 * g + i), :] - mid for i in range(8)]
+            parts = to_blocks([part.astype(BF16) for part in parts])
+            rows = slice(ROWS * (2 * k + g), ROWS * (2 * k + g + 1))
+            for z in range(WZ):
+                send[owner(t, z), rows, :] = parts[z]
+            if k:
+                cl[2 * t + g] = parts[0]
+                cr[2 * t + g] = parts[7]
+        return 0
+
+    v_flat, b_flat = (buf.reshape(ROWS * SPAN, LANES) for buf in (v_buf, b_buf))
+
+    def first(t, _):
+        copy(0, t).wait()
+        move(t, 1, v_flat, MID)
+        return 0
+
+    lax.fori_loop(0, WY, first, 0)
+    es[0] = (v_flat[strided(0), :] - MID).astype(BF16)
+    es[1] = (v_flat[strided(SPAN - 1), :] - MID).astype(BF16)
+    dl[...] = edge_lanes(cl[...], 0, 0, SPAN)
+    dr[...] = edge_lanes(cr[...], BX - 1, 1, SPAN)
+    for edge in edges:
+        edge.start()
     metric.wait()
     rest = m_buf[...]
     parts = []
@@ -132,32 +160,9 @@
     for k in range(WY * WZ):
         send[k, 4 * ROWS :, :] = tail
 
-    def move(t, k, buf, mid):
-        for g in range(2):
-            parts = [buf[strided(16 * t + 8 * g + i), :] - mid for i in range(8)]
-            parts = to_blocks([part.astype(BF16) for part in parts])
-            rows = slice(ROWS * (2 * k + g), ROWS * (2 * k + g + 1))
-            for z in range(WZ):
-                send[owner(t, z), rows, :] = parts[z]
-            if k:
-                cl[2 * t + g] = parts[0]
-                cr[2 * t + g] = parts[7]
-        return 0
-
-    for w in range(ROWS):
-        copy(0, w).wait()
-    lax.fori_loop(0, WY, lambda t, _: move(t, 1, v_buf, MID), 0)
-    es[0] = (v_buf[strided(0), :] - MID).astype(BF16)
-    es[1] = (v_buf[strided(SPAN - 1), :] - MID).astype(BF16)
-    dl[...] = edge_lanes(cl[...], 0, 0, SPAN)
-    dr[...] = edge_lanes(cr[...], BX - 1, 1, SPAN)
-    for edge in edges:
-        edge.start()
-    for w in range(ROWS):
-        copy(1, w).wait()
-
     def last(t, _):
-        move(t, 0, b_buf, 0.0)
+        copy(1, t).wait()
+        move(t, 0, b_flat, 0.0)
         result(owner(t, 0) // WZ).start()
         return 0
 
@@ -248,23 +253,10 @@
     for i in range(CHUNKS):
         x1[busy(i), :] = y[:, i * LANES : (i + 1) * LANES]
     mirror(x1)
-    last = lax.broadcasted_iota(jnp.int32, (RUN, LANES), 1) == LANES - 1
-
-    def one(c, _):
-        after = jnp.zeros((RUN, LANES), F32)
-        for i in reversed(range(CHUNKS)):
-            rows = pl.ds(ROW_COUNT * i + FIRST + RUN * c, RUN)
-            half = hf[rows, :] * metric[:, i * LANES : (i + 1) * LANES]
-            moved = pltpu.roll(half, LANES - 1, 1)
-            fw[rows, :] = half + jnp.where(last, after, moved)
-            after = moved
-        return 0
-
-    lax.fori_loop(0, BUSY // RUN, one, 0)
-    line_resid(bf, x1, hf, fw, metric, resid)
-
-
-def line_resid(bf, xe, he, fw, metric, out):
+    line_resid(bf, x1, hf, fw, metric, resid, make_weights=True)
+
+
+def line_resid(bf, xe, he, fw, metric, out, make_weights=False):
     lane = lax.broadcasted_iota(jnp.int32, (RUN, LANES), 1)
     last, first = lane == LANES - 1, lane == 0
 
@@ -274,14 +266,24 @@
 
         xc = load(xe, 0)
         moved_x = pltpu.roll(xc, LANES - 1, 1)
-        entry = load(he, 0) * metric[:, :LANES] * -xc
+        kappa = load(he, 0) * metric[:, :LANES]
+        entry = kappa * -xc
+        moved_k = pltpu.roll(kappa, LANES - 1, 1)
         for i in range(CHUNKS):
             if i + 1 < CHUNKS:
                 after = load(xe, i + 1)
                 moved_after = pltpu.roll(after, LANES - 1, 1)
+                kappa_after = load(he, i + 1) * metric[:, (i + 1) * LANES : (i + 2) * LANES]
+                moved_k_after = pltpu.roll(kappa_after, LANES - 1, 1)
             else:
                 after = moved_after = jnp.zeros((RUN, LANES), F32)
-            above = load(fw, i) * (xc - jnp.where(last, moved_after, moved_x))
+                kappa_after = moved_k_after = after
+            if make_weights:
+                weight = kappa + jnp.where(last, moved_k_after, moved_k)
+                fw[pl.ds(ROW_COUNT * i + FIRST + RUN * c, RUN), :] = weight
+            else:
+                weight = load(fw, i)
+            above = weight * (xc - jnp.where(last, moved_after, moved_x))
             below = pltpu.roll(above, 1, 1)
             hc = load(he, i)
             total = above - jnp.where(first, entry, below)
@@ -289,6 +291,7 @@
                 total += (hc + load(he, i, shift)) * (xc - load(xe, i, shift))
             out[pl.ds(ROW_COUNT * i + FIRST + RUN * c, RUN), :] = load(bf, i) - (xc + total)
             xc, moved_x, entry = after, moved_after, below
+            kappa, moved_k = kappa_after, moved_k_after
         return 0
 
     lax.fori_loop(0, BUSY // RUN, one, 0)
@@ -366,7 +369,7 @@
     return pl.ds(block_row(0, s), ROWS, stride=CP)
 
 
-def unpack(recv, ves, vdl, vdr, xf, kappas, es, dl, dr, cl, cr):
+def unpack(recv, ves, vdl, vdr, xf, es, dl, dr, cl, cr):
     def one(t, _):
         for g in range(2):
             rows = slice(ROWS * g, ROWS * (g + 1))
@@ -377,14 +380,6 @@
             for i in range(8):
                 s = 16 * t + 8 * g + i
                 xf[pl.ds(block_row(0) + s, ROWS, stride=CP), :] = parts[i].astype(F32)
-        parts = from_blocks([recv[owner(t, z), 2 * ROWS :, :].astype(F32) for z in range(WZ)])
-        for g in range(2):
-            for i in range(8):
-                s = 16 * t + 8 * g + i
-                for k, (ref, row) in enumerate(
-                    ((xf, block_row(-1)), (xf, block_row(ROWS)), (kappas, 0), (kappas, SPAN))
-                ):
-                    ref[pl.ds(row + s, 1), :] = parts[i][4 * g + k : 4 * g + k + 1]
         return 0
 
     lax.fori_loop(0, WY, one, 0)
@@ -392,6 +387,8 @@
         edge = xf[block_span(s), :]
         xf[block_span(beside), :] = edge
         es[k] = edge.astype(BF16)
+    for w, beside in ((0, -1), (ROWS - 1, ROWS)):
+        xf[pl.ds(block_row(beside), SPAN), :] = xf[pl.ds(block_row(w), SPAN), :]
     es[2] = ves[0]
     es[3] = ves[1]
     dl[...] = edge_lanes(cl[...], 0, 0, 0) + vdl[...]
@@ -416,7 +413,15 @@
         hf[block_span(s), :] = jnp.zeros((ROWS, LANES), F32)
 
 
-def inner_resid(xf, hf, gx, gk, kappas, b_ref, x3, resid, x_buf, sems):
+def placed(right, left):
+    at = lax.broadcasted_iota(jnp.int32, (2 * ROWS, LANES), 0)
+    to = lax.broadcasted_iota(jnp.int32, (2 * ROWS, LANES), 1)
+    place = jnp.where(to == 2 * (at % ROWS) + at // ROWS, 1.0, 0.0).astype(BF16)
+    both = jnp.concatenate([right[...], left[...]], axis=0)
+    return lax.dot_general(both, place, (((0,), (0,)), ((), ())), preferred_element_type=F32)
+
+
+def inner_resid(xf, hf, gx, gk, recv, b_ref, dl, dr, x3, resid, own, x_buf, beyond, sems):
     lane = lax.broadcasted_iota(jnp.int32, (ROWS, LANES), 1)
     halves = (0, ROWS)
 
@@ -431,12 +436,10 @@
         carry = list(carry)
         for n in range(4):
             w = 4 * q + n
-            top = jnp.where(w == ROWS - 1, 0.5, 0.0)
             for h, s in enumerate(halves):
                 xc, hc = load(xf, w, s), load(hf, w, s)
                 x_buf[w, s : s + ROWS, :] = xc
-                weight = gk[pl.ds(SPAN * (w + 1) + s, ROWS), :] + top * kappas[SPAN + s : SPAN + s + ROWS, :]
-                above = weight * (xc - load(xf, w + 1, s))
+                above = gk[pl.ds(SPAN * (w + 1) + s, ROWS), :] * (xc - load(xf, w + 1, s))
                 total = above - carry[h]
                 carry[h] = above
                 for d in (-1, 1):
@@ -448,28 +451,34 @@
         result(q).start()
         return tuple(carry)
 
-    start = []
-    for s in halves:
-        weight = gk[s : s + ROWS, :] + 0.5 * kappas[s : s + ROWS, :]
-        start.append(weight * (load(xf, -1, s) - load(xf, 0, s)))
-    lax.fori_loop(0, ROWS // 4, four, tuple(start))
+    zero = jnp.zeros((ROWS, LANES), F32)
+    lax.fori_loop(0, ROWS // 4, four, (zero, zero))
+
+    def tail(t, _):
+        parts = from_blocks([recv[owner(t, z), 2 * ROWS :, :].astype(F32) for z in range(WZ)])
+        for g in range(2):
+            for i in range(8):
+                for k in range(4):
+                    row = pl.ds(SPAN * k + 16 * t + 8 * g + i, 1)
+                    beyond[row, :] = parts[i][4 * g + k : 4 * g + k + 1]
+        return 0
+
+    lax.fori_loop(0, WY, tail, 0)
+    for k, w in enumerate((0, ROWS - 1)):
+        face = gk[SPAN * ROWS * k : SPAN * (ROWS * k + 1), :]
+        weight = face + 0.5 * beyond[SPAN * (2 + k) : SPAN * (3 + k), :]
+        x = xf[pl.ds(block_row(w), SPAN), :]
+        resid[w] = resid[w] - weight * (x - beyond[SPAN * k : SPAN * (k + 1), :])
+    own[...] = placed(dr, dl)
     for q in range(ROWS // 4):
         result(q).wait()
 
 
-def last_resid(resid, xf, hf, spans, lefts, rights, dl, dr, out, side_rows, r_buf, sems):
+def last_resid(resid, xf, hf, own, spans, lefts, rights, out, side_rows, r_buf, sems):
     for k, s in enumerate((0, SPAN - 1)):
         weight = hf[block_span(s), :] + 0.5 * spans[3 - k].astype(F32) + 0.5 * MID
         side_rows[k] = weight * (xf[block_span(s), :] - spans[1 - k].astype(F32))
-    at = lax.broadcasted_iota(jnp.int32, (2 * ROWS, LANES), 0)
-    to = lax.broadcasted_iota(jnp.int32, (2 * ROWS, LANES), 1)
-    place = jnp.where(to == 2 * (at % ROWS) + at // ROWS, 1.0, 0.0).astype(BF16)
-
-    def placed(right, left):
-        both = jnp.concatenate([right[...], left[...]], axis=0)
-        return lax.dot_general(both, place, (((0,), (0,)), ((), ())), preferred_element_type=F32)
-
-    own, near = placed(dr, dl), placed(rights, lefts)
+    near = placed(rights, lefts)
     sides = (0.5 * (own[SPAN:] + near[SPAN:]) + MID) * (own[:SPAN] - near[:SPAN])
     lane = lax.broadcasted_iota(jnp.int32, (SPAN, LANES), 1)
     ends = (lane == 0) | (lane == LANES - 1)
@@ -538,14 +547,13 @@
     dense = shape((ROWS, LANES), BF16)
     hbm, vmem = pl.BlockSpec(memory_space=pltpu.HBM), pl.BlockSpec(memory_space=pltpu.VMEM)
     sent = (WY * WZ, 4 * ROWS + TAIL, LANES)
-    loose = pltpu.VMEM(((SPAN + 1) * ROWS, LANES), F32)
     dma = pltpu.SemaphoreType.DMA
     send, *v_edges = call(
         pack,
         (shape(sent, BF16), shape((2, ROWS, LANES), BF16), dense, dense),
         (
-            loose,
-            loose,
+            block,
+            block,
             pltpu.VMEM((1, ROWS), F32),
             pltpu.VMEM(sent, BF16),
             pltpu.VMEM((2, ROWS, LANES), BF16),
@@ -553,7 +561,7 @@
             pltpu.VMEM((ROWS, LANES), BF16),
             side,
             side,
-            dma((2, ROWS)),
+            dma((2, WY)),
             dma((WY,)),
             dma((4,)),
         ),
@@ -593,22 +601,25 @@
         third_step, shape((WY * WZ, 2 * ROWS + TAIL, LANES), BF16), (ext, rounded)
     )(resid, x2, d2, hf, *x_near, *near, line_inverse, ends)
     recv = lax.all_to_all(send, "wall", 0, 0, tiled=True)
-    xf, kappas, *edges = call(
+    xf, *edges = call(
         unpack,
-        (cells, shape((2 * SPAN, LANES), F32), shape((4, ROWS, LANES), BF16), dense, dense),
+        (cells, shape((4, ROWS, LANES), BF16), dense, dense),
         (side, side),
     )(recv, *v_edges)
     x_edges = block_edges(*edges)
     whole = shape(right_side.shape, F32)
-    x3, resid = call(
-        inner_resid, (whole, whole), (block, dma((ROWS // 4,))), out_specs=(hbm, vmem)
-    )(xf, *face_weights, kappas, right_side)
+    x3, resid, own = call(
+        inner_resid,
+        (whole, whole, shape((LANES, LANES), F32)),
+        (block, pltpu.VMEM((4 * SPAN, LANES), F32), dma((ROWS // 4,))),
+        out_specs=(hbm, vmem, vmem),
+    )(xf, *face_weights, recv, right_side, *edges[1:])
     residual = call(
         last_resid,
         whole,
         (pltpu.VMEM((2, ROWS, LANES), F32), block, dma((ROWS // 4,))),
         out_specs=hbm,
-    )(resid, xf, face_weights[0], *x_edges, *edges[1:])
+    )(resid, xf, face_weights[0], own, *x_edges)
     return x3, residual
 
 

time: 102 us -> 101 us (level)
    ppermute x1, starting transfers between devices: 7.38 us -> 0.19 us  [block_edges(): lax.ppermute(dr, 'stream', right)]
    ppermute x1, starting transfers between devices: 0.01 us -> 7.19 us  [block_edges(): lax.ppermute(dl, 'stream', left)]
  transfers between devices with their start and end apart: 11 -> 11, of which waited for: 3 -> 2; matrix products, arithmetic and copies ran while one was open for 0% -> 0% of each run, Pallas kernels for 9% -> 9%
where the time goes in v2:
time: 101 us
  blocking collectives  59.1 us (59%)
  starting transfers between devices  21 us (21%)
  Pallas kernels  18.6 us (18%)
    all_to_all x2, blocking collectives, body(): recv = lax.all_to_all(send, 'wall', 0, 0, tiled=True)  59.1 us
    ppermute x8, starting transfers between devices, line_shift(): return lax.ppermute(value, ('wall', 'span', 'stream'), pairs)  12.1 us
    ppermute x1, starting transfers between devices, block_edges(): lax.ppermute(dl, 'stream', left)  7.19 us
    pallas_call x1, Pallas kernels, body(): call(pack, (shape(sent, BF16), shape((2, ROWS, LANES), BF16), dense, dens...  3.83 us
    pallas_call x1, Pallas kernels, body(): call(first_lines, (field, field, field))(b0, bf, hf, metric, line_inverse)  3.29 us
    pallas_call x1, Pallas kernels, body(): call(inner_resid, (whole, whole, shape((LANES, LANES), F32)), (block, plt...  2.38 us
  transfers between devices with their start and end apart: 11, of which 2 were waited for; matrix products, arithmetic and copies ran while one was open for 0% of the time, Pallas kernels for 9%

profile of v2, /device:TPU:1, one launch (start us, length us, event | category | flops | bytes accessed | tf_op | source)
XLA Modules:
  0.0 100.5 jit_solution(13510987657800608644)
XLA Ops:
  0.6 3.8 %shard_map.59 = (bf16[32,136,128]{2,1,0:T(8,128)(2,1)}, bf16[2,32,128]{2,1,0:T(8,128)(2,1)}, bf16[32,128]{1,0:T(8,128)(2,1)}, bf16[32,128]{1,0:T(8,128)(2,1)}) custom-call(f32[32,64,128]{2,1,0:T(8,128)} %b_ref.1, f32[32,64,128]{2,1,0:T(8,128)} %v_ref, f32[1,32]{1,0:T(1,128)} %bitcast.1), custom_call_target="tpu_custom_call" | custom-call | flops 10000000 | bytes 4000000 | tf_op jit(solution)/shard_map/pallas_call | solution.py:551
  4.5 0.0 copy-start
  4.5 42.6 %all_to_all.10.recv = bf16[32,136,128]{2,1,0:T(8,128)(2,1)S(1)} all-to-all(bf16[32,136,128]{2,1,0:T(8,128)(2,1)} %get-tuple-element.40), channel_id=1, replica_groups=mesh['wall'=32,'span'=2,'stream'=4] {'wall'}, dimensions={0} | all-to-all | bytes 2228224 | tf_op jit(solution)/shard_map/all_to_all | solution.py:572
  47.1 0.7 shard_map.60
  47.7 0.4 collective-permute-start
  48.1 2.7 %collective-permute-start.1 = (bf16[32,1024]{1,0:T(8,128)(2,1)S(1)}, bf16[32,1024]{1,0:T(8,128)(2,1)S(1)}, u32[]{:S(2)}, u32[]{:S(2)}) collective-permute-start(bf16[32,1024]{1,0:T(8,128)(2,1)S(1)} %get-tuple-element.48), channel_id=1, source_target_pairs={{0,4},{8,12},{16,20},{24,28},{32,36},{40,44},{48,52},{56,60},{57,6... | collective-permute-start | bytes 196616 | tf_op jit(solution)/shard_map/ppermute | solution.py:532
  50.8 3.9 %collective-permute-start.2 = (bf16[32,1024]{1,0:T(8,128)(2,1)S(1)}, bf16[32,1024]{1,0:T(8,128)(2,1)S(1)}, u32[]{:S(2)}, u32[]{:S(2)}) collective-permute-start(bf16[32,1024]{1,0:T(8,128)(2,1)S(1)} %get-tuple-element.49), channel_id=1, source_target_pairs={{0,8},{8,16},{16,24},{24,32},{32,40},{40,48},{48,56},{56,57},{57,4... | collective-permute-start | bytes 196616 | tf_op jit(solution)/shard_map/ppermute | solution.py:532
  54.7 3.3 %shard_map.61 = (f32[2688,128]{1,0:T(8,128)S(1)}, f32[2688,128]{1,0:T(8,128)S(1)}, f32[2688,128]{1,0:T(8,128)S(1)}) custom-call(bf16[288,1024]{1,0:T(8,128)(2,1)S(1)} %get-tuple-element.41.b0, f32[2688,128]{1,0:T(8,128)S(1)} %get-tuple-element.42.bf, f32[2688,128]{1,0:T(8,128)S(1)} %get-tuple-element.43.hf.he, f32[1,1024]{1,0:T(1,128)S(1)} %get-tuple-element.44.metric, ...), custom_call_target="tpu_custom_call" | custom-call | flops 10000000 | bytes 4000000 | tf_op jit(solution)/shard_map/pallas_call | solution.py:581
  58.0 0.4 collective-permute-done.3.xr.vxr
  58.4 1.6 %shard_map.62 = (f32[2688,128]{1,0:T(8,128)S(1)}, f32[2688,128]{1,0:T(8,128)S(1)}, bf16[16,1024]{1,0:T(8,128)(2,1)S(1)}, bf16[16,1024]{1,0:T(8,128)(2,1)S(1)}, b...) custom-call(f32[2688,128]{1,0:T(8,128)S(1)} %get-tuple-element.45.resid, f32[2688,128]{1,0:T(8,128)S(1)} %get-tuple-element.46.x1, ...), custom_call_target="tpu_custom_call" | custom-call | flops 10000000 | bytes 4000000 | tf_op jit(solution)/shard_map/pallas_call | solution.py:584
  60.0 0.1 collective-permute-start.4
  60.1 3.0 %collective-permute-start.5 = (bf16[16,1024]{1,0:T(8,128)(2,1)S(1)}, bf16[16,1024]{1,0:T(8,128)(2,1)S(1)}, u32[]{:S(2)}, u32[]{:S(2)}) collective-permute-start(bf16[16,1024]{1,0:T(8,128)(2,1)S(1)} %get-tuple-element.61), channel_id=1, source_target_pairs={{0,4},{8,12},{16,20},{24,28},{32,36},{40,44},{48,52},{56,60},{57,6... | collective-permute-start | bytes 98312 | tf_op jit(solution)/shard_map/ppermute | solution.py:532
  63.1 2.0 %collective-permute-start.6 = (bf16[16,1024]{1,0:T(8,128)(2,1)S(1)}, bf16[16,1024]{1,0:T(8,128)(2,1)S(1)}, u32[]{:S(2)}, u32[]{:S(2)}) collective-permute-start(bf16[16,1024]{1,0:T(8,128)(2,1)S(1)} %get-tuple-element.62), channel_id=1, source_target_pairs={{0,8},{8,16},{16,24},{24,32},{32,40},{40,48},{48,56},{56,57},{57,4... | collective-permute-start | bytes 98312 | tf_op jit(solution)/shard_map/ppermute | solution.py:532
  65.1 1.6 %shard_map.64.resid = f32[2688,128]{1,0:T(8,128)S(1)} custom-call(f32[2688,128]{1,0:T(8,128)S(1)} %get-tuple-element.42.bf, f32[2688,128]{1,0:T(8,128)S(1)} %get-tuple-element.57.xe.x2, f32[2688,128]{1,0:T(8,128)S(1)} %get-tuple-element.43.hf.he, f32[2688,128]{1,0:T(8,128)S(1)} %get-tuple-element.58.fw, f32[1,1024]{1,0:T(1,128)S(1)} %get-tuple-element.44.metric), custom_call_target="tpu_custom_call" | custom-call | flops 10000000 | bytes 4000000 | tf_op jit(solution)/shard_map/pallas_call | solution.py:590
  66.8 1.4 %shard_map.63 = (f32[2280,128]{1,0:T(8,128)S(1)}, f32[2048,128]{1,0:T(8,128)S(1)}, f32[2112,128]{1,0:T(8,128)S(1)}) custom-call(f32[32,64,128]{2,1,0:T(8,128)S(1)} %copy-done.1, f32[32]{0:T(128)S(1)} %copy-done.6), custom_call_target="tpu_custom_call" | custom-call | flops 10000000 | bytes 4000000 | tf_op jit(solution)/shard_map/pallas_call | solution.py:594
  68.2 0.4 collective-permute-done.7.xr
  68.7 1.3 %shard_map.65 = bf16[32,72,128]{2,1,0:T(8,128)(2,1)S(1)} custom-call(f32[2688,128]{1,0:T(8,128)S(1)} %shard_map.64.resid, f32[2688,128]{1,0:T(8,128)S(1)} %get-tuple-element.57.xe.x2, f32[2688,128]{1,0:T(8,128)S(1)} %get-tuple-element.51.d2, f32[2688,128]{1,0:T(8,128)S(1)} %get-tuple-element.43.hf.he, bf16[16,1024]{1,0:T(8,128)(2,1)S(1)} %collective-permute-done.4.su, ...), custom_call_target="tpu_custom_call" | custom-call | flops 10000000 | bytes 4000000 | tf_op jit(solution)/shard_map/pallas_call | solution.py:600
  69.9 16.6 %all_to_all.11.recv = bf16[32,72,128]{2,1,0:T(8,128)(2,1)S(1)} all-to-all(bf16[32,72,128]{2,1,0:T(8,128)(2,1)S(1)} %shard_map.65), channel_id=1, replica_groups=mesh['wall'=32,'span'=2,'stream'=4] {'wall'}, dimensions={0} | all-to-all | bytes 1179648 | tf_op jit(solution)/shard_map/all_to_all | solution.py:603
  86.5 0.8 shard_map.66
  87.3 1.5 %collective-permute-start.8 = (bf16[4,32,128]{2,1,0:T(8,128)(2,1)S(1)}, bf16[4,32,128]{2,1,0:T(8,128)(2,1)S(1)}, u32[]{:S(2)}, u32[]{:S(2)}) collective-permute-start(bf16[4,32,128]{2,1,0:T(8,128)(2,1)S(1)} %get-tuple-element.77), channel_id=1, source_target_pairs={{0,4},{4,0},{1,5},{5,1},{2,6},{6,2},{3,7},{7,3},{8,12},{12,8},{9,1... | collective-permute-start | bytes 98312 | tf_op jit(solution)/shard_map/ppermute | solution.py:512
  88.8 7.2 %collective-permute-start.10 = (bf16[32,128]{1,0:T(8,128)(2,1)S(1)}, bf16[32,128]{1,0:T(8,128)(2,1)S(1)}, u32[]{:S(2)}, u32[]{:S(2)}) collective-permute-start(bf16[32,128]{1,0:T(8,128)(2,1)S(1)} %get-tuple-element.72.dl), channel_id=1, source_target_pairs={{1,0},{2,1},{3,2},{0,3},{5,4},{6,5},{7,6},{4,7},{9,8},{10,9},{11,1... | collective-permute-start | bytes 24584 | tf_op jit(solution)/shard_map/ppermute | solution.py:514
  96.0 0.2 collective-permute-start.9
  96.2 2.4 %shard_map.67 = (f32[32,64,128]{2,1,0:T(8,128)}, f32[32,64,128]{2,1,0:T(8,128)S(1)}, f32[128,128]{1,0:T(8,128)S(1)}) custom-call(f32[2280,128]{1,0:T(8,128)S(1)} %get-tuple-element.68.xf, f32[2280,128]{1,0:T(8,128)S(1)} %get-tuple-element.69.hf, f32[2048,128]{1,0:T(8,128)S(1)} %get-tuple-element.70.gx, f32[2112,128]{1,0:T(8,128)S(1)} %get-tuple-element.71.gk, ...), custom_call_target="tpu_custom_call" | custom-call | flops 10000000 | bytes 4000000 | tf_op jit(solution)/shard_map/pallas_call | solution.py:611
  98.6 1.7 %shard_map.68 = f32[32,64,128]{2,1,0:T(8,128)} custom-call(f32[32,64,128]{2,1,0:T(8,128)S(1)} %get-tuple-element.75.resid, f32[2280,128]{1,0:T(8,128)S(1)} %get-tuple-element.68.xf, f32[2280,128]{1,0:T(8,128)S(1)} %get-tuple-element.69.hf, f32[128,128]{1,0:T(8,128)S(1)} %get-tuple-element.76.own, bf16[4,32,128]{2,1,0:T(8,128)(2,1)S(1)} %collective-permute-done.8.spans, ...), custom_call_target="tpu_custom_call" | custom-call | flops 10000000 | bytes 4000000 | tf_op jit(solution)/shard_map/pallas_call | solution.py:617
  (24 shorter events, 0.1 us)
Async XLA Ops:
  4.5 50.2 %copy-start = (bf16[1024,1024]{1,0:T(8,128)(2,1)S(1)}, bf16[1024,1024]{1,0:T(8,128)(2,1)}, u32[]{:S(2)}) copy-start(bf16[1024,1024]{1,0:T(8,128)(2,1)} %line.5) | copy-start | bytes 6291460
  47.7 10.3 %collective-permute-start = (bf16[32,1024]{1,0:T(8,128)(2,1)S(1)}, bf16[32,1024]{1,0:T(8,128)(2,1)S(1)}, u32[]{:S(2)}, u32[]{:S(2)}) collective-permute-start(bf16[32,1024]{1,0:T(8,128)(2,1)S(1)} %get-tuple-element.47), channel_id=1, source_target_pairs={{0,64},{8,72},{16,80},{24,88},{32,96},{40,104},{48,112},{56,120},{... | collective-permute-start | bytes 196616 | tf_op jit(solution)/shard_map/ppermute | solution.py:532
  48.1 9.9 %collective-permute-start.1 = (bf16[32,1024]{1,0:T(8,128)(2,1)S(1)}, bf16[32,1024]{1,0:T(8,128)(2,1)S(1)}, u32[]{:S(2)}, u32[]{:S(2)}) collective-permute-start(bf16[32,1024]{1,0:T(8,128)(2,1)S(1)} %get-tuple-element.48), channel_id=1, source_target_pairs={{0,4},{8,12},{16,20},{24,28},{32,36},{40,44},{48,52},{56,60},{57,6... | collective-permute-start | bytes 196616 | tf_op jit(solution)/shard_map/ppermute | solution.py:532
  50.8 7.2 %collective-permute-start.2 = (bf16[32,1024]{1,0:T(8,128)(2,1)S(1)}, bf16[32,1024]{1,0:T(8,128)(2,1)S(1)}, u32[]{:S(2)}, u32[]{:S(2)}) collective-permute-start(bf16[32,1024]{1,0:T(8,128)(2,1)S(1)} %get-tuple-element.49), channel_id=1, source_target_pairs={{0,8},{8,16},{16,24},{24,32},{32,40},{40,48},{48,56},{56,57},{57,4... | collective-permute-start | bytes 196616 | tf_op jit(solution)/shard_map/ppermute | solution.py:532
  54.7 3.7 %collective-permute-start.3 = (bf16[32,1024]{1,0:T(8,128)(2,1)S(1)}, bf16[32,1024]{1,0:T(8,128)(2,1)S(1)}, u32[]{:S(2)}, u32[]{:S(2)}) collective-permute-start(bf16[32,1024]{1,0:T(8,128)(2,1)S(1)} %get-tuple-element.50), channel_id=1, source_target_pairs={{0,3},{8,0},{16,8},{24,16},{32,24},{40,32},{48,40},{56,48},{57,56}... | collective-permute-start | bytes 196616 | tf_op jit(solution)/shard_map/ppermute | solution.py:532
  60.0 8.2 %collective-permute-start.4 = (bf16[16,1024]{1,0:T(8,128)(2,1)S(1)}, bf16[16,1024]{1,0:T(8,128)(2,1)S(1)}, u32[]{:S(2)}, u32[]{:S(2)}) collective-permute-start(bf16[16,1024]{1,0:T(8,128)(2,1)S(1)} %get-tuple-element.60), channel_id=1, source_target_pairs={{0,64},{8,72},{16,80},{24,88},{32,96},{40,104},{48,112},{56,120},{... | collective-permute-start | bytes 98312 | tf_op jit(solution)/shard_map/ppermute | solution.py:532
  60.1 8.1 %collective-permute-start.5 = (bf16[16,1024]{1,0:T(8,128)(2,1)S(1)}, bf16[16,1024]{1,0:T(8,128)(2,1)S(1)}, u32[]{:S(2)}, u32[]{:S(2)}) collective-permute-start(bf16[16,1024]{1,0:T(8,128)(2,1)S(1)} %get-tuple-element.61), channel_id=1, source_target_pairs={{0,4},{8,12},{16,20},{24,28},{32,36},{40,44},{48,52},{56,60},{57,6... | collective-permute-start | bytes 98312 | tf_op jit(solution)/shard_map/ppermute | solution.py:532
  63.1 5.1 %collective-permute-start.6 = (bf16[16,1024]{1,0:T(8,128)(2,1)S(1)}, bf16[16,1024]{1,0:T(8,128)(2,1)S(1)}, u32[]{:S(2)}, u32[]{:S(2)}) collective-permute-start(bf16[16,1024]{1,0:T(8,128)(2,1)S(1)} %get-tuple-element.62), channel_id=1, source_target_pairs={{0,8},{8,16},{16,24},{24,32},{32,40},{40,48},{48,56},{56,57},{57,4... | collective-permute-start | bytes 98312 | tf_op jit(solution)/shard_map/ppermute | solution.py:532
  65.1 3.5 %collective-permute-start.7 = (bf16[16,1024]{1,0:T(8,128)(2,1)S(1)}, bf16[16,1024]{1,0:T(8,128)(2,1)S(1)}, u32[]{:S(2)}, u32[]{:S(2)}) collective-permute-start(bf16[16,1024]{1,0:T(8,128)(2,1)S(1)} %get-tuple-element.63), channel_id=1, source_target_pairs={{0,3},{8,0},{16,8},{24,16},{32,24},{40,32},{48,40},{56,48},{57,56}... | collective-permute-start | bytes 98312 | tf_op jit(solution)/shard_map/ppermute | solution.py:532
  65.1 1.7 %copy-start.1 = (f32[32,64,128]{2,1,0:T(8,128)S(1)}, f32[32,64,128]{2,1,0:T(8,128)}, u32[]{:S(2)}) copy-start(f32[32,64,128]{2,1,0:T(8,128)} %v_ref) | copy-start | bytes 3145732
  65.1 1.7 %copy-start.6 = (f32[32]{0:T(128)S(1)}, f32[32]{0:T(128)}, u32[]{:S(2)}) copy-start(f32[32]{0:T(128)} %m_ref) | copy-start | bytes 388
  68.6 17.9 %copy-start.3 = (bf16[2,32,128]{2,1,0:T(8,128)(2,1)S(1)}, bf16[2,32,128]{2,1,0:T(8,128)(2,1)}, u32[]{:S(2)}) copy-start(bf16[2,32,128]{2,1,0:T(8,128)(2,1)} %get-tuple-element.65.ves) | copy-start | bytes 49156
  68.6 17.9 %copy-start.4 = (bf16[32,128]{1,0:T(8,128)(2,1)S(1)}, bf16[32,128]{1,0:T(8,128)(2,1)}, u32[]{:S(2)}) copy-start(bf16[32,128]{1,0:T(8,128)(2,1)} %get-tuple-element.66.vdl) | copy-start | bytes 24580
  68.7 17.9 %copy-start.5 = (bf16[32,128]{1,0:T(8,128)(2,1)S(1)}, bf16[32,128]{1,0:T(8,128)(2,1)}, u32[]{:S(2)}) copy-start(bf16[32,128]{1,0:T(8,128)(2,1)} %get-tuple-element.67.vdr) | copy-start | bytes 24580
  69.9 26.3 %copy-start.2 = (f32[32,64,128]{2,1,0:T(8,128)S(1)}, f32[32,64,128]{2,1,0:T(8,128)}, u32[]{:S(2)}) copy-start(f32[32,64,128]{2,1,0:T(8,128)} %b_ref.1) | copy-start | bytes 3145732
  87.3 11.3 %collective-permute-start.8 = (bf16[4,32,128]{2,1,0:T(8,128)(2,1)S(1)}, bf16[4,32,128]{2,1,0:T(8,128)(2,1)S(1)}, u32[]{:S(2)}, u32[]{:S(2)}) collective-permute-start(bf16[4,32,128]{2,1,0:T(8,128)(2,1)S(1)} %get-tuple-element.77), channel_id=1, source_target_pairs={{0,4},{4,0},{1,5},{5,1},{2,6},{6,2},{3,7},{7,3},{8,12},{12,8},{9,1... | collective-permute-start | bytes 98312 | tf_op jit(solution)/shard_map/ppermute | solution.py:512
  88.8 9.8 %collective-permute-start.10 = (bf16[32,128]{1,0:T(8,128)(2,1)S(1)}, bf16[32,128]{1,0:T(8,128)(2,1)S(1)}, u32[]{:S(2)}, u32[]{:S(2)}) collective-permute-start(bf16[32,128]{1,0:T(8,128)(2,1)S(1)} %get-tuple-element.72.dl), channel_id=1, source_target_pairs={{1,0},{2,1},{3,2},{0,3},{5,4},{6,5},{7,6},{4,7},{9,8},{10,9},{11,1... | collective-permute-start | bytes 24584 | tf_op jit(solution)/shard_map/ppermute | solution.py:514
  96.0 2.6 %collective-permute-start.9 = (bf16[32,128]{1,0:T(8,128)(2,1)S(1)}, bf16[32,128]{1,0:T(8,128)(2,1)S(1)}, u32[]{:S(2)}, u32[]{:S(2)}) collective-permute-start(bf16[32,128]{1,0:T(8,128)(2,1)S(1)} %get-tuple-element.73.dr), channel_id=1, source_target_pairs={{0,1},{1,2},{2,3},{3,0},{4,5},{5,6},{6,7},{7,4},{8,9},{9,10},{10,1... | collective-permute-start | bytes 24584 | tf_op jit(solution)/shard_map/ppermute | solution.py:513

commit v3 on v2

--- a/solution.py
+++ b/solution.py
@@ -108,9 +108,9 @@
         rows = pl.ds(BS * t, BS)
         return pltpu.make_async_copy(src.at[:, rows, :], dst.at[:, rows, :], sems.at[k, t])
 
-    def result(y):
-        peers = pl.ds(WZ * y, WZ)
-        return pltpu.make_async_copy(send.at[peers], send_hbm.at[peers], done.at[y])
+    def result(k, y):
+        part = (pl.ds(WZ * y, WZ), slice(2 * ROWS, None) if k else slice(0, 2 * ROWS))
+        return pltpu.make_async_copy(send.at[part], send_hbm.at[part], done.at[k, y])
 
     for k in range(2):
         for t in range(WY):
@@ -141,13 +141,7 @@
         move(t, 1, v_flat, MID)
         return 0
 
-    lax.fori_loop(0, WY, first, 0)
-    es[0] = (v_flat[strided(0), :] - MID).astype(BF16)
-    es[1] = (v_flat[strided(SPAN - 1), :] - MID).astype(BF16)
-    dl[...] = edge_lanes(cl[...], 0, 0, SPAN)
-    dr[...] = edge_lanes(cr[...], BX - 1, 1, SPAN)
-    for edge in edges:
-        edge.start()
+    lax.fori_loop(0, WY, first, 0, unroll=2)
     metric.wait()
     rest = m_buf[...]
     parts = []
@@ -159,34 +153,30 @@
     tail = jnp.concatenate([tail, jnp.zeros((TAIL, LANES - ROWS), F32)], axis=1).astype(BF16)
     for k in range(WY * WZ):
         send[k, 4 * ROWS :, :] = tail
+    for t in range(WY):
+        result(1, t).start()
 
     def last(t, _):
         copy(1, t).wait()
         move(t, 0, b_flat, 0.0)
-        result(owner(t, 0) // WZ).start()
+        result(0, owner(t, 0) // WZ).start()
         return 0
 
-    lax.fori_loop(0, WY, last, 0)
-    for t in range(WY):
-        result(t).wait()
+    lax.fori_loop(0, WY, last, 0, unroll=2)
+    es[0] = (v_flat[strided(0), :] - MID).astype(BF16)
+    es[1] = (v_flat[strided(SPAN - 1), :] - MID).astype(BF16)
+    dl[...] = edge_lanes(cl[...], 0, 0, SPAN)
+    dr[...] = edge_lanes(cr[...], BX - 1, 1, SPAN)
+    for edge in edges:
+        edge.start()
+    for k in range(2):
+        for t in range(WY):
+            result(k, t).wait()
     for edge in edges:
         edge.wait()
 
 
-def to_lines(recv, bf, hf, b0, metric, ends, *edges):
-    count = WY * WZ
-    nothing = jnp.zeros((1, LANES), F32)
-    for k in range(count):
-        rows = []
-        for g in range(2):
-            for other, at in ((k - 1, ROWS - 1), (k + 1, 0)):
-                if not 0 <= other < count:
-                    rows.append(nothing)
-                    continue
-                m = jnp.sum(recv[other, 4 * ROWS :, :].astype(F32), axis=0, keepdims=True)
-                v = recv[other, ROWS * (2 + g) : ROWS * (3 + g), :].astype(F32) + MID
-                rows.append(v[at : at + 1] * m[:, at : at + 1])
-        ends[k] = jnp.concatenate(rows, axis=0)
+def to_lines(recv, bf, hf, metric, *edges):
     for i in range(8):
         row = jnp.zeros((TAIL, LANES), F32)
         for j in range(4):
@@ -203,7 +193,6 @@
                     ref[line_rows(i, 8 * g + turned(p)), :] = tile[BX * p : BX * (p + 1)]
     for i in range(CHUNKS):
         lanes = slice(i * LANES, (i + 1) * LANES)
-        b0[:, lanes] = bf[pl.ds(ROW_COUNT * i + FIRST, BUSY), :].astype(BF16)
         for n, rows in enumerate(edge_rows(i)):
             edges[n][:BX, lanes] = bf[rows, :].astype(BF16)
             edges[n][BX:, lanes] = (2.0 * hf[rows, :] - MID).astype(BF16)
@@ -248,8 +237,10 @@
     return lax.dot_general(rows, line, (((1,), (1,)), ((), ())), preferred_element_type=F32)
 
 
-def first_lines(b0, bf, hf, metric, line, x1, fw, resid):
-    y = WEIGHTS[0][1] * apply_lines(b0[...], line[...])
+def first_lines(bf, hf, metric, line, x1, fw, resid, rounded):
+    for i in range(CHUNKS):
+        rounded[:, i * LANES : (i + 1) * LANES] = bf[busy(i), :].astype(BF16)
+    y = WEIGHTS[0][1] * apply_lines(rounded[...], line[...])
     for i in range(CHUNKS):
         x1[busy(i), :] = y[:, i * LANES : (i + 1) * LANES]
     mirror(x1)
@@ -382,7 +373,7 @@
                 xf[pl.ds(block_row(0) + s, ROWS, stride=CP), :] = parts[i].astype(F32)
         return 0
 
-    lax.fori_loop(0, WY, one, 0)
+    lax.fori_loop(0, WY, one, 0, unroll=4)
     for k, (s, beside) in enumerate(((0, -1), (SPAN - 1, SPAN))):
         edge = xf[block_span(s), :]
         xf[block_span(beside), :] = edge
@@ -395,7 +386,7 @@
     dr[...] = edge_lanes(cr[...], BX - 1, 1, 0) + vdr[...]
 
 
-def weights(v_ref, m_ref, hf, gx, gk):
+def weights(v_ref, m_ref, recv, metric, hf, gx, gk, ends):
     def four(n, below):
         for k in range(4):
             w = 4 * n + k
@@ -411,6 +402,18 @@
     gk[SPAN * ROWS :, :] = lax.fori_loop(0, ROWS // 4, four, jnp.zeros((SPAN, LANES), F32))
     for s in (-1, SPAN):
         hf[block_span(s), :] = jnp.zeros((ROWS, LANES), F32)
+    count = WY * WZ
+    nothing = jnp.zeros((1, LANES), F32)
+    for k in range(count):
+        rows = []
+        for g in range(2):
+            for other, at in ((k - 1, ROWS - 1), (k + 1, 0)):
+                if not 0 <= other < count:
+                    rows.append(nothing)
+                    continue
+                v = recv[other, ROWS * (2 + g) : ROWS * (3 + g), :].astype(F32) + MID
+                rows.append(v[at : at + 1] * metric[:, ROWS * other + at : ROWS * other + at + 1])
+        ends[k] = jnp.concatenate(rows, axis=0)
 
 
 def placed(right, left):
@@ -562,7 +565,7 @@
             side,
             side,
             dma((2, WY)),
-            dma((WY,)),
+            dma((2, WY)),
             dma((4,)),
         ),
         62 * MIB + MIB // 2,
@@ -571,16 +574,17 @@
     )(right_side, viscosity, wall_metric.reshape(1, ROWS))
     recv = lax.all_to_all(send, "wall", 0, 0, tiled=True)
     field = shape((CHUNKS * ROW_COUNT, LANES), F32)
-    bf, hf, b0, metric, ends, *edges = call(
+    bf, hf, metric, *edges = call(
         to_lines,
-        (field, field, shape((BUSY, NW), BF16), shape((1, NW), F32))
-        + (shape((WY * WZ, 4, LANES), F32),)
+        (field, field, shape((1, NW), F32))
         + (shape((2 * BX, NW), BF16),) * 4,
     )(recv)
     near = line_edges(*edges)
-    x1, fw, resid = call(first_lines, (field, field, field))(b0, bf, hf, metric, line_inverse)
     ext = pltpu.VMEM((CHUNKS * ROW_COUNT, LANES), F32)
     rounded = pltpu.VMEM((BUSY, NW), BF16)
+    x1, fw, resid = call(first_lines, (field, field, field), (rounded,))(
+        bf, hf, metric, line_inverse
+    )
     x2, d2, *edges = call(
         second_step,
         (field, field) + (shape((BX, NW), BF16),) * 4,
@@ -591,11 +595,16 @@
     v, m, _ = lax.optimization_barrier((viscosity, wall_metric, d2))
     smem = pl.BlockSpec(memory_space=pltpu.SMEM)
     cells = shape((BLOCK_ROWS, LANES), F32)
-    face_weights = call(
+    *face_weights, ends = call(
         weights,
-        (cells, shape((ROWS * SPAN, LANES), F32), shape(((ROWS + 1) * SPAN, LANES), F32)),
-        in_specs=(vmem, smem),
-    )(v, m)
+        (
+            cells,
+            shape((ROWS * SPAN, LANES), F32),
+            shape(((ROWS + 1) * SPAN, LANES), F32),
+            shape((WY * WZ, 4, LANES), F32),
+        ),
+        in_specs=(vmem, smem, vmem, vmem),
+    )(v, m, recv, metric)
     face_weights, resid = lax.optimization_barrier((face_weights, resid))
     send = call(
         third_step, shape((WY * WZ, 2 * ROWS + TAIL, LANES), BF16), (ext, rounded)

time: 101 us -> 99.8 us (0.988)
  Pallas kernels: 18.6 us -> 17.5 us
  transfers between devices with their start and end apart: 11 -> 11, of which waited for: 2 -> 2; matrix products, arithmetic and copies ran while one was open for 0% -> 0% of each run, Pallas kernels for 9% -> 8%
where the time goes in v3:
time: 99.8 us; the launch traced here: 99.6 us
  blocking collectives  59.4 us (60%)
  starting transfers between devices  20.8 us (21%)
  Pallas kernels  17.5 us (18%)
    all_to_all x2, blocking collectives, body(): recv = lax.all_to_all(send, 'wall', 0, 0, tiled=True)  59.4 us
    ppermute x8, starting transfers between devices, line_shift(): return lax.ppermute(value, ('wall', 'span', 'stream'), pairs)  12.1 us
    ppermute x1, starting transfers between devices, block_edges(): lax.ppermute(dl, 'stream', left)  7.25 us
    pallas_call x1, Pallas kernels, body(): call(pack, (shape(sent, BF16), shape((2, ROWS, LANES), BF16), dense, dens...  3.73 us
    pallas_call x1, Pallas kernels, body(): call(first_lines, (field, field, field), (rounded,))  2.98 us
    pallas_call x1, Pallas kernels, body(): call(inner_resid, (whole, whole, shape((LANES, LANES), F32)), (block, plt...  2.34 us
  transfers between devices with their start and end apart: 11, of which 2 were waited for; matrix products, arithmetic and copies ran while one was open for 0% of the time, Pallas kernels for 8%

profile of v3, /device:TPU:1, one launch (start us, length us, event | category | flops | bytes accessed | tf_op | source)
XLA Modules:
  0.0 99.6 jit_solution(13895898245320497211)
XLA Ops:
  0.6 3.7 %shard_map.59 = (bf16[32,136,128]{2,1,0:T(8,128)(2,1)}, bf16[2,32,128]{2,1,0:T(8,128)(2,1)}, bf16[32,128]{1,0:T(8,128)(2,1)}, bf16[32,128]{1,0:T(8,128)(2,1)}) custom-call(f32[32,64,128]{2,1,0:T(8,128)} %b_ref.1, f32[32,64,128]{2,1,0:T(8,128)} %v_ref, f32[1,32]{1,0:T(1,128)} %bitcast.1), custom_call_target="tpu_custom_call" | custom-call | flops 10000000 | bytes 4000000 | tf_op jit(solution)/shard_map/pallas_call | solution.py:554
  4.4 0.0 copy-start
  4.4 42.6 %all_to_all.10.recv = bf16[32,136,128]{2,1,0:T(8,128)(2,1)S(1)} all-to-all(bf16[32,136,128]{2,1,0:T(8,128)(2,1)} %get-tuple-element.39), channel_id=1, replica_groups=mesh['wall'=32,'span'=2,'stream'=4] {'wall'}, dimensions={0} | all-to-all | bytes 2228224 | tf_op jit(solution)/shard_map/all_to_all | solution.py:575
  47.0 0.4 shard_map.60
  47.4 0.4 collective-permute-start
  47.8 2.7 %collective-permute-start.1 = (bf16[32,1024]{1,0:T(8,128)(2,1)S(1)}, bf16[32,1024]{1,0:T(8,128)(2,1)S(1)}, u32[]{:S(2)}, u32[]{:S(2)}) collective-permute-start(bf16[32,1024]{1,0:T(8,128)(2,1)S(1)} %get-tuple-element.46), channel_id=1, source_target_pairs={{0,4},{8,12},{16,20},{24,28},{32,36},{40,44},{48,52},{56,60},{57,6... | collective-permute-start | bytes 196616 | tf_op jit(solution)/shard_map/ppermute | solution.py:535
  50.5 3.9 %collective-permute-start.2 = (bf16[32,1024]{1,0:T(8,128)(2,1)S(1)}, bf16[32,1024]{1,0:T(8,128)(2,1)S(1)}, u32[]{:S(2)}, u32[]{:S(2)}) collective-permute-start(bf16[32,1024]{1,0:T(8,128)(2,1)S(1)} %get-tuple-element.47), channel_id=1, source_target_pairs={{0,8},{8,16},{16,24},{24,32},{32,40},{40,48},{48,56},{56,57},{57,4... | collective-permute-start | bytes 196616 | tf_op jit(solution)/shard_map/ppermute | solution.py:535
  54.4 3.0 %shard_map.61 = (f32[2688,128]{1,0:T(8,128)S(1)}, f32[2688,128]{1,0:T(8,128)S(1)}, f32[2688,128]{1,0:T(8,128)S(1)}) custom-call(f32[2688,128]{1,0:T(8,128)S(1)} %get-tuple-element.40.bf, f32[2688,128]{1,0:T(8,128)S(1)} %get-tuple-element.41.hf.he, f32[1,1024]{1,0:T(1,128)S(1)} %get-tuple-element.42.metric, bf16[1024,1024]{1,0:T(8,128)(2,1)S(1)} %copy-done), custom_call_target="tpu_custom_call" | custom-call | flops 10000000 | bytes 4000000 | tf_op jit(solution)/shard_map/pallas_call | solution.py:585
  57.4 0.7 collective-permute-done.3.xr.vxr
  58.1 1.6 %shard_map.62 = (f32[2688,128]{1,0:T(8,128)S(1)}, f32[2688,128]{1,0:T(8,128)S(1)}, bf16[16,1024]{1,0:T(8,128)(2,1)S(1)}, bf16[16,1024]{1,0:T(8,128)(2,1)S(1)}, b...) custom-call(f32[2688,128]{1,0:T(8,128)S(1)} %get-tuple-element.43.resid, f32[2688,128]{1,0:T(8,128)S(1)} %get-tuple-element.44.x1, ...), custom_call_target="tpu_custom_call" | custom-call | flops 10000000 | bytes 4000000 | tf_op jit(solution)/shard_map/pallas_call | solution.py:588
  59.7 0.1 collective-permute-start.4
  59.7 3.0 %collective-permute-start.5 = (bf16[16,1024]{1,0:T(8,128)(2,1)S(1)}, bf16[16,1024]{1,0:T(8,128)(2,1)S(1)}, u32[]{:S(2)}, u32[]{:S(2)}) collective-permute-start(bf16[16,1024]{1,0:T(8,128)(2,1)S(1)} %get-tuple-element.59), channel_id=1, source_target_pairs={{0,4},{8,12},{16,20},{24,28},{32,36},{40,44},{48,52},{56,60},{57,6... | collective-permute-start | bytes 98312 | tf_op jit(solution)/shard_map/ppermute | solution.py:535
  62.7 2.0 %collective-permute-start.6 = (bf16[16,1024]{1,0:T(8,128)(2,1)S(1)}, bf16[16,1024]{1,0:T(8,128)(2,1)S(1)}, u32[]{:S(2)}, u32[]{:S(2)}) collective-permute-start(bf16[16,1024]{1,0:T(8,128)(2,1)S(1)} %get-tuple-element.60), channel_id=1, source_target_pairs={{0,8},{8,16},{16,24},{24,32},{32,40},{40,48},{48,56},{56,57},{57,4... | collective-permute-start | bytes 98312 | tf_op jit(solution)/shard_map/ppermute | solution.py:535
  64.8 1.6 %shard_map.64.resid = f32[2688,128]{1,0:T(8,128)S(1)} custom-call(f32[2688,128]{1,0:T(8,128)S(1)} %get-tuple-element.40.bf, f32[2688,128]{1,0:T(8,128)S(1)} %get-tuple-element.55.xe.x2, f32[2688,128]{1,0:T(8,128)S(1)} %get-tuple-element.41.hf.he, f32[2688,128]{1,0:T(8,128)S(1)} %get-tuple-element.56.fw, f32[1,1024]{1,0:T(1,128)S(1)} %get-tuple-element.42.metric), custom_call_target="tpu_custom_call" | custom-call | flops 10000000 | bytes 4000000 | tf_op jit(solution)/shard_map/pallas_call | solution.py:594
  66.4 1.5 %shard_map.63 = (f32[2280,128]{1,0:T(8,128)S(1)}, f32[2048,128]{1,0:T(8,128)S(1)}, f32[2112,128]{1,0:T(8,128)S(1)}, f32[32,4,128]{2,1,0:T(4,128)S(1)}) custom-call(f32[32,64,128]{2,1,0:T(8,128)S(1)} %copy-done.1, f32[32]{0:T(128)S(1)} %copy-done.6, bf16[32,136,128]{2,1,0:T(8,128)(2,1)S(1)} %all_to_all.10.recv, f32[1,1024]{1,0:T(1,128)S(1)} %get-tuple-element.42.metric), custom_call_target="tpu_custom_call" | custom-call | flops 10000000 | bytes 4000000 | tf_op jit(solution)/shard_map/pallas_call | solution.py:598
  67.9 0.2 collective-permute-done.7.xr
  68.1 1.2 %shard_map.65 = bf16[32,72,128]{2,1,0:T(8,128)(2,1)S(1)} custom-call(f32[2688,128]{1,0:T(8,128)S(1)} %shard_map.64.resid, f32[2688,128]{1,0:T(8,128)S(1)} %get-tuple-element.55.xe.x2, f32[2688,128]{1,0:T(8,128)S(1)} %get-tuple-element.49.d2, f32[2688,128]{1,0:T(8,128)S(1)} %get-tuple-element.41.hf.he, bf16[16,1024]{1,0:T(8,128)(2,1)S(1)} %collective-permute-done.4.su, ...), custom_call_target="tpu_custom_call" | custom-call | flops 10000000 | bytes 4000000 | tf_op jit(solution)/shard_map/pallas_call | solution.py:609
  69.3 16.8 %all_to_all.11.recv = bf16[32,72,128]{2,1,0:T(8,128)(2,1)S(1)} all-to-all(bf16[32,72,128]{2,1,0:T(8,128)(2,1)S(1)} %shard_map.65), channel_id=1, replica_groups=mesh['wall'=32,'span'=2,'stream'=4] {'wall'}, dimensions={0} | all-to-all | bytes 1179648 | tf_op jit(solution)/shard_map/all_to_all | solution.py:612
  86.1 0.4 shard_map.66
  86.5 1.3 %collective-permute-start.8 = (bf16[4,32,128]{2,1,0:T(8,128)(2,1)S(1)}, bf16[4,32,128]{2,1,0:T(8,128)(2,1)S(1)}, u32[]{:S(2)}, u32[]{:S(2)}) collective-permute-start(bf16[4,32,128]{2,1,0:T(8,128)(2,1)S(1)} %get-tuple-element.75), channel_id=1, source_target_pairs={{0,4},{4,0},{1,5},{5,1},{2,6},{6,2},{3,7},{7,3},{8,12},{12,8},{9,1... | collective-permute-start | bytes 98312 | tf_op jit(solution)/shard_map/ppermute | solution.py:515
  87.8 7.2 %collective-permute-start.10 = (bf16[32,128]{1,0:T(8,128)(2,1)S(1)}, bf16[32,128]{1,0:T(8,128)(2,1)S(1)}, u32[]{:S(2)}, u32[]{:S(2)}) collective-permute-start(bf16[32,128]{1,0:T(8,128)(2,1)S(1)} %get-tuple-element.70.dl), channel_id=1, source_target_pairs={{1,0},{2,1},{3,2},{0,3},{5,4},{6,5},{7,6},{4,7},{9,8},{10,9},{11,1... | collective-permute-start | bytes 24584 | tf_op jit(solution)/shard_map/ppermute | solution.py:517
  95.1 0.2 collective-permute-start.9
  95.3 2.3 %shard_map.67 = (f32[32,64,128]{2,1,0:T(8,128)}, f32[32,64,128]{2,1,0:T(8,128)S(1)}, f32[128,128]{1,0:T(8,128)S(1)}) custom-call(f32[2280,128]{1,0:T(8,128)S(1)} %get-tuple-element.66.xf, f32[2280,128]{1,0:T(8,128)S(1)} %get-tuple-element.67.hf, f32[2048,128]{1,0:T(8,128)S(1)} %get-tuple-element.68.gx, f32[2112,128]{1,0:T(8,128)S(1)} %get-tuple-element.69.gk, ...), custom_call_target="tpu_custom_call" | custom-call | flops 10000000 | bytes 4000000 | tf_op jit(solution)/shard_map/pallas_call | solution.py:620
  97.7 1.7 %shard_map.68 = f32[32,64,128]{2,1,0:T(8,128)} custom-call(f32[32,64,128]{2,1,0:T(8,128)S(1)} %get-tuple-element.73.resid, f32[2280,128]{1,0:T(8,128)S(1)} %get-tuple-element.66.xf, f32[2280,128]{1,0:T(8,128)S(1)} %get-tuple-element.67.hf, f32[128,128]{1,0:T(8,128)S(1)} %get-tuple-element.74.own, bf16[4,32,128]{2,1,0:T(8,128)(2,1)S(1)} %collective-permute-done.8.spans, ...), custom_call_target="tpu_custom_call" | custom-call | flops 10000000 | bytes 4000000 | tf_op jit(solution)/shard_map/pallas_call | solution.py:626
  (24 shorter events, 0.1 us)
Async XLA Ops:
  4.4 50.0 %copy-start = (bf16[1024,1024]{1,0:T(8,128)(2,1)S(1)}, bf16[1024,1024]{1,0:T(8,128)(2,1)}, u32[]{:S(2)}) copy-start(bf16[1024,1024]{1,0:T(8,128)(2,1)} %line.5) | copy-start | bytes 6291460
  47.4 10.0 %collective-permute-start = (bf16[32,1024]{1,0:T(8,128)(2,1)S(1)}, bf16[32,1024]{1,0:T(8,128)(2,1)S(1)}, u32[]{:S(2)}, u32[]{:S(2)}) collective-permute-start(bf16[32,1024]{1,0:T(8,128)(2,1)S(1)} %get-tuple-element.45), channel_id=1, source_target_pairs={{0,64},{8,72},{16,80},{24,88},{32,96},{40,104},{48,112},{56,120},{... | collective-permute-start | bytes 196616 | tf_op jit(solution)/shard_map/ppermute | solution.py:535
  47.8 9.6 %collective-permute-start.1 = (bf16[32,1024]{1,0:T(8,128)(2,1)S(1)}, bf16[32,1024]{1,0:T(8,128)(2,1)S(1)}, u32[]{:S(2)}, u32[]{:S(2)}) collective-permute-start(bf16[32,1024]{1,0:T(8,128)(2,1)S(1)} %get-tuple-element.46), channel_id=1, source_target_pairs={{0,4},{8,12},{16,20},{24,28},{32,36},{40,44},{48,52},{56,60},{57,6... | collective-permute-start | bytes 196616 | tf_op jit(solution)/shard_map/ppermute | solution.py:535
  50.5 6.9 %collective-permute-start.2 = (bf16[32,1024]{1,0:T(8,128)(2,1)S(1)}, bf16[32,1024]{1,0:T(8,128)(2,1)S(1)}, u32[]{:S(2)}, u32[]{:S(2)}) collective-permute-start(bf16[32,1024]{1,0:T(8,128)(2,1)S(1)} %get-tuple-element.47), channel_id=1, source_target_pairs={{0,8},{8,16},{16,24},{24,32},{32,40},{40,48},{48,56},{56,57},{57,4... | collective-permute-start | bytes 196616 | tf_op jit(solution)/shard_map/ppermute | solution.py:535
  54.4 3.7 %collective-permute-start.3 = (bf16[32,1024]{1,0:T(8,128)(2,1)S(1)}, bf16[32,1024]{1,0:T(8,128)(2,1)S(1)}, u32[]{:S(2)}, u32[]{:S(2)}) collective-permute-start(bf16[32,1024]{1,0:T(8,128)(2,1)S(1)} %get-tuple-element.48), channel_id=1, source_target_pairs={{0,3},{8,0},{16,8},{24,16},{32,24},{40,32},{48,40},{56,48},{57,56}... | collective-permute-start | bytes 196616 | tf_op jit(solution)/shard_map/ppermute | solution.py:535
  59.7 8.2 %collective-permute-start.4 = (bf16[16,1024]{1,0:T(8,128)(2,1)S(1)}, bf16[16,1024]{1,0:T(8,128)(2,1)S(1)}, u32[]{:S(2)}, u32[]{:S(2)}) collective-permute-start(bf16[16,1024]{1,0:T(8,128)(2,1)S(1)} %get-tuple-element.58), channel_id=1, source_target_pairs={{0,64},{8,72},{16,80},{24,88},{32,96},{40,104},{48,112},{56,120},{... | collective-permute-start | bytes 98312 | tf_op jit(solution)/shard_map/ppermute | solution.py:535
  59.7 8.2 %collective-permute-start.5 = (bf16[16,1024]{1,0:T(8,128)(2,1)S(1)}, bf16[16,1024]{1,0:T(8,128)(2,1)S(1)}, u32[]{:S(2)}, u32[]{:S(2)}) collective-permute-start(bf16[16,1024]{1,0:T(8,128)(2,1)S(1)} %get-tuple-element.59), channel_id=1, source_target_pairs={{0,4},{8,12},{16,20},{24,28},{32,36},{40,44},{48,52},{56,60},{57,6... | collective-permute-start | bytes 98312 | tf_op jit(solution)/shard_map/ppermute | solution.py:535
  62.7 5.2 %collective-permute-start.6 = (bf16[16,1024]{1,0:T(8,128)(2,1)S(1)}, bf16[16,1024]{1,0:T(8,128)(2,1)S(1)}, u32[]{:S(2)}, u32[]{:S(2)}) collective-permute-start(bf16[16,1024]{1,0:T(8,128)(2,1)S(1)} %get-tuple-element.60), channel_id=1, source_target_pairs={{0,8},{8,16},{16,24},{24,32},{32,40},{40,48},{48,56},{56,57},{57,4... | collective-permute-start | bytes 98312 | tf_op jit(solution)/shard_map/ppermute | solution.py:535
  64.8 3.3 %collective-permute-start.7 = (bf16[16,1024]{1,0:T(8,128)(2,1)S(1)}, bf16[16,1024]{1,0:T(8,128)(2,1)S(1)}, u32[]{:S(2)}, u32[]{:S(2)}) collective-permute-start(bf16[16,1024]{1,0:T(8,128)(2,1)S(1)} %get-tuple-element.61), channel_id=1, source_target_pairs={{0,3},{8,0},{16,8},{24,16},{32,24},{40,32},{48,40},{56,48},{57,56}... | collective-permute-start | bytes 98312 | tf_op jit(solution)/shard_map/ppermute | solution.py:535
  64.8 1.6 %copy-start.1 = (f32[32,64,128]{2,1,0:T(8,128)S(1)}, f32[32,64,128]{2,1,0:T(8,128)}, u32[]{:S(2)}) copy-start(f32[32,64,128]{2,1,0:T(8,128)} %v_ref) | copy-start | bytes 3145732
  64.8 1.6 %copy-start.6 = (f32[32]{0:T(128)S(1)}, f32[32]{0:T(128)}, u32[]{:S(2)}) copy-start(f32[32]{0:T(128)} %m_ref) | copy-start | bytes 388
  68.1 18.0 %copy-start.3 = (bf16[2,32,128]{2,1,0:T(8,128)(2,1)S(1)}, bf16[2,32,128]{2,1,0:T(8,128)(2,1)}, u32[]{:S(2)}) copy-start(bf16[2,32,128]{2,1,0:T(8,128)(2,1)} %get-tuple-element.63.ves) | copy-start | bytes 49156
  68.1 18.0 %copy-start.4 = (bf16[32,128]{1,0:T(8,128)(2,1)S(1)}, bf16[32,128]{1,0:T(8,128)(2,1)}, u32[]{:S(2)}) copy-start(bf16[32,128]{1,0:T(8,128)(2,1)} %get-tuple-element.64.vdl) | copy-start | bytes 24580
  68.1 18.0 %copy-start.5 = (bf16[32,128]{1,0:T(8,128)(2,1)S(1)}, bf16[32,128]{1,0:T(8,128)(2,1)}, u32[]{:S(2)}) copy-start(bf16[32,128]{1,0:T(8,128)(2,1)} %get-tuple-element.65.vdr) | copy-start | bytes 24580
  69.3 26.0 %copy-start.2 = (f32[32,64,128]{2,1,0:T(8,128)S(1)}, f32[32,64,128]{2,1,0:T(8,128)}, u32[]{:S(2)}) copy-start(f32[32,64,128]{2,1,0:T(8,128)} %b_ref.1) | copy-start | bytes 3145732
  86.5 11.2 %collective-permute-start.8 = (bf16[4,32,128]{2,1,0:T(8,128)(2,1)S(1)}, bf16[4,32,128]{2,1,0:T(8,128)(2,1)S(1)}, u32[]{:S(2)}, u32[]{:S(2)}) collective-permute-start(bf16[4,32,128]{2,1,0:T(8,128)(2,1)S(1)} %get-tuple-element.75), channel_id=1, source_target_pairs={{0,4},{4,0},{1,5},{5,1},{2,6},{6,2},{3,7},{7,3},{8,12},{12,8},{9,1... | collective-permute-start | bytes 98312 | tf_op jit(solution)/shard_map/ppermute | solution.py:515
  87.8 9.8 %collective-permute-start.10 = (bf16[32,128]{1,0:T(8,128)(2,1)S(1)}, bf16[32,128]{1,0:T(8,128)(2,1)S(1)}, u32[]{:S(2)}, u32[]{:S(2)}) collective-permute-start(bf16[32,128]{1,0:T(8,128)(2,1)S(1)} %get-tuple-element.70.dl), channel_id=1, source_target_pairs={{1,0},{2,1},{3,2},{0,3},{5,4},{6,5},{7,6},{4,7},{9,8},{10,9},{11,1... | collective-permute-start | bytes 24584 | tf_op jit(solution)/shard_map/ppermute | solution.py:517
  95.1 2.6 %collective-permute-start.9 = (bf16[32,128]{1,0:T(8,128)(2,1)S(1)}, bf16[32,128]{1,0:T(8,128)(2,1)S(1)}, u32[]{:S(2)}, u32[]{:S(2)}) collective-permute-start(bf16[32,128]{1,0:T(8,128)(2,1)S(1)} %get-tuple-element.71.dr), channel_id=1, source_target_pairs={{0,1},{1,2},{2,3},{3,0},{4,5},{5,6},{6,7},{7,4},{8,9},{9,10},{10,1... | collective-permute-start | bytes 24584 | tf_op jit(solution)/shard_map/ppermute | solution.py:516

commit v4 on v3

--- a/solution.py
+++ b/solution.py
@@ -141,7 +141,7 @@
         move(t, 1, v_flat, MID)
         return 0
 
-    lax.fori_loop(0, WY, first, 0, unroll=2)
+    lax.fori_loop(0, WY, first, 0, unroll=4)
     metric.wait()
     rest = m_buf[...]
     parts = []
@@ -162,7 +162,7 @@
         result(0, owner(t, 0) // WZ).start()
         return 0
 
-    lax.fori_loop(0, WY, last, 0, unroll=2)
+    lax.fori_loop(0, WY, last, 0, unroll=4)
     es[0] = (v_flat[strided(0), :] - MID).astype(BF16)
     es[1] = (v_flat[strided(SPAN - 1), :] - MID).astype(BF16)
     dl[...] = edge_lanes(cl[...], 0, 0, SPAN)
@@ -502,7 +502,7 @@
         results(q).start()
         return carry
 
-    lax.fori_loop(0, ROWS // 4, four, 0)
+    lax.fori_loop(0, ROWS // 4, four, 0, unroll=4)
     for q in range(ROWS // 4):
         results(q).wait()
 

time: 99.8 us -> 99.1 us (level)
  transfers between devices with their start and end apart: 11 -> 11, of which waited for: 2 -> 2; matrix products, arithmetic and copies ran while one was open for 0% -> 0% of each run, Pallas kernels for 8% -> 9%
where the time goes in v4:
time: 99.1 us; the launch traced here: 98.8 us
  blocking collectives  59.1 us (60%)
  starting transfers between devices  20.9 us (21%)
  Pallas kernels  16.9 us (17%)
    all_to_all x2, blocking collectives, body(): recv = lax.all_to_all(send, 'wall', 0, 0, tiled=True)  59.1 us
    ppermute x8, starting transfers between devices, line_shift(): return lax.ppermute(value, ('wall', 'span', 'stream'), pairs)  12.1 us
    ppermute x1, starting transfers between devices, block_edges(): lax.ppermute(dl, 'stream', left)  7.25 us
    pallas_call x1, Pallas kernels, body(): call(pack, (shape(sent, BF16), shape((2, ROWS, LANES), BF16), dense, dens...  3.57 us
    pallas_call x1, Pallas kernels, body(): call(first_lines, (field, field, field), (rounded,))  2.98 us
    pallas_call x1, Pallas kernels, body(): call(inner_resid, (whole, whole, shape((LANES, LANES), F32)), (block, plt...  2.34 us
  transfers between devices with their start and end apart: 11, of which 2 were waited for; matrix products, arithmetic and copies ran while one was open for 0% of the time, Pallas kernels for 9%

profile of v4, /device:TPU:1, one launch (start us, length us, event | category | flops | bytes accessed | tf_op | source)
XLA Modules:
  0.0 98.8 jit_solution(17330827252844642341)
XLA Ops:
  0.6 3.6 %shard_map.59 = (bf16[32,136,128]{2,1,0:T(8,128)(2,1)}, bf16[2,32,128]{2,1,0:T(8,128)(2,1)}, bf16[32,128]{1,0:T(8,128)(2,1)}, bf16[32,128]{1,0:T(8,128)(2,1)}) custom-call(f32[32,64,128]{2,1,0:T(8,128)} %b_ref.1, f32[32,64,128]{2,1,0:T(8,128)} %v_ref, f32[1,32]{1,0:T(1,128)} %bitcast.1), custom_call_target="tpu_custom_call" | custom-call | flops 10000000 | bytes 4000000 | tf_op jit(solution)/shard_map/pallas_call | solution.py:554
  4.2 42.6 %all_to_all.10.recv = bf16[32,136,128]{2,1,0:T(8,128)(2,1)S(1)} all-to-all(bf16[32,136,128]{2,1,0:T(8,128)(2,1)} %get-tuple-element.39), channel_id=1, replica_groups=mesh['wall'=32,'span'=2,'stream'=4] {'wall'}, dimensions={0} | all-to-all | bytes 2228224 | tf_op jit(solution)/shard_map/all_to_all | solution.py:575
  46.8 0.4 shard_map.60
  47.2 0.4 collective-permute-start
  47.6 2.7 %collective-permute-start.1 = (bf16[32,1024]{1,0:T(8,128)(2,1)S(1)}, bf16[32,1024]{1,0:T(8,128)(2,1)S(1)}, u32[]{:S(2)}, u32[]{:S(2)}) collective-permute-start(bf16[32,1024]{1,0:T(8,128)(2,1)S(1)} %get-tuple-element.46), channel_id=1, source_target_pairs={{0,4},{8,12},{16,20},{24,28},{32,36},{40,44},{48,52},{56,60},{57,6... | collective-permute-start | bytes 196616 | tf_op jit(solution)/shard_map/ppermute | solution.py:535
  50.3 3.9 %collective-permute-start.2 = (bf16[32,1024]{1,0:T(8,128)(2,1)S(1)}, bf16[32,1024]{1,0:T(8,128)(2,1)S(1)}, u32[]{:S(2)}, u32[]{:S(2)}) collective-permute-start(bf16[32,1024]{1,0:T(8,128)(2,1)S(1)} %get-tuple-element.47), channel_id=1, source_target_pairs={{0,8},{8,16},{16,24},{24,32},{32,40},{40,48},{48,56},{56,57},{57,4... | collective-permute-start | bytes 196616 | tf_op jit(solution)/shard_map/ppermute | solution.py:535
  54.2 3.0 %shard_map.61 = (f32[2688,128]{1,0:T(8,128)S(1)}, f32[2688,128]{1,0:T(8,128)S(1)}, f32[2688,128]{1,0:T(8,128)S(1)}) custom-call(f32[2688,128]{1,0:T(8,128)S(1)} %get-tuple-element.40.bf, f32[2688,128]{1,0:T(8,128)S(1)} %get-tuple-element.41.hf.he, f32[1,1024]{1,0:T(1,128)S(1)} %get-tuple-element.42.metric, bf16[1024,1024]{1,0:T(8,128)(2,1)S(1)} %copy-done), custom_call_target="tpu_custom_call" | custom-call | flops 10000000 | bytes 4000000 | tf_op jit(solution)/shard_map/pallas_call | solution.py:585
  57.2 0.7 collective-permute-done.3.xr.vxr
  57.9 1.6 %shard_map.62 = (f32[2688,128]{1,0:T(8,128)S(1)}, f32[2688,128]{1,0:T(8,128)S(1)}, bf16[16,1024]{1,0:T(8,128)(2,1)S(1)}, bf16[16,1024]{1,0:T(8,128)(2,1)S(1)}, b...) custom-call(f32[2688,128]{1,0:T(8,128)S(1)} %get-tuple-element.43.resid, f32[2688,128]{1,0:T(8,128)S(1)} %get-tuple-element.44.x1, ...), custom_call_target="tpu_custom_call" | custom-call | flops 10000000 | bytes 4000000 | tf_op jit(solution)/shard_map/pallas_call | solution.py:588
  59.5 0.1 collective-permute-start.4
  59.6 3.0 %collective-permute-start.5 = (bf16[16,1024]{1,0:T(8,128)(2,1)S(1)}, bf16[16,1024]{1,0:T(8,128)(2,1)S(1)}, u32[]{:S(2)}, u32[]{:S(2)}) collective-permute-start(bf16[16,1024]{1,0:T(8,128)(2,1)S(1)} %get-tuple-element.59), channel_id=1, source_target_pairs={{0,4},{8,12},{16,20},{24,28},{32,36},{40,44},{48,52},{56,60},{57,6... | collective-permute-start | bytes 98312 | tf_op jit(solution)/shard_map/ppermute | solution.py:535
  62.5 2.0 %collective-permute-start.6 = (bf16[16,1024]{1,0:T(8,128)(2,1)S(1)}, bf16[16,1024]{1,0:T(8,128)(2,1)S(1)}, u32[]{:S(2)}, u32[]{:S(2)}) collective-permute-start(bf16[16,1024]{1,0:T(8,128)(2,1)S(1)} %get-tuple-element.60), channel_id=1, source_target_pairs={{0,8},{8,16},{16,24},{24,32},{32,40},{40,48},{48,56},{56,57},{57,4... | collective-permute-start | bytes 98312 | tf_op jit(solution)/shard_map/ppermute | solution.py:535
  64.6 1.6 %shard_map.64.resid = f32[2688,128]{1,0:T(8,128)S(1)} custom-call(f32[2688,128]{1,0:T(8,128)S(1)} %get-tuple-element.40.bf, f32[2688,128]{1,0:T(8,128)S(1)} %get-tuple-element.55.xe.x2, f32[2688,128]{1,0:T(8,128)S(1)} %get-tuple-element.41.hf.he, f32[2688,128]{1,0:T(8,128)S(1)} %get-tuple-element.56.fw, f32[1,1024]{1,0:T(1,128)S(1)} %get-tuple-element.42.metric), custom_call_target="tpu_custom_call" | custom-call | flops 10000000 | bytes 4000000 | tf_op jit(solution)/shard_map/pallas_call | solution.py:594
  66.2 1.5 %shard_map.63 = (f32[2280,128]{1,0:T(8,128)S(1)}, f32[2048,128]{1,0:T(8,128)S(1)}, f32[2112,128]{1,0:T(8,128)S(1)}, f32[32,4,128]{2,1,0:T(4,128)S(1)}) custom-call(f32[32,64,128]{2,1,0:T(8,128)S(1)} %copy-done.1, f32[32]{0:T(128)S(1)} %copy-done.6, bf16[32,136,128]{2,1,0:T(8,128)(2,1)S(1)} %all_to_all.10.recv, f32[1,1024]{1,0:T(1,128)S(1)} %get-tuple-element.42.metric), custom_call_target="tpu_custom_call" | custom-call | flops 10000000 | bytes 4000000 | tf_op jit(solution)/shard_map/pallas_call | solution.py:598
  67.8 0.2 collective-permute-done.7.xr
  67.9 1.2 %shard_map.65 = bf16[32,72,128]{2,1,0:T(8,128)(2,1)S(1)} custom-call(f32[2688,128]{1,0:T(8,128)S(1)} %shard_map.64.resid, f32[2688,128]{1,0:T(8,128)S(1)} %get-tuple-element.55.xe.x2, f32[2688,128]{1,0:T(8,128)S(1)} %get-tuple-element.49.d2, f32[2688,128]{1,0:T(8,128)S(1)} %get-tuple-element.41.hf.he, bf16[16,1024]{1,0:T(8,128)(2,1)S(1)} %collective-permute-done.4.su, ...), custom_call_target="tpu_custom_call" | custom-call | flops 10000000 | bytes 4000000 | tf_op jit(solution)/shard_map/pallas_call | solution.py:609
  69.2 0.0 copy-start.2
  69.2 16.6 %all_to_all.11.recv = bf16[32,72,128]{2,1,0:T(8,128)(2,1)S(1)} all-to-all(bf16[32,72,128]{2,1,0:T(8,128)(2,1)S(1)} %shard_map.65), channel_id=1, replica_groups=mesh['wall'=32,'span'=2,'stream'=4] {'wall'}, dimensions={0} | all-to-all | bytes 1179648 | tf_op jit(solution)/shard_map/all_to_all | solution.py:612
  85.8 0.4 shard_map.66
  86.1 1.4 %collective-permute-start.8 = (bf16[4,32,128]{2,1,0:T(8,128)(2,1)S(1)}, bf16[4,32,128]{2,1,0:T(8,128)(2,1)S(1)}, u32[]{:S(2)}, u32[]{:S(2)}) collective-permute-start(bf16[4,32,128]{2,1,0:T(8,128)(2,1)S(1)} %get-tuple-element.75), channel_id=1, source_target_pairs={{0,4},{4,0},{1,5},{5,1},{2,6},{6,2},{3,7},{7,3},{8,12},{12,8},{9,1... | collective-permute-start | bytes 98312 | tf_op jit(solution)/shard_map/ppermute | solution.py:515
  87.5 7.3 %collective-permute-start.10 = (bf16[32,128]{1,0:T(8,128)(2,1)S(1)}, bf16[32,128]{1,0:T(8,128)(2,1)S(1)}, u32[]{:S(2)}, u32[]{:S(2)}) collective-permute-start(bf16[32,128]{1,0:T(8,128)(2,1)S(1)} %get-tuple-element.70.dl), channel_id=1, source_target_pairs={{1,0},{2,1},{3,2},{0,3},{5,4},{6,5},{7,6},{4,7},{9,8},{10,9},{11,1... | collective-permute-start | bytes 24584 | tf_op jit(solution)/shard_map/ppermute | solution.py:517
  94.8 0.2 collective-permute-start.9
  94.9 2.3 %shard_map.67 = (f32[32,64,128]{2,1,0:T(8,128)}, f32[32,64,128]{2,1,0:T(8,128)S(1)}, f32[128,128]{1,0:T(8,128)S(1)}) custom-call(f32[2280,128]{1,0:T(8,128)S(1)} %get-tuple-element.66.xf, f32[2280,128]{1,0:T(8,128)S(1)} %get-tuple-element.67.hf, f32[2048,128]{1,0:T(8,128)S(1)} %get-tuple-element.68.gx, f32[2112,128]{1,0:T(8,128)S(1)} %get-tuple-element.69.gk, ...), custom_call_target="tpu_custom_call" | custom-call | flops 10000000 | bytes 4000000 | tf_op jit(solution)/shard_map/pallas_call | solution.py:620
  97.3 1.4 %shard_map.68 = f32[32,64,128]{2,1,0:T(8,128)} custom-call(f32[32,64,128]{2,1,0:T(8,128)S(1)} %get-tuple-element.73.resid, f32[2280,128]{1,0:T(8,128)S(1)} %get-tuple-element.66.xf, f32[2280,128]{1,0:T(8,128)S(1)} %get-tuple-element.67.hf, f32[128,128]{1,0:T(8,128)S(1)} %get-tuple-element.74.own, bf16[4,32,128]{2,1,0:T(8,128)(2,1)S(1)} %collective-permute-done.8.spans, ...), custom_call_target="tpu_custom_call" | custom-call | flops 10000000 | bytes 4000000 | tf_op jit(solution)/shard_map/pallas_call | solution.py:626
  (24 shorter events, 0.1 us)
Async XLA Ops:
  4.2 50.0 %copy-start = (bf16[1024,1024]{1,0:T(8,128)(2,1)S(1)}, bf16[1024,1024]{1,0:T(8,128)(2,1)}, u32[]{:S(2)}) copy-start(bf16[1024,1024]{1,0:T(8,128)(2,1)} %line.5) | copy-start | bytes 6291460
  47.2 10.0 %collective-permute-start = (bf16[32,1024]{1,0:T(8,128)(2,1)S(1)}, bf16[32,1024]{1,0:T(8,128)(2,1)S(1)}, u32[]{:S(2)}, u32[]{:S(2)}) collective-permute-start(bf16[32,1024]{1,0:T(8,128)(2,1)S(1)} %get-tuple-element.45), channel_id=1, source_target_pairs={{0,64},{8,72},{16,80},{24,88},{32,96},{40,104},{48,112},{56,120},{... | collective-permute-start | bytes 196616 | tf_op jit(solution)/shard_map/ppermute | solution.py:535
  47.6 9.6 %collective-permute-start.1 = (bf16[32,1024]{1,0:T(8,128)(2,1)S(1)}, bf16[32,1024]{1,0:T(8,128)(2,1)S(1)}, u32[]{:S(2)}, u32[]{:S(2)}) collective-permute-start(bf16[32,1024]{1,0:T(8,128)(2,1)S(1)} %get-tuple-element.46), channel_id=1, source_target_pairs={{0,4},{8,12},{16,20},{24,28},{32,36},{40,44},{48,52},{56,60},{57,6... | collective-permute-start | bytes 196616 | tf_op jit(solution)/shard_map/ppermute | solution.py:535
  50.3 6.9 %collective-permute-start.2 = (bf16[32,1024]{1,0:T(8,128)(2,1)S(1)}, bf16[32,1024]{1,0:T(8,128)(2,1)S(1)}, u32[]{:S(2)}, u32[]{:S(2)}) collective-permute-start(bf16[32,1024]{1,0:T(8,128)(2,1)S(1)} %get-tuple-element.47), channel_id=1, source_target_pairs={{0,8},{8,16},{16,24},{24,32},{32,40},{40,48},{48,56},{56,57},{57,4... | collective-permute-start | bytes 196616 | tf_op jit(solution)/shard_map/ppermute | solution.py:535
  54.2 3.7 %collective-permute-start.3 = (bf16[32,1024]{1,0:T(8,128)(2,1)S(1)}, bf16[32,1024]{1,0:T(8,128)(2,1)S(1)}, u32[]{:S(2)}, u32[]{:S(2)}) collective-permute-start(bf16[32,1024]{1,0:T(8,128)(2,1)S(1)} %get-tuple-element.48), channel_id=1, source_target_pairs={{0,3},{8,0},{16,8},{24,16},{32,24},{40,32},{48,40},{56,48},{57,56}... | collective-permute-start | bytes 196616 | tf_op jit(solution)/shard_map/ppermute | solution.py:535
  59.5 8.2 %collective-permute-start.4 = (bf16[16,1024]{1,0:T(8,128)(2,1)S(1)}, bf16[16,1024]{1,0:T(8,128)(2,1)S(1)}, u32[]{:S(2)}, u32[]{:S(2)}) collective-permute-start(bf16[16,1024]{1,0:T(8,128)(2,1)S(1)} %get-tuple-element.58), channel_id=1, source_target_pairs={{0,64},{8,72},{16,80},{24,88},{32,96},{40,104},{48,112},{56,120},{... | collective-permute-start | bytes 98312 | tf_op jit(solution)/shard_map/ppermute | solution.py:535
  59.6 8.2 %collective-permute-start.5 = (bf16[16,1024]{1,0:T(8,128)(2,1)S(1)}, bf16[16,1024]{1,0:T(8,128)(2,1)S(1)}, u32[]{:S(2)}, u32[]{:S(2)}) collective-permute-start(bf16[16,1024]{1,0:T(8,128)(2,1)S(1)} %get-tuple-element.59), channel_id=1, source_target_pairs={{0,4},{8,12},{16,20},{24,28},{32,36},{40,44},{48,52},{56,60},{57,6... | collective-permute-start | bytes 98312 | tf_op jit(solution)/shard_map/ppermute | solution.py:535
  62.5 5.2 %collective-permute-start.6 = (bf16[16,1024]{1,0:T(8,128)(2,1)S(1)}, bf16[16,1024]{1,0:T(8,128)(2,1)S(1)}, u32[]{:S(2)}, u32[]{:S(2)}) collective-permute-start(bf16[16,1024]{1,0:T(8,128)(2,1)S(1)} %get-tuple-element.60), channel_id=1, source_target_pairs={{0,8},{8,16},{16,24},{24,32},{32,40},{40,48},{48,56},{56,57},{57,4... | collective-permute-start | bytes 98312 | tf_op jit(solution)/shard_map/ppermute | solution.py:535
  64.6 3.3 %collective-permute-start.7 = (bf16[16,1024]{1,0:T(8,128)(2,1)S(1)}, bf16[16,1024]{1,0:T(8,128)(2,1)S(1)}, u32[]{:S(2)}, u32[]{:S(2)}) collective-permute-start(bf16[16,1024]{1,0:T(8,128)(2,1)S(1)} %get-tuple-element.61), channel_id=1, source_target_pairs={{0,3},{8,0},{16,8},{24,16},{32,24},{40,32},{48,40},{56,48},{57,56}... | collective-permute-start | bytes 98312 | tf_op jit(solution)/shard_map/ppermute | solution.py:535
  64.6 1.6 %copy-start.1 = (f32[32,64,128]{2,1,0:T(8,128)S(1)}, f32[32,64,128]{2,1,0:T(8,128)}, u32[]{:S(2)}) copy-start(f32[32,64,128]{2,1,0:T(8,128)} %v_ref) | copy-start | bytes 3145732
  64.6 1.6 %copy-start.6 = (f32[32]{0:T(128)S(1)}, f32[32]{0:T(128)}, u32[]{:S(2)}) copy-start(f32[32]{0:T(128)} %m_ref) | copy-start | bytes 388
  67.9 17.8 %copy-start.3 = (bf16[2,32,128]{2,1,0:T(8,128)(2,1)S(1)}, bf16[2,32,128]{2,1,0:T(8,128)(2,1)}, u32[]{:S(2)}) copy-start(bf16[2,32,128]{2,1,0:T(8,128)(2,1)} %get-tuple-element.63.ves) | copy-start | bytes 49156
  67.9 17.8 %copy-start.4 = (bf16[32,128]{1,0:T(8,128)(2,1)S(1)}, bf16[32,128]{1,0:T(8,128)(2,1)}, u32[]{:S(2)}) copy-start(bf16[32,128]{1,0:T(8,128)(2,1)} %get-tuple-element.64.vdl) | copy-start | bytes 24580
  67.9 17.8 %copy-start.5 = (bf16[32,128]{1,0:T(8,128)(2,1)S(1)}, bf16[32,128]{1,0:T(8,128)(2,1)}, u32[]{:S(2)}) copy-start(bf16[32,128]{1,0:T(8,128)(2,1)} %get-tuple-element.65.vdr) | copy-start | bytes 24580
  69.2 25.8 %copy-start.2 = (f32[32,64,128]{2,1,0:T(8,128)S(1)}, f32[32,64,128]{2,1,0:T(8,128)}, u32[]{:S(2)}) copy-start(f32[32,64,128]{2,1,0:T(8,128)} %b_ref.1) | copy-start | bytes 3145732
  86.1 11.2 %collective-permute-start.8 = (bf16[4,32,128]{2,1,0:T(8,128)(2,1)S(1)}, bf16[4,32,128]{2,1,0:T(8,128)(2,1)S(1)}, u32[]{:S(2)}, u32[]{:S(2)}) collective-permute-start(bf16[4,32,128]{2,1,0:T(8,128)(2,1)S(1)} %get-tuple-element.75), channel_id=1, source_target_pairs={{0,4},{4,0},{1,5},{5,1},{2,6},{6,2},{3,7},{7,3},{8,12},{12,8},{9,1... | collective-permute-start | bytes 98312 | tf_op jit(solution)/shard_map/ppermute | solution.py:515
  87.5 9.8 %collective-permute-start.10 = (bf16[32,128]{1,0:T(8,128)(2,1)S(1)}, bf16[32,128]{1,0:T(8,128)(2,1)S(1)}, u32[]{:S(2)}, u32[]{:S(2)}) collective-permute-start(bf16[32,128]{1,0:T(8,128)(2,1)S(1)} %get-tuple-element.70.dl), channel_id=1, source_target_pairs={{1,0},{2,1},{3,2},{0,3},{5,4},{6,5},{7,6},{4,7},{9,8},{10,9},{11,1... | collective-permute-start | bytes 24584 | tf_op jit(solution)/shard_map/ppermute | solution.py:517
  94.8 2.5 %collective-permute-start.9 = (bf16[32,128]{1,0:T(8,128)(2,1)S(1)}, bf16[32,128]{1,0:T(8,128)(2,1)S(1)}, u32[]{:S(2)}, u32[]{:S(2)}) collective-permute-start(bf16[32,128]{1,0:T(8,128)(2,1)S(1)} %get-tuple-element.71.dr), channel_id=1, source_target_pairs={{0,1},{1,2},{2,3},{3,0},{4,5},{5,6},{6,7},{7,4},{8,9},{9,10},{10,1... | collective-permute-start | bytes 24584 | tf_op jit(solution)/shard_map/ppermute | solution.py:516

commit v5 on v4

--- a/solution.py
+++ b/solution.py
@@ -399,7 +399,8 @@
             below = half
         return below
 
-    gk[SPAN * ROWS :, :] = lax.fori_loop(0, ROWS // 4, four, jnp.zeros((SPAN, LANES), F32))
+    start = jnp.zeros((SPAN, LANES), F32)
+    gk[SPAN * ROWS :, :] = lax.fori_loop(0, ROWS // 4, four, start, unroll=2)
     for s in (-1, SPAN):
         hf[block_span(s), :] = jnp.zeros((ROWS, LANES), F32)
     count = WY * WZ
@@ -455,7 +456,7 @@
         return tuple(carry)
 
     zero = jnp.zeros((ROWS, LANES), F32)
-    lax.fori_loop(0, ROWS // 4, four, (zero, zero))
+    lax.fori_loop(0, ROWS // 4, four, (zero, zero), unroll=2)
 
     def tail(t, _):
         parts = from_blocks([recv[owner(t, z), 2 * ROWS :, :].astype(F32) for z in range(WZ)])

time: 99.1 us -> 98.8 us (level)
  transfers between devices with their start and end apart: 11 -> 11, of which waited for: 2 -> 2; matrix products, arithmetic and copies ran while one was open for 0% -> 0% of each run, Pallas kernels for 9% -> 8%
where the time goes in v5:
time: 98.8 us; the launch traced here: 98.5 us
  blocking collectives  59.4 us (60%)
  starting transfers between devices  20.5 us (21%)
  Pallas kernels  16.4 us (17%)
  waiting for transfers between devices  1.09 us (1%)
    all_to_all x2, blocking collectives, body(): recv = lax.all_to_all(send, 'wall', 0, 0, tiled=True)  59.4 us
    ppermute x8, starting transfers between devices, line_shift(): return lax.ppermute(value, ('wall', 'span', 'stream'), pairs)  12.1 us
    ppermute x1, starting transfers between devices, block_edges(): lax.ppermute(dl, 'stream', left)  7.12 us
    pallas_call x1, Pallas kernels, body(): call(pack, (shape(sent, BF16), shape((2, ROWS, LANES), BF16), dense, dens...  3.57 us
    pallas_call x1, Pallas kernels, body(): call(first_lines, (field, field, field), (rounded,))  2.98 us
    pallas_call x1, Pallas kernels, body(): call(inner_resid, (whole, whole, shape((LANES, LANES), F32)), (block, plt...  2.05 us
  transfers between devices with their start and end apart: 11, of which 2 were waited for; matrix products, arithmetic and copies ran while one was open for 0% of the time, Pallas kernels for 8%

profile of v5, /device:TPU:1, one launch (start us, length us, event | category | flops | bytes accessed | tf_op | source)
XLA Modules:
  0.0 98.5 jit_solution(1522464287861926358)
XLA Ops:
  0.6 3.6 %shard_map.59 = (bf16[32,136,128]{2,1,0:T(8,128)(2,1)}, bf16[2,32,128]{2,1,0:T(8,128)(2,1)}, bf16[32,128]{1,0:T(8,128)(2,1)}, bf16[32,128]{1,0:T(8,128)(2,1)}) custom-call(f32[32,64,128]{2,1,0:T(8,128)} %b_ref.1, f32[32,64,128]{2,1,0:T(8,128)} %v_ref, f32[1,32]{1,0:T(1,128)} %bitcast.1), custom_call_target="tpu_custom_call" | custom-call | flops 10000000 | bytes 4000000 | tf_op jit(solution)/shard_map/pallas_call | solution.py:555
  4.2 42.6 %all_to_all.10.recv = bf16[32,136,128]{2,1,0:T(8,128)(2,1)S(1)} all-to-all(bf16[32,136,128]{2,1,0:T(8,128)(2,1)} %get-tuple-element.39), channel_id=1, replica_groups=mesh['wall'=32,'span'=2,'stream'=4] {'wall'}, dimensions={0} | all-to-all | bytes 2228224 | tf_op jit(solution)/shard_map/all_to_all | solution.py:576
  46.8 0.4 shard_map.60
  47.2 0.4 collective-permute-start
  47.6 2.7 %collective-permute-start.1 = (bf16[32,1024]{1,0:T(8,128)(2,1)S(1)}, bf16[32,1024]{1,0:T(8,128)(2,1)S(1)}, u32[]{:S(2)}, u32[]{:S(2)}) collective-permute-start(bf16[32,1024]{1,0:T(8,128)(2,1)S(1)} %get-tuple-element.46), channel_id=1, source_target_pairs={{0,4},{8,12},{16,20},{24,28},{32,36},{40,44},{48,52},{56,60},{57,6... | collective-permute-start | bytes 196616 | tf_op jit(solution)/shard_map/ppermute | solution.py:536
  50.3 3.9 %collective-permute-start.2 = (bf16[32,1024]{1,0:T(8,128)(2,1)S(1)}, bf16[32,1024]{1,0:T(8,128)(2,1)S(1)}, u32[]{:S(2)}, u32[]{:S(2)}) collective-permute-start(bf16[32,1024]{1,0:T(8,128)(2,1)S(1)} %get-tuple-element.47), channel_id=1, source_target_pairs={{0,8},{8,16},{16,24},{24,32},{32,40},{40,48},{48,56},{56,57},{57,4... | collective-permute-start | bytes 196616 | tf_op jit(solution)/shard_map/ppermute | solution.py:536
  54.2 3.0 %shard_map.61 = (f32[2688,128]{1,0:T(8,128)S(1)}, f32[2688,128]{1,0:T(8,128)S(1)}, f32[2688,128]{1,0:T(8,128)S(1)}) custom-call(f32[2688,128]{1,0:T(8,128)S(1)} %get-tuple-element.40.bf, f32[2688,128]{1,0:T(8,128)S(1)} %get-tuple-element.41.hf.he, f32[1,1024]{1,0:T(1,128)S(1)} %get-tuple-element.42.metric, bf16[1024,1024]{1,0:T(8,128)(2,1)S(1)} %copy-done), custom_call_target="tpu_custom_call" | custom-call | flops 10000000 | bytes 4000000 | tf_op jit(solution)/shard_map/pallas_call | solution.py:586
  57.2 0.7 collective-permute-done.3.xr.vxr
  57.9 1.6 %shard_map.62 = (f32[2688,128]{1,0:T(8,128)S(1)}, f32[2688,128]{1,0:T(8,128)S(1)}, bf16[16,1024]{1,0:T(8,128)(2,1)S(1)}, bf16[16,1024]{1,0:T(8,128)(2,1)S(1)}, b...) custom-call(f32[2688,128]{1,0:T(8,128)S(1)} %get-tuple-element.43.resid, f32[2688,128]{1,0:T(8,128)S(1)} %get-tuple-element.44.x1, ...), custom_call_target="tpu_custom_call" | custom-call | flops 10000000 | bytes 4000000 | tf_op jit(solution)/shard_map/pallas_call | solution.py:589
  59.5 0.1 collective-permute-start.4
  59.6 3.0 %collective-permute-start.5 = (bf16[16,1024]{1,0:T(8,128)(2,1)S(1)}, bf16[16,1024]{1,0:T(8,128)(2,1)S(1)}, u32[]{:S(2)}, u32[]{:S(2)}) collective-permute-start(bf16[16,1024]{1,0:T(8,128)(2,1)S(1)} %get-tuple-element.59), channel_id=1, source_target_pairs={{0,4},{8,12},{16,20},{24,28},{32,36},{40,44},{48,52},{56,60},{57,6... | collective-permute-start | bytes 98312 | tf_op jit(solution)/shard_map/ppermute | solution.py:536
  62.5 2.0 %collective-permute-start.6 = (bf16[16,1024]{1,0:T(8,128)(2,1)S(1)}, bf16[16,1024]{1,0:T(8,128)(2,1)S(1)}, u32[]{:S(2)}, u32[]{:S(2)}) collective-permute-start(bf16[16,1024]{1,0:T(8,128)(2,1)S(1)} %get-tuple-element.60), channel_id=1, source_target_pairs={{0,8},{8,16},{16,24},{24,32},{32,40},{40,48},{48,56},{56,57},{57,4... | collective-permute-start | bytes 98312 | tf_op jit(solution)/shard_map/ppermute | solution.py:536
  64.6 1.6 %shard_map.64.resid = f32[2688,128]{1,0:T(8,128)S(1)} custom-call(f32[2688,128]{1,0:T(8,128)S(1)} %get-tuple-element.40.bf, f32[2688,128]{1,0:T(8,128)S(1)} %get-tuple-element.55.xe.x2, f32[2688,128]{1,0:T(8,128)S(1)} %get-tuple-element.41.hf.he, f32[2688,128]{1,0:T(8,128)S(1)} %get-tuple-element.56.fw, f32[1,1024]{1,0:T(1,128)S(1)} %get-tuple-element.42.metric), custom_call_target="tpu_custom_call" | custom-call | flops 10000000 | bytes 4000000 | tf_op jit(solution)/shard_map/pallas_call | solution.py:595
  66.2 1.3 %shard_map.63 = (f32[2280,128]{1,0:T(8,128)S(1)}, f32[2048,128]{1,0:T(8,128)S(1)}, f32[2112,128]{1,0:T(8,128)S(1)}, f32[32,4,128]{2,1,0:T(4,128)S(1)}) custom-call(f32[32,64,128]{2,1,0:T(8,128)S(1)} %copy-done.1, f32[32]{0:T(128)S(1)} %copy-done.6, bf16[32,136,128]{2,1,0:T(8,128)(2,1)S(1)} %all_to_all.10.recv, f32[1,1024]{1,0:T(1,128)S(1)} %get-tuple-element.42.metric), custom_call_target="tpu_custom_call" | custom-call | flops 10000000 | bytes 4000000 | tf_op jit(solution)/shard_map/pallas_call | solution.py:599
  67.5 0.4 collective-permute-done.7.xr
  67.9 1.2 %shard_map.65 = bf16[32,72,128]{2,1,0:T(8,128)(2,1)S(1)} custom-call(f32[2688,128]{1,0:T(8,128)S(1)} %shard_map.64.resid, f32[2688,128]{1,0:T(8,128)S(1)} %get-tuple-element.55.xe.x2, f32[2688,128]{1,0:T(8,128)S(1)} %get-tuple-element.49.d2, f32[2688,128]{1,0:T(8,128)S(1)} %get-tuple-element.41.hf.he, bf16[16,1024]{1,0:T(8,128)(2,1)S(1)} %collective-permute-done.4.su, ...), custom_call_target="tpu_custom_call" | custom-call | flops 10000000 | bytes 4000000 | tf_op jit(solution)/shard_map/pallas_call | solution.py:610
  69.2 0.0 copy-start.2
  69.2 16.9 %all_to_all.11.recv = bf16[32,72,128]{2,1,0:T(8,128)(2,1)S(1)} all-to-all(bf16[32,72,128]{2,1,0:T(8,128)(2,1)S(1)} %shard_map.65), channel_id=1, replica_groups=mesh['wall'=32,'span'=2,'stream'=4] {'wall'}, dimensions={0} | all-to-all | bytes 1179648 | tf_op jit(solution)/shard_map/all_to_all | solution.py:613
  86.1 0.4 shard_map.66
  86.4 1.2 %collective-permute-start.8 = (bf16[4,32,128]{2,1,0:T(8,128)(2,1)S(1)}, bf16[4,32,128]{2,1,0:T(8,128)(2,1)S(1)}, u32[]{:S(2)}, u32[]{:S(2)}) collective-permute-start(bf16[4,32,128]{2,1,0:T(8,128)(2,1)S(1)} %get-tuple-element.75), channel_id=1, source_target_pairs={{0,4},{4,0},{1,5},{5,1},{2,6},{6,2},{3,7},{7,3},{8,12},{12,8},{9,1... | collective-permute-start | bytes 98312 | tf_op jit(solution)/shard_map/ppermute | solution.py:516
  87.6 7.1 %collective-permute-start.10 = (bf16[32,128]{1,0:T(8,128)(2,1)S(1)}, bf16[32,128]{1,0:T(8,128)(2,1)S(1)}, u32[]{:S(2)}, u32[]{:S(2)}) collective-permute-start(bf16[32,128]{1,0:T(8,128)(2,1)S(1)} %get-tuple-element.70.dl), channel_id=1, source_target_pairs={{1,0},{2,1},{3,2},{0,3},{5,4},{6,5},{7,6},{4,7},{9,8},{10,9},{11,1... | collective-permute-start | bytes 24584 | tf_op jit(solution)/shard_map/ppermute | solution.py:518
  94.7 0.2 collective-permute-start.9
  94.9 2.1 %shard_map.67 = (f32[32,64,128]{2,1,0:T(8,128)}, f32[32,64,128]{2,1,0:T(8,128)S(1)}, f32[128,128]{1,0:T(8,128)S(1)}) custom-call(f32[2280,128]{1,0:T(8,128)S(1)} %get-tuple-element.66.xf, f32[2280,128]{1,0:T(8,128)S(1)} %get-tuple-element.67.hf, f32[2048,128]{1,0:T(8,128)S(1)} %get-tuple-element.68.gx, f32[2112,128]{1,0:T(8,128)S(1)} %get-tuple-element.69.gk, ...), custom_call_target="tpu_custom_call" | custom-call | flops 10000000 | bytes 4000000 | tf_op jit(solution)/shard_map/pallas_call | solution.py:621
  97.0 1.4 %shard_map.68 = f32[32,64,128]{2,1,0:T(8,128)} custom-call(f32[32,64,128]{2,1,0:T(8,128)S(1)} %get-tuple-element.73.resid, f32[2280,128]{1,0:T(8,128)S(1)} %get-tuple-element.66.xf, f32[2280,128]{1,0:T(8,128)S(1)} %get-tuple-element.67.hf, f32[128,128]{1,0:T(8,128)S(1)} %get-tuple-element.74.own, bf16[4,32,128]{2,1,0:T(8,128)(2,1)S(1)} %collective-permute-done.8.spans, ...), custom_call_target="tpu_custom_call" | custom-call | flops 10000000 | bytes 4000000 | tf_op jit(solution)/shard_map/pallas_call | solution.py:627
  (24 shorter events, 0.1 us)
Async XLA Ops:
  4.2 50.0 %copy-start = (bf16[1024,1024]{1,0:T(8,128)(2,1)S(1)}, bf16[1024,1024]{1,0:T(8,128)(2,1)}, u32[]{:S(2)}) copy-start(bf16[1024,1024]{1,0:T(8,128)(2,1)} %line.5) | copy-start | bytes 6291460
  47.2 10.0 %collective-permute-start = (bf16[32,1024]{1,0:T(8,128)(2,1)S(1)}, bf16[32,1024]{1,0:T(8,128)(2,1)S(1)}, u32[]{:S(2)}, u32[]{:S(2)}) collective-permute-start(bf16[32,1024]{1,0:T(8,128)(2,1)S(1)} %get-tuple-element.45), channel_id=1, source_target_pairs={{0,64},{8,72},{16,80},{24,88},{32,96},{40,104},{48,112},{56,120},{... | collective-permute-start | bytes 196616 | tf_op jit(solution)/shard_map/ppermute | solution.py:536
  47.6 9.6 %collective-permute-start.1 = (bf16[32,1024]{1,0:T(8,128)(2,1)S(1)}, bf16[32,1024]{1,0:T(8,128)(2,1)S(1)}, u32[]{:S(2)}, u32[]{:S(2)}) collective-permute-start(bf16[32,1024]{1,0:T(8,128)(2,1)S(1)} %get-tuple-element.46), channel_id=1, source_target_pairs={{0,4},{8,12},{16,20},{24,28},{32,36},{40,44},{48,52},{56,60},{57,6... | collective-permute-start | bytes 196616 | tf_op jit(solution)/shard_map/ppermute | solution.py:536
  50.3 6.9 %collective-permute-start.2 = (bf16[32,1024]{1,0:T(8,128)(2,1)S(1)}, bf16[32,1024]{1,0:T(8,128)(2,1)S(1)}, u32[]{:S(2)}, u32[]{:S(2)}) collective-permute-start(bf16[32,1024]{1,0:T(8,128)(2,1)S(1)} %get-tuple-element.47), channel_id=1, source_target_pairs={{0,8},{8,16},{16,24},{24,32},{32,40},{40,48},{48,56},{56,57},{57,4... | collective-permute-start | bytes 196616 | tf_op jit(solution)/shard_map/ppermute | solution.py:536
  54.2 3.7 %collective-permute-start.3 = (bf16[32,1024]{1,0:T(8,128)(2,1)S(1)}, bf16[32,1024]{1,0:T(8,128)(2,1)S(1)}, u32[]{:S(2)}, u32[]{:S(2)}) collective-permute-start(bf16[32,1024]{1,0:T(8,128)(2,1)S(1)} %get-tuple-element.48), channel_id=1, source_target_pairs={{0,3},{8,0},{16,8},{24,16},{32,24},{40,32},{48,40},{56,48},{57,56}... | collective-permute-start | bytes 196616 | tf_op jit(solution)/shard_map/ppermute | solution.py:536
  59.5 8.0 %collective-permute-start.4 = (bf16[16,1024]{1,0:T(8,128)(2,1)S(1)}, bf16[16,1024]{1,0:T(8,128)(2,1)S(1)}, u32[]{:S(2)}, u32[]{:S(2)}) collective-permute-start(bf16[16,1024]{1,0:T(8,128)(2,1)S(1)} %get-tuple-element.58), channel_id=1, source_target_pairs={{0,64},{8,72},{16,80},{24,88},{32,96},{40,104},{48,112},{56,120},{... | collective-permute-start | bytes 98312 | tf_op jit(solution)/shard_map/ppermute | solution.py:536
  59.6 7.9 %collective-permute-start.5 = (bf16[16,1024]{1,0:T(8,128)(2,1)S(1)}, bf16[16,1024]{1,0:T(8,128)(2,1)S(1)}, u32[]{:S(2)}, u32[]{:S(2)}) collective-permute-start(bf16[16,1024]{1,0:T(8,128)(2,1)S(1)} %get-tuple-element.59), channel_id=1, source_target_pairs={{0,4},{8,12},{16,20},{24,28},{32,36},{40,44},{48,52},{56,60},{57,6... | collective-permute-start | bytes 98312 | tf_op jit(solution)/shard_map/ppermute | solution.py:536
  62.5 5.0 %collective-permute-start.6 = (bf16[16,1024]{1,0:T(8,128)(2,1)S(1)}, bf16[16,1024]{1,0:T(8,128)(2,1)S(1)}, u32[]{:S(2)}, u32[]{:S(2)}) collective-permute-start(bf16[16,1024]{1,0:T(8,128)(2,1)S(1)} %get-tuple-element.60), channel_id=1, source_target_pairs={{0,8},{8,16},{16,24},{24,32},{32,40},{40,48},{48,56},{56,57},{57,4... | collective-permute-start | bytes 98312 | tf_op jit(solution)/shard_map/ppermute | solution.py:536
  64.6 3.3 %collective-permute-start.7 = (bf16[16,1024]{1,0:T(8,128)(2,1)S(1)}, bf16[16,1024]{1,0:T(8,128)(2,1)S(1)}, u32[]{:S(2)}, u32[]{:S(2)}) collective-permute-start(bf16[16,1024]{1,0:T(8,128)(2,1)S(1)} %get-tuple-element.61), channel_id=1, source_target_pairs={{0,3},{8,0},{16,8},{24,16},{32,24},{40,32},{48,40},{56,48},{57,56}... | collective-permute-start | bytes 98312 | tf_op jit(solution)/shard_map/ppermute | solution.py:536
  64.6 1.6 %copy-start.1 = (f32[32,64,128]{2,1,0:T(8,128)S(1)}, f32[32,64,128]{2,1,0:T(8,128)}, u32[]{:S(2)}) copy-start(f32[32,64,128]{2,1,0:T(8,128)} %v_ref) | copy-start | bytes 3145732
  64.6 1.6 %copy-start.6 = (f32[32]{0:T(128)S(1)}, f32[32]{0:T(128)}, u32[]{:S(2)}) copy-start(f32[32]{0:T(128)} %m_ref) | copy-start | bytes 388
  67.9 18.1 %copy-start.3 = (bf16[2,32,128]{2,1,0:T(8,128)(2,1)S(1)}, bf16[2,32,128]{2,1,0:T(8,128)(2,1)}, u32[]{:S(2)}) copy-start(bf16[2,32,128]{2,1,0:T(8,128)(2,1)} %get-tuple-element.63.ves) | copy-start | bytes 49156
  67.9 18.1 %copy-start.4 = (bf16[32,128]{1,0:T(8,128)(2,1)S(1)}, bf16[32,128]{1,0:T(8,128)(2,1)}, u32[]{:S(2)}) copy-start(bf16[32,128]{1,0:T(8,128)(2,1)} %get-tuple-element.64.vdl) | copy-start | bytes 24580
  67.9 18.1 %copy-start.5 = (bf16[32,128]{1,0:T(8,128)(2,1)S(1)}, bf16[32,128]{1,0:T(8,128)(2,1)}, u32[]{:S(2)}) copy-start(bf16[32,128]{1,0:T(8,128)(2,1)} %get-tuple-element.65.vdr) | copy-start | bytes 24580
  69.2 25.7 %copy-start.2 = (f32[32,64,128]{2,1,0:T(8,128)S(1)}, f32[32,64,128]{2,1,0:T(8,128)}, u32[]{:S(2)}) copy-start(f32[32,64,128]{2,1,0:T(8,128)} %b_ref.1) | copy-start | bytes 3145732
  86.4 10.6 %collective-permute-start.8 = (bf16[4,32,128]{2,1,0:T(8,128)(2,1)S(1)}, bf16[4,32,128]{2,1,0:T(8,128)(2,1)S(1)}, u32[]{:S(2)}, u32[]{:S(2)}) collective-permute-start(bf16[4,32,128]{2,1,0:T(8,128)(2,1)S(1)} %get-tuple-element.75), channel_id=1, source_target_pairs={{0,4},{4,0},{1,5},{5,1},{2,6},{6,2},{3,7},{7,3},{8,12},{12,8},{9,1... | collective-permute-start | bytes 98312 | tf_op jit(solution)/shard_map/ppermute | solution.py:516
  87.6 9.4 %collective-permute-start.10 = (bf16[32,128]{1,0:T(8,128)(2,1)S(1)}, bf16[32,128]{1,0:T(8,128)(2,1)S(1)}, u32[]{:S(2)}, u32[]{:S(2)}) collective-permute-start(bf16[32,128]{1,0:T(8,128)(2,1)S(1)} %get-tuple-element.70.dl), channel_id=1, source_target_pairs={{1,0},{2,1},{3,2},{0,3},{5,4},{6,5},{7,6},{4,7},{9,8},{10,9},{11,1... | collective-permute-start | bytes 24584 | tf_op jit(solution)/shard_map/ppermute | solution.py:518
  94.7 2.3 %collective-permute-start.9 = (bf16[32,128]{1,0:T(8,128)(2,1)S(1)}, bf16[32,128]{1,0:T(8,128)(2,1)S(1)}, u32[]{:S(2)}, u32[]{:S(2)}) collective-permute-start(bf16[32,128]{1,0:T(8,128)(2,1)S(1)} %get-tuple-element.71.dr), channel_id=1, source_target_pairs={{0,1},{1,2},{2,3},{3,0},{4,5},{5,6},{6,7},{7,4},{8,9},{9,10},{10,1... | collective-permute-start | bytes 24584 | tf_op jit(solution)/shard_map/ppermute | solution.py:517
